TPU v7x, 32 devices: a whole 2x2x4 slice. The times are simulated.
32 devices in a mesh: pipe: 2 (over x), seq: 4 (over z), dp: 4 (over y, core).
Axes of the slice: x: 2, y: 2, z: 4, core: 2. Of those that a mesh axis runs over, the one named last changes fastest.
Arguments:
- embedded_families: bfloat16 [8, 4, 128, 768], P('dp', 'seq'), may hold values from -6 to 6
- order: int32 [4, 2], P('dp'), may hold values from 0 to 1, each once within a row
- token_quarter_factor: int32 [8, 4, 128], P('dp', 'seq'), may hold values from 0 to 4
- genuine_residue_tally: int32 [8], P('dp'), may hold values from 64 to 128
- standardizer_scales: float32 [2, 3, 768], P('pipe', None, 'seq'), may hold values from 0.5 to 1.5
- standardizer_offsets: float32 [2, 3, 768], P('pipe', None, 'seq'), may hold values from -1.5 to 1.5
- row_qkv: bfloat16 [2, 768, 2304], P('pipe', 'seq'), may hold values from -0.21875 to 0.21875
- row_out: bfloat16 [2, 768, 768], P('pipe', 'seq'), may hold values from -1.75 to 1.75
- col_qkv: bfloat16 [2, 768, 2304], P('pipe', 'seq'), may hold values from -0.21875 to 0.21875
- col_out: bfloat16 [2, 768, 768], P('pipe', 'seq'), may hold values from -1.75 to 1.75
- ffn_up: bfloat16 [2, 768, 3072], P('pipe', 'seq'), may hold values from -0.21875 to 0.21875
- ffn_down: bfloat16 [2, 3072, 768], P('pipe', 'seq'), may hold values from -0.109375 to 0.109375
- upstream_sensitivity: bfloat16 [8, 4, 128, 768], P('dp', 'seq'), may hold values from -6 to 6
Outputs:
- activations: bfloat16 [2, 8, 4, 128, 768], P('pipe', 'dp', 'seq')
- block_entry_derivs: bfloat16 [2, 8, 4, 128, 768], P('pipe', 'dp', 'seq')
- disorder_cost: float32 [2, 8], P('pipe', 'dp')
- grad_row_qkv: float32 [2, 768, 2304], P('pipe', 'seq')
- grad_row_out: float32 [2, 768, 768], P('pipe', 'seq')
- grad_col_qkv: float32 [2, 768, 2304], P('pipe', 'seq')
- grad_col_out: float32 [2, 768, 768], P('pipe', 'seq')
- grad_ffn_up: float32 [2, 768, 3072], P('pipe', 'seq')
- grad_ffn_down: float32 [2, 3072, 768], P('pipe', 'seq')
- grad_ln_gain: float32 [2, 3, 768], P('pipe', None, 'seq')
- grad_ln_bias: float32 [2, 3, 768], P('pipe', None, 'seq')
Inputs may be any that keep to these rules, and one draw needn't show every extreme that they name: Each row of order is a permutation of 0 to 1.
All inputs are finite; a program needn't handle non-finite values.
Results may differ from a plain program's by a relative error of at most 0.04.
Values may be sent and summed in bfloat16 or wider, within the bound.
A program may use at most 320 MiB of HBM per device.

v0:
```python
import math

import jax
import jax.numpy as jnp
from jax import lax
from jax.sharding import PartitionSpec as P

HEAD_TALLY = 12


norm_epsilon = 1e-05


def shifted(value, axis, steps):
    count = lax.axis_size(axis)
    initial, last = (max(0, -steps), min(count, count - steps))
    return lax.ppermute(value, axis, [(source, source + steps) for source in range(initial, last)])


def normed(values, gain_row, bias_row):
    average = jnp.mean(values, axis=-1, keepdims=True)
    centered = values - average
    variance = jnp.mean(centered * centered, axis=-1, keepdims=True)
    return centered * lax.rsqrt(variance + norm_epsilon) * gain_row + bias_row


def gelu_exact(values):
    return jax.nn.gelu(values, approximate=False)


def product(left, weight):
    return lax.dot_general(
        left, weight, (((left.ndim - 1,), (0,)), ((), ())), preferred_element_type=jnp.float32
    )


def product_back(left, weight):
    return lax.dot_general(
        left, weight, (((left.ndim - 1,), (1,)), ((), ())), preferred_element_type=jnp.float32
    )


def weight_term(left, right):
    return lax.dot_general(
        left, right, (((0, 1), (0, 1)), ((), ())), preferred_element_type=jnp.float32
    )


def split_heads(values, head_count):
    return values.reshape(values.shape[:-1] + (head_count, values.shape[-1] // head_count))


def choose(flag, first_tree, second_tree):
    return jax.tree.map(lambda early, later: jnp.where(flag, early, later), first_tree, second_tree)


def column_scores(queries, key_rows, head_count):
    query_heads = split_heads(queries, head_count)
    raw = jnp.einsum(
        "rche,sche->chrs",
        query_heads,
        split_heads(key_rows, head_count),
        preferred_element_type=jnp.float32,
    )
    return raw / math.sqrt(query_heads.shape[-1])


def column_forward(queries, key_rows, content_lines, head_count):
    scores = column_scores(queries, key_rows, head_count)
    log_total = jax.nn.logsumexp(scores, axis=-1)
    vertical_factors = jnp.exp(scores - log_total[..., None]).astype(jnp.bfloat16)
    mixed_cols = jnp.einsum(
        "gmqi,igmu->qgmu",
        vertical_factors,
        split_heads(content_lines, head_count),
        preferred_element_type=jnp.float32,
    )
    return (mixed_cols.reshape(queries.shape).astype(jnp.bfloat16), log_total)


def column_backward(queries, key_rows, content_lines, log_total, grad_mixed, head_count):
    scores = column_scores(queries, key_rows, head_count)
    softmax_share = jnp.exp(scores - log_total[..., None])
    grad_heads = split_heads(grad_mixed, head_count)
    grad_probs = jnp.einsum(
        "rche,sche->chrs",
        grad_heads,
        split_heads(content_lines, head_count),
        preferred_element_type=jnp.float32,
    )
    grad_values = jnp.einsum(
        "chrs,rche->sche",
        softmax_share.astype(jnp.bfloat16),
        grad_heads,
        preferred_element_type=jnp.float32,
    )
    grad_scores = (
        softmax_share * (grad_probs - jnp.sum(softmax_share * grad_probs, axis=-1, keepdims=True))
    ).astype(jnp.bfloat16)
    root_size = math.sqrt(queries.shape[-1] // head_count)
    grad_queries = (
        jnp.einsum(
            "gmqi,igmu->qgmu",
            grad_scores,
            split_heads(key_rows, head_count),
            preferred_element_type=jnp.float32,
        )
        / root_size
    )
    grad_keys = (
        jnp.einsum(
            "chrs,rche->sche",
            grad_scores,
            split_heads(queries, head_count),
            preferred_element_type=jnp.float32,
        )
        / root_size
    )
    return (
        grad_queries.reshape(queries.shape),
        grad_keys.reshape(key_rows.shape),
        grad_values.reshape(content_lines.shape),
    )


def row_split(horizontal_mixer, model_width, head_count):
    queries = split_heads(horizontal_mixer[..., :model_width], head_count)
    key_rows = split_heads(horizontal_mixer[..., model_width : 2 * model_width], head_count)
    content_lines = split_heads(horizontal_mixer[..., 2 * model_width :], head_count)
    return (queries, key_rows, content_lines)


def layer_forward(source_rows, family_residues, projection_tables, head_count):
    (
        horizontal_coefficients,
        w_row_out,
        vertical_coefficients,
        w_col_out,
        w_up,
        w_down,
        gain_rows,
        bias_rows,
    ) = projection_tables
    row_count, columns, model_width = source_rows.shape
    total_rows = row_count * lax.axis_size("seq")
    start = source_rows.astype(jnp.float32)
    layernorm_first = normed(start, gain_rows[0], bias_rows[0]).astype(jnp.bfloat16)
    horizontal_mixer = product(layernorm_first, horizontal_coefficients).astype(jnp.bfloat16)
    queries, key_rows, content_lines = row_split(horizontal_mixer, model_width, head_count)
    logit_factor = 1.0 / (math.sqrt(model_width // head_count) * math.sqrt(total_rows))
    partial_value = logit_factor * jnp.einsum(
        "rihe,rjhe->hij", queries, key_rows, preferred_element_type=jnp.float32
    )
    logits = lax.psum(partial_value.astype(jnp.bfloat16), "seq").astype(jnp.float32)
    softmax_share = jax.nn.softmax(logits, axis=-1)
    log_probs = jax.nn.log_softmax(logits, axis=-1)
    entropy = -jnp.sum(softmax_share * log_probs, axis=-1)
    valid_residues = (jnp.arange(columns, dtype=jnp.int32) < family_residues).astype(jnp.float32)
    disorder_cost = jnp.sum(entropy * valid_residues[None, :]) / float(head_count * columns)
    blended_lines = jnp.einsum(
        "vyp,opvl->oyvl",
        softmax_share.astype(jnp.bfloat16),
        content_lines,
        preferred_element_type=jnp.float32,
    )
    blended_lines = blended_lines.reshape(row_count, columns, model_width).astype(jnp.bfloat16)
    after_row = start + product(blended_lines, w_row_out)
    layernorm_second = normed(after_row, gain_rows[1], bias_rows[1]).astype(jnp.bfloat16)
    vertical_mixer = product(layernorm_second, vertical_coefficients).astype(jnp.bfloat16)
    everyone = lax.all_gather(vertical_mixer[..., model_width:], "seq", axis=0, tiled=True)
    mixed_values, log_total = column_forward(
        vertical_mixer[..., :model_width],
        everyone[..., :model_width],
        everyone[..., model_width:],
        head_count,
    )
    column_state = (everyone, log_total)
    after_col = after_row + product(mixed_values, w_col_out)
    normal_c = normed(after_col, gain_rows[2], bias_rows[2]).astype(jnp.bfloat16)
    upward = product(normal_c, w_up)
    hidden = gelu_exact(upward).astype(jnp.bfloat16)
    result = after_col + product(hidden, w_down)
    kept_state = (
        source_rows,
        layernorm_first,
        horizontal_mixer,
        logits,
        blended_lines,
        after_row,
        layernorm_second,
        vertical_mixer,
        column_state,
        mixed_values,
        after_col,
        normal_c,
        upward,
        hidden,
    )
    return (result.astype(jnp.bfloat16), disorder_cost, kept_state)


def layer_backward(kept_state, family_residues, grad_result, projection_tables, head_count):
    (
        horizontal_coefficients,
        w_row_out,
        vertical_coefficients,
        w_col_out,
        w_up,
        w_down,
        gain_rows,
        bias_rows,
    ) = projection_tables
    (
        source_rows,
        layernorm_first,
        horizontal_mixer,
        logits,
        blended_lines,
        after_row,
        layernorm_second,
        vertical_mixer,
        column_state,
        mixed_values,
        after_col,
        normal_c,
        upward,
        hidden,
    ) = kept_state
    row_count, columns, model_width = source_rows.shape
    total_rows = row_count * lax.axis_size("seq")
    grad_branch_ffn = grad_result.astype(jnp.bfloat16)
    grad_hidden = product_back(grad_branch_ffn, w_down)
    grad_upward = jax.vjp(gelu_exact, upward)[1](grad_hidden)[0].astype(jnp.bfloat16)
    grad_normal_c = product_back(grad_upward, w_up)
    from_norm, gain_last, bias_last = jax.vjp(normed, after_col, gain_rows[2], bias_rows[2])[1](
        grad_normal_c
    )
    grad_col = grad_result + from_norm
    grad_branch_col = grad_col.astype(jnp.bfloat16)
    grad_attended = product_back(grad_branch_col, w_col_out).astype(jnp.bfloat16)
    everyone, log_total = column_state
    grad_query_col, grad_key_col, grad_value_col = column_backward(
        vertical_mixer[..., :model_width],
        everyone[..., :model_width],
        everyone[..., model_width:],
        log_total,
        grad_attended,
        head_count,
    )
    grad_kv_rows = lax.psum_scatter(
        jnp.concatenate([grad_key_col, grad_value_col], axis=-1).astype(jnp.bfloat16),
        "seq",
        scatter_dimension=0,
        tiled=True,
    ).astype(jnp.float32)
    grad_col_proj = jnp.concatenate([grad_query_col, grad_kv_rows], axis=-1).astype(jnp.bfloat16)
    grad_normal_b = product_back(grad_col_proj, vertical_coefficients)
    from_norm, gain_middle, bias_middle = jax.vjp(normed, after_row, gain_rows[1], bias_rows[1])[1](
        grad_normal_b
    )
    grad_row = grad_col + from_norm
    grad_branch_row = grad_row.astype(jnp.bfloat16)
    grad_mixed = split_heads(
        product_back(grad_branch_row, w_row_out).astype(jnp.bfloat16), head_count
    )
    queries, key_rows, content_lines = row_split(horizontal_mixer, model_width, head_count)
    softmax_share = jax.nn.softmax(logits, axis=-1)
    log_probs = jax.nn.log_softmax(logits, axis=-1)
    entropy = -jnp.sum(softmax_share * log_probs, axis=-1)
    partial_value = jnp.einsum(
        "rihe,rjhe->hij", grad_mixed, content_lines, preferred_element_type=jnp.float32
    )
    grad_probs = lax.psum(partial_value.astype(jnp.bfloat16), "seq").astype(jnp.float32)
    grad_values = jnp.einsum(
        "hij,rihe->rjhe",
        softmax_share.astype(jnp.bfloat16),
        grad_mixed,
        preferred_element_type=jnp.float32,
    )
    valid_residues = (jnp.arange(columns, dtype=jnp.int32) < family_residues).astype(jnp.float32)
    column_weight = float(total_rows * columns) * valid_residues / float(head_count * columns)
    grad_logits = softmax_share * (
        grad_probs - jnp.sum(softmax_share * grad_probs, axis=-1, keepdims=True)
    )
    grad_logits = grad_logits - column_weight[None, :, None] * softmax_share * (
        log_probs + entropy[..., None]
    )
    grad_logits = grad_logits.astype(jnp.bfloat16)
    logit_factor = 1.0 / (math.sqrt(model_width // head_count) * math.sqrt(total_rows))
    grad_queries = logit_factor * jnp.einsum(
        "vyp,opvl->oyvl", grad_logits, key_rows, preferred_element_type=jnp.float32
    )
    grad_keys = logit_factor * jnp.einsum(
        "hij,rihe->rjhe", grad_logits, queries, preferred_element_type=jnp.float32
    )
    grad_row_proj = jnp.concatenate(
        [
            grad_queries.reshape(row_count, columns, model_width),
            grad_keys.reshape(row_count, columns, model_width),
            grad_values.reshape(row_count, columns, model_width),
        ],
        axis=-1,
    ).astype(jnp.bfloat16)
    grad_normal_a = product_back(grad_row_proj, horizontal_coefficients)
    from_norm, gain_first, bias_first = jax.vjp(
        normed, source_rows.astype(jnp.float32), gain_rows[0], bias_rows[0]
    )[1](grad_normal_a)
    grad_source = (grad_row + from_norm).astype(jnp.bfloat16)
    operand_pairs = (
        (layernorm_first, grad_row_proj),
        (blended_lines, grad_branch_row),
        (layernorm_second, grad_col_proj),
        (mixed_values, grad_branch_col),
        (normal_c, grad_upward),
        (hidden, grad_branch_ffn),
    )
    norm_grads = (
        jnp.stack([gain_first, gain_middle, gain_last]),
        jnp.stack([bias_first, bias_middle, bias_last]),
    )
    return (grad_source, operand_pairs, norm_grads)


def on_device(
    embedded_families,
    order,
    token_quarter_factor,
    genuine_residue_tally,
    standardizer_scales,
    standardizer_offsets,
    row_qkv,
    row_out,
    col_qkv,
    col_out,
    ffn_up,
    ffn_down,
    upstream_sensitivity,
):
    head_count = HEAD_TALLY
    segment_place = lax.axis_index("pipe")
    gathered = (
        lax.all_gather(row_qkv, "seq", axis=1, tiled=True),
        lax.all_gather(row_out, "seq", axis=1, tiled=True),
        lax.all_gather(col_qkv, "seq", axis=1, tiled=True),
        lax.all_gather(col_out, "seq", axis=1, tiled=True),
        lax.all_gather(ffn_up, "seq", axis=1, tiled=True),
        lax.all_gather(ffn_down, "seq", axis=1, tiled=True),
        lax.all_gather(standardizer_scales.astype(jnp.bfloat16), "seq", axis=2, tiled=True).astype(
            standardizer_scales.dtype
        ),
        lax.all_gather(standardizer_offsets.astype(jnp.bfloat16), "seq", axis=2, tiled=True).astype(
            standardizer_offsets.dtype
        ),
    )
    projection_tables = tuple((gathered_piece[0] for gathered_piece in gathered))
    small_batch_number = embedded_families.shape[0]
    sequence = order[0]
    received = jnp.zeros(embedded_families.shape[1:], jnp.bfloat16)
    results = []
    focus_spread_levies = []
    kept_list = []
    for period in range(small_batch_number + 1):
        slot_here = jnp.clip(period - segment_place, 0, small_batch_number - 1)
        align_here = sequence[slot_here]
        source_rows = jnp.where(segment_place == 0, embedded_families[align_here], received)
        result, disorder_cost, kept_state = layer_forward(
            source_rows, genuine_residue_tally[align_here], projection_tables, head_count
        )
        results.append(result)
        focus_spread_levies.append(disorder_cost)
        kept_list.append(kept_state)
        if period < small_batch_number:
            received = shifted(result, "pipe", 1)
    activations = lax.dynamic_slice_in_dim(jnp.stack(results), segment_place, small_batch_number, 0)
    penalty_output = lax.dynamic_slice_in_dim(
        jnp.stack(focus_spread_levies), segment_place, small_batch_number, 0
    )
    grad_received = jnp.zeros(embedded_families.shape[1:], jnp.bfloat16)
    left_lists = [[] for index in range(6)]
    right_lists = [[] for index in range(6)]
    gain_total = None
    bias_total = None
    grad_sources = []
    for period in range(small_batch_number + 1):
        slot_raw = period - 1 + segment_place
        in_range = jnp.logical_and(slot_raw >= 0, slot_raw < small_batch_number)
        slot_here = jnp.clip(slot_raw, 0, small_batch_number - 1)
        align_here = sequence[slot_here]
        kept_state = choose(
            segment_place == 0,
            kept_list[max(period - 1, 0)],
            kept_list[min(period + 1, small_batch_number)],
        )
        outgrad = (
            upstream_sensitivity[slot_here].astype(jnp.float32)
            * token_quarter_factor[align_here].astype(jnp.float32)[..., None]
            * 0.25
        )
        incoming_grad = jnp.where(segment_place == 1, outgrad, grad_received.astype(jnp.float32))
        grad_source, operand_pairs, norm_grads = layer_backward(
            kept_state,
            genuine_residue_tally[align_here],
            incoming_grad,
            projection_tables,
            head_count,
        )
        for index in range(6):
            left_lists[index].append(operand_pairs[index][0])
            right_lists[index].append(
                jnp.where(
                    in_range, operand_pairs[index][1], jnp.zeros_like(operand_pairs[index][1])
                )
            )
        gain_term = jnp.where(in_range, norm_grads[0], jnp.zeros_like(norm_grads[0]))
        bias_term = jnp.where(in_range, norm_grads[1], jnp.zeros_like(norm_grads[1]))
        gain_total = gain_term if gain_total is None else gain_total + gain_term
        bias_total = bias_term if bias_total is None else bias_total + bias_term
        grad_sources.append(grad_source)
        if period < small_batch_number:
            grad_received = shifted(grad_source, "pipe", -1)
    block_entry_derivs = lax.dynamic_slice_in_dim(
        jnp.stack(grad_sources), 1 - segment_place, small_batch_number, 0
    )
    weight_totals = [
        weight_term(
            jnp.concatenate(left_lists[index], axis=0), jnp.concatenate(right_lists[index], axis=0)
        )
        for index in range(6)
    ]
    shared = (
        lax.psum_scatter(
            weight_totals[0].astype(jnp.bfloat16), "seq", scatter_dimension=0, tiled=True
        ).astype(jnp.float32),
        lax.psum_scatter(
            weight_totals[1].astype(jnp.bfloat16), "seq", scatter_dimension=0, tiled=True
        ).astype(jnp.float32),
        lax.psum_scatter(
            weight_totals[2].astype(jnp.bfloat16), "seq", scatter_dimension=0, tiled=True
        ).astype(jnp.float32),
        lax.psum_scatter(
            weight_totals[3].astype(jnp.bfloat16), "seq", scatter_dimension=0, tiled=True
        ).astype(jnp.float32),
        lax.psum_scatter(
            weight_totals[4].astype(jnp.bfloat16), "seq", scatter_dimension=0, tiled=True
        ).astype(jnp.float32),
        lax.psum_scatter(
            weight_totals[5].astype(jnp.bfloat16), "seq", scatter_dimension=0, tiled=True
        ).astype(jnp.float32),
        lax.psum_scatter(
            gain_total.astype(jnp.bfloat16), "seq", scatter_dimension=1, tiled=True
        ).astype(jnp.float32),
        lax.psum_scatter(
            bias_total.astype(jnp.bfloat16), "seq", scatter_dimension=1, tiled=True
        ).astype(jnp.float32),
    )
    (
        shared_row_qkv,
        shared_row_out,
        shared_col_qkv,
        shared_col_out,
        shared_up,
        shared_down,
        shared_gain,
        shared_bias,
    ) = shared
    summed = (
        lax.psum(shared_row_qkv.astype(jnp.bfloat16), "dp").astype(jnp.float32),
        lax.psum(shared_row_out.astype(jnp.bfloat16), "dp").astype(jnp.float32),
        lax.psum(shared_col_qkv.astype(jnp.bfloat16), "dp").astype(jnp.float32),
        lax.psum(shared_col_out.astype(jnp.bfloat16), "dp").astype(jnp.float32),
        lax.psum(shared_up.astype(jnp.bfloat16), "dp").astype(jnp.float32),
        lax.psum(shared_down.astype(jnp.bfloat16), "dp").astype(jnp.float32),
        lax.psum(shared_gain.astype(jnp.bfloat16), "dp").astype(jnp.float32),
        lax.psum(shared_bias.astype(jnp.bfloat16), "dp").astype(jnp.float32),
    )
    return (
        activations[None],
        block_entry_derivs[None],
        penalty_output[None],
        summed[0][None],
        summed[1][None],
        summed[2][None],
        summed[3][None],
        summed[4][None],
        summed[5][None],
        summed[6][None],
        summed[7][None],
    )


def solution(mesh):
    in_specs = (
        P("dp", "seq", None, None),
        P("dp", None),
        P("dp", "seq", None),
        P("dp"),
        P("pipe", None, "seq"),
        P("pipe", None, "seq"),
        P("pipe", "seq", None),
        P("pipe", "seq", None),
        P("pipe", "seq", None),
        P("pipe", "seq", None),
        P("pipe", "seq", None),
        P("pipe", "seq", None),
        P("dp", "seq", None, None),
    )
    out_specs = (
        P("pipe", "dp", "seq", None, None),
        P("pipe", "dp", "seq", None, None),
        P("pipe", "dp"),
        P("pipe", "seq", None),
        P("pipe", "seq", None),
        P("pipe", "seq", None),
        P("pipe", "seq", None),
        P("pipe", "seq", None),
        P("pipe", "seq", None),
        P("pipe", None, "seq"),
        P("pipe", None, "seq"),
    )
    return jax.shard_map(
        on_device, mesh=mesh, in_specs=in_specs, out_specs=out_specs, check_vma=False
    )
```

profile of v0, /device:TPU:0, one launch (start us, length us, event | category | flops | bytes accessed | tf_op | source)
XLA Modules:
  0.0 1591.1 jit_solution(9706193364601322542)
XLA Ops:
  12.5 19.4 %all_gather.33 = bf16[1,3,768]{1,0,2:T(2,128)(2,1)S(1)} all-gather(bf16[1,3,192]{1,0,2:T(2,128)(2,1)S(1)} %copy.344), channel_id=1, replica_groups=mesh['pipe'=2,'seq'=4,'dp'=4] {'seq'}, dimensions={2}, use_global_device_ids=true | all-gather | bytes 5760 | tf_op jit(solution)/shard_map/all_gather | solution.py:348
  32.3 18.9 %all_gather.34 = bf16[1,3,768]{1,0,2:T(2,128)(2,1)S(1)} all-gather(bf16[1,3,192]{1,0,2:T(2,128)(2,1)S(1)} %copy.346), channel_id=1, replica_groups=mesh['pipe'=2,'seq'=4,'dp'=4] {'seq'}, dimensions={2}, use_global_device_ids=true | all-gather | bytes 5760 | tf_op jit(solution)/shard_map/all_gather | solution.py:351
  68.3 22.7 %all-gather.10.cloned.1.call-done = bf16[1,768,2304]{2,1,0:T(8,128)(2,1)} async-done(((bf16[1,192,2304]{2,1,0:T(8,128)(2,1)}), bf16[1,768,2304]{2,1,0:T(8,128)(2,1)}) %all-gather.10.cloned.1.call-update) | async-done | bytes 3538960 | tf_op jit(solution)/shard_map/all_gather | solution.py:342
  96.8 34.9 %all-reduce.10.cloned.1.call-done = bf16[12,128,128]{2,1,0:T(8,128)(2,1)} async-done(((bf16[12,128,128]{2,1,0:T(8,128)(2,1)}), bf16[12,128,128]{2,1,0:T(8,128)(2,1)}) %all-reduce.10.cloned.1.call-update) | async-done | bytes 393232 | tf_op jit(solution)/shard_map/psum | solution.py:154
  136.2 27.4 %all-gather.12.cloned.1.call-done = bf16[1,768,768]{2,1,0:T(8,128)(2,1)} async-done(((bf16[1,192,768]{2,1,0:T(8,128)(2,1)}), bf16[1,768,768]{2,1,0:T(8,128)(2,1)}) %all-gather.12.cloned.1.call-update) | async-done | bytes 1179664 | tf_op jit(solution)/shard_map/all_gather | solution.py:343
  165.5 68.7 %all-gather.14.cloned.1.call-done = bf16[1,768,2304]{2,1,0:T(8,128)(2,1)} async-done(((bf16[1,192,2304]{2,1,0:T(8,128)(2,1)}), bf16[1,768,2304]{2,1,0:T(8,128)(2,1)}) %all-gather.14.cloned.1.call-update) | async-done | bytes 3538960 | tf_op jit(solution)/shard_map/all_gather | solution.py:344
  240.9 32.7 %all-gather.16.cloned.1.call-done = bf16[4,128,1536]{2,1,0:T(8,128)(2,1)} async-done(((bf16[1,128,1536]{2,1,0:T(8,128)(2,1)}), bf16[4,128,1536]{2,1,0:T(8,128)(2,1)}) %all-gather.16.cloned.1.call-update) | async-done | bytes 1572880 | tf_op jit(solution)/shard_map/all_gather | solution.py:170
  277.3 27.1 %all-gather.18.cloned.1.call-done = bf16[1,768,768]{2,1,0:T(8,128)(2,1)} async-done(((bf16[1,192,768]{2,1,0:T(8,128)(2,1)}), bf16[1,768,768]{2,1,0:T(8,128)(2,1)}) %all-gather.18.cloned.1.call-update) | async-done | bytes 1179664 | tf_op jit(solution)/shard_map/all_gather | solution.py:345
  306.4 88.2 %all-gather.20.cloned.1.call-done = bf16[1,768,3072]{2,1,0:T(8,128)(2,1)} async-done(((bf16[1,192,3072]{2,1,0:T(8,128)(2,1)}), bf16[1,768,3072]{2,1,0:T(8,128)(2,1)}) %all-gather.20.cloned.1.call-update) | async-done | bytes 4718608 | tf_op jit(solution)/shard_map/all_gather | solution.py:346
  402.4 81.7 %all-gather.22.cloned.1.call-done = bf16[1,3072,768]{2,1,0:T(8,128)(2,1)} async-done(((bf16[1,768,768]{2,1,0:T(8,128)(2,1)}), bf16[1,3072,768]{2,1,0:T(8,128)(2,1)}) %all-gather.22.cloned.1.call-update) | async-done | bytes 4718608 | tf_op jit(solution)/shard_map/all_gather | solution.py:347
  503.0 36.6 %all-reduce.12.cloned.1.call-done = bf16[12,128,128]{2,1,0:T(8,128)(2,1)} async-done(((bf16[12,128,128]{2,1,0:T(8,128)(2,1)}), bf16[12,128,128]{2,1,0:T(8,128)(2,1)}) %all-reduce.12.cloned.1.call-update) | async-done | bytes 393232 | tf_op jit(solution)/shard_map/psum | solution.py:154
  691.7 28.2 %all-reduce.20.cloned.1.call-done = (bf16[12,128,128]{2,1,0:T(8,128)(2,1)}, bf16[12,128,128]{2,1,0:T(8,128)(2,1)}) async-done(((bf16[12,128,128]{2,1,0:T(8,128)(2,1)}, bf16[12,128,128]{2,1,0:T(8,128)(2,1)}), (bf16[12,128,128]{2,1,0:T(8,128)(2,1)}, bf16[12,128,128]{2,1,0:T(8,128)(2,1)})) %all-reduce.20.cloned.1.call-update) | async-done | bytes 786448 | tf_op jit(solution)/shard_map/psum | solution.py:273
  731.0 11.1 fusion.240
  772.4 20.8 %all-gather.26.cloned.1.call-done = bf16[4,128,1536]{2,1,0:T(8,128)(2,1)} async-done(((bf16[1,128,1536]{2,1,0:T(8,128)(2,1)}), bf16[4,128,1536]{2,1,0:T(8,128)(2,1)}) %all-gather.26.cloned.1.call-update) | async-done | bytes 1572880 | tf_op jit(solution)/shard_map/all_gather | solution.py:170
  889.6 29.2 %all-reduce.14.cloned.1.call-done = bf16[12,128,128]{2,1,0:T(8,128)(2,1)} async-done(((bf16[12,128,128]{2,1,0:T(8,128)(2,1)}), bf16[12,128,128]{2,1,0:T(8,128)(2,1)}) %all-reduce.14.cloned.1.call-update) | async-done | bytes 393232 | tf_op jit(solution)/shard_map/psum | solution.py:273
  918.8 11.2 fusion.243
  930.0 11.2 fusion.242
  991.4 26.8 %reduce-scatter.20.cloned.1.call-done = bf16[1,128,1536]{2,1,0:T(8,128)(2,1)} async-done(((bf16[4,128,1536]{2,1,0:T(8,128)(2,1)}), bf16[1,128,1536]{2,1,0:T(8,128)(2,1)}) %reduce-scatter.20.cloned.1.call-update) | async-done | bytes 393232 | tf_op jit(solution)/shard_map/reduce_scatter | solution.py:250
  1134.5 75.0 %reduce-scatter.30.cloned.1.call-done = bf16[192,3072]{1,0:T(8,128)(2,1)} async-done(((bf16[768,3072]{1,0:T(8,128)(2,1)}), bf16[192,3072]{1,0:T(8,128)(2,1)}) %reduce-scatter.30.cloned.1.call-update) | async-done | bytes 1179664 | tf_op jit(solution)/shard_map/reduce_scatter | solution.py:443
  1209.5 88.1 %reduce-scatter.32.cloned.1.call-done = bf16[768,768]{1,0:T(8,128)(2,1)} async-done(((bf16[3072,768]{1,0:T(8,128)(2,1)}), bf16[768,768]{1,0:T(8,128)(2,1)}) %reduce-scatter.32.cloned.1.call-update) | async-done | bytes 1179664 | tf_op jit(solution)/shard_map/reduce_scatter | solution.py:446
  1297.6 69.2 %reduce-scatter.26.cloned.1.call-done = bf16[192,2304]{1,0:T(8,128)(2,1)} async-done(((bf16[768,2304]{1,0:T(8,128)(2,1)}), bf16[192,2304]{1,0:T(8,128)(2,1)}) %reduce-scatter.26.cloned.1.call-update) | async-done | bytes 884752 | tf_op jit(solution)/shard_map/reduce_scatter | solution.py:437
  1366.8 69.0 %reduce-scatter.22.cloned.1.call-done = bf16[192,2304]{1,0:T(8,128)(2,1)} async-done(((bf16[768,2304]{1,0:T(8,128)(2,1)}), bf16[192,2304]{1,0:T(8,128)(2,1)}) %reduce-scatter.22.cloned.1.call-update) | async-done | bytes 884752 | tf_op jit(solution)/shard_map/reduce_scatter | solution.py:431
  1459.1 19.1 %reduce-scatter.36.cloned.1.call-done = bf16[192,3]{1,0:T(8,128)(2,1)} async-done(((bf16[768,3]{1,0:T(8,128)(2,1)}), bf16[192,3]{1,0:T(8,128)(2,1)}) %reduce-scatter.36.cloned.1.call-update) | async-done | bytes 1168
  1485.9 88.1 %all-reduce.18.cloned.1.call-done = (bf16[1,192,2304]{2,1,0:T(8,128)(2,1)}, bf16[1,192,768]{2,1,0:T(8,128)(2,1)}, bf16[1,192,2304]{2,1,0:T(8,128)(2,1)}, bf16[1,...) async-done(((bf16[1,192,2304]{2,1,0:T(8,128)(2,1)}, bf16[1,192,768]{2,1,0:T(8,128)(2,1)}, bf16[1,192,2304]{2,1,0:T(8,128)(2,1)}, ...) | async-done | bytes 4718608 | tf_op jit(solution)/shard_map/psum | solution.py:467
  (1042 shorter events, 553.7 us)
Async XLA Ops:
  7.2 83.9 %all-gather.10.cloned.1.call-start = ((), (), s32[]{:S(2)}) async-start(), calls=%async_computation.11 | async-start | bytes 4423680 | tf_op jit(solution)/shard_map/all_gather | solution.py:342
  7.9 123.9 %all-reduce.10.cloned.1.call-start = ((), (), s32[]{:S(2)}) async-start(), calls=%async_computation.12 | async-start | bytes 786432 | tf_op jit(solution)/shard_map/psum | solution.py:154
  96.1 138.1 %all-gather.14.cloned.1.call-start = ((), (), s32[]{:S(2)}) async-start(), calls=%async_computation.14 | async-start | bytes 4423680 | tf_op jit(solution)/shard_map/all_gather | solution.py:344
  96.6 177.0 %all-gather.16.cloned.1.call-start = ((), (), s32[]{:S(2)}) async-start(), calls=%async_computation.15 | async-start | bytes 1966080 | tf_op jit(solution)/shard_map/all_gather | solution.py:170
  238.3 156.3 %all-gather.20.cloned.1.call-start = ((), (), s32[]{:S(2)}) async-start(), calls=%async_computation.17 | async-start | bytes 5898240 | tf_op jit(solution)/shard_map/all_gather | solution.py:346
  239.1 245.1 %all-gather.22.cloned.1.call-start = ((), (), s32[]{:S(2)}) async-start(), calls=%async_computation.18 | async-start | bytes 5898240 | tf_op jit(solution)/shard_map/all_gather | solution.py:347
  239.8 299.8 %all-reduce.12.cloned.1.call-start = ((), (), s32[]{:S(2)}) async-start(), calls=%async_computation.19 | async-start | bytes 786432 | tf_op jit(solution)/shard_map/psum | solution.py:154
  502.8 83.8 %all-gather.24.cloned.1.call-start = ((), (), s32[]{:S(2)}) async-start(), calls=%async_computation.20 | async-start | bytes 1966080 | tf_op jit(solution)/shard_map/all_gather | solution.py:170
  549.8 116.3 %reduce-scatter.16.cloned.1.call-start = ((), (), s32[]{:S(2)}) async-start(), calls=%async_computation.22 | async-start | bytes 1966080 | tf_op jit(solution)/shard_map/reduce_scatter | solution.py:250
  631.8 88.1 %all-reduce.20.cloned.1.call-start = ((), (), s32[]{:S(2)}) async-start(), calls=%async_computation.36 | async-start | bytes 1572864 | tf_op jit(solution)/shard_map/psum | solution.py:273
  676.7 116.5 %all-gather.26.cloned.1.call-start = ((), (), s32[]{:S(2)}) async-start(), calls=%async_computation.21 | async-start | bytes 1966080 | tf_op jit(solution)/shard_map/all_gather | solution.py:170
  756.8 115.1 %reduce-scatter.18.cloned.1.call-start = ((), (), s32[]{:S(2)}) async-start(), calls=%async_computation.23 | async-start | bytes 1966080 | tf_op jit(solution)/shard_map/reduce_scatter | solution.py:250
  838.5 80.3 %all-reduce.14.cloned.1.call-start = ((), (), s32[]{:S(2)}) async-start(), calls=%async_computation.24 | async-start | bytes 786432 | tf_op jit(solution)/shard_map/psum | solution.py:273
  882.5 135.7 %reduce-scatter.20.cloned.1.call-start = ((), (), s32[]{:S(2)}) async-start(), calls=%async_computation.25 | async-start | bytes 1966080 | tf_op jit(solution)/shard_map/reduce_scatter | solution.py:250
  984.1 82.3 %all-reduce.16.cloned.1.call-start = ((), (), s32[]{:S(2)}) async-start(), calls=%async_computation.26 | async-start | bytes 786432 | tf_op jit(solution)/shard_map/psum | solution.py:273
  1024.8 109.7 %reduce-scatter.28.cloned.1.call-start = ((), (), s32[]{:S(2)}) async-start(), calls=%async_computation.30 | async-start | bytes 1474560 | tf_op jit(solution)/shard_map/reduce_scatter | solution.py:440
  1026.8 107.7 %reduce-scatter.24.cloned.1.call-start = ((), (), s32[]{:S(2)}) async-start(), calls=%async_computation.28 | async-start | bytes 1474560 | tf_op jit(solution)/shard_map/reduce_scatter | solution.py:434
  1028.7 180.7 %reduce-scatter.30.cloned.1.call-start = ((), (), s32[]{:S(2)}) async-start(), calls=%async_computation.31 | async-start | bytes 5898240 | tf_op jit(solution)/shard_map/reduce_scatter | solution.py:443
  1035.7 261.9 %reduce-scatter.32.cloned.1.call-start = ((), (), s32[]{:S(2)}) async-start(), calls=%async_computation.32 | async-start | bytes 5898240 | tf_op jit(solution)/shard_map/reduce_scatter | solution.py:446
  1047.5 319.3 %reduce-scatter.26.cloned.1.call-start = ((), (), s32[]{:S(2)}) async-start(), calls=%async_computation.29 | async-start | bytes 4423680 | tf_op jit(solution)/shard_map/reduce_scatter | solution.py:437
  1053.8 382.0 %reduce-scatter.22.cloned.1.call-start = ((), (), s32[]{:S(2)}) async-start(), calls=%async_computation.27 | async-start | bytes 4423680 | tf_op jit(solution)/shard_map/reduce_scatter | solution.py:431
  1091.5 366.7 %reduce-scatter.34.cloned.1.call-start = ((), (), s32[]{:S(2)}) async-start(), calls=%async_computation.33 | async-start | bytes 245760
  1131.4 346.7 %reduce-scatter.36.cloned.1.call-start = ((), (), s32[]{:S(2)}) async-start(), calls=%async_computation.34 | async-start | bytes 245760
  1133.1 440.9 %all-reduce.18.cloned.1.call-start = ((), (), s32[]{:S(2)}) async-start(), calls=%async_computation.35 | async-start | bytes 9437184 | tf_op jit(solution)/shard_map/psum | solution.py:467
  (294 other events, 2188.0 us)
Sparse Core Ops, SparseCore 0:
  9.6 81.4 all-gather.9
  95.4 36.3 all-reduce.9
  133.4 30.0 all-gather.11
  165.0 69.0 all-gather.13
  237.9 35.6 all-gather.15
  275.1 29.2 all-gather.17
  306.1 88.5 all-gather.19
  396.3 87.8 all-gather.21
  502.9 36.6 all-reduce.11
  549.9 36.6 all-gather.23
  631.9 34.1 reduce-scatter.15
  676.9 42.9 all-reduce.19
  756.9 36.3 all-gather.25
  838.6 33.2 reduce-scatter.17
  882.7 36.0 all-reduce.13
  984.2 33.9 reduce-scatter.19
  1024.9 35.8 all-reduce.15
  1063.5 28.8 reduce-scatter.27
  1095.3 27.9 reduce-scatter.23
  1125.5 83.9 reduce-scatter.29
  1211.8 85.7 reduce-scatter.31
  1299.9 66.8 reduce-scatter.25
  1369.1 66.6 reduce-scatter.21
  1480.8 93.1 all-reduce.17
  (2 shorter events, 37.1 us)
where the time goes:
time: 1610 us; the launch traced here: 1590 us
  waiting for transfers between devices  970 us (60%)
  matrix products  199 us (12%)
  other arithmetic  178 us (11%)
  local copies, waits for them, and re-layouts  155 us (10%)
  blocking collectives  44 us (3%)
  between operations  31.9 us (2%)
    all_gather x1, waiting for transfers between devices, on_device(): lax.all_gather(ffn_up, 'seq', axis=1, tiled=True)  88.2 us
    reduce_scatter x1, waiting for transfers between devices, on_device(): lax.psum_scatter(weight_totals[5].astype(jnp.bfloat16), 'seq', scatter_di...  88.1 us
    psum x1, waiting for transfers between devices, on_device(): lax.psum(shared_row_qkv.astype(jnp.bfloat16), 'dp').astype(jnp.float32)  88.1 us
    all_gather x1, waiting for transfers between devices, on_device(): lax.all_gather(ffn_down, 'seq', axis=1, tiled=True)  81.7 us
    reduce_scatter x1, waiting for transfers between devices, on_device(): lax.psum_scatter(weight_totals[4].astype(jnp.bfloat16), 'seq', scatter_di...  75 us
    psum x2, waiting for transfers between devices, layer_forward(): lax.psum(partial_value.astype(jnp.bfloat16), 'seq').astype(jnp.float32)  71.5 us
    reduce_scatter x1, waiting for transfers between devices, on_device(): lax.psum_scatter(weight_totals[2].astype(jnp.bfloat16), 'seq', scatter_di...  69.2 us
    reduce_scatter x1, waiting for transfers between devices, on_device(): lax.psum_scatter(weight_totals[0].astype(jnp.bfloat16), 'seq', scatter_di...  69 us
  transfers between devices with their start and end apart: 30, of which 26 were waited for; matrix products, arithmetic and copies ran while one was open for 18% of the time, Pallas kernels for 0%

commit v1 on v0

--- a/solution.py
+++ b/solution.py
@@ -1,11 +1,16 @@
+import functools
 import math
 
 import jax
 import jax.numpy as jnp
 from jax import lax
+from jax.experimental import pallas as pl
+from jax.experimental.pallas import tpu as pltpu
 from jax.sharding import PartitionSpec as P
 
 HEAD_TALLY = 12
+LINE = 4
+MESH = pl.DeviceIdType.MESH
 
 
 norm_epsilon = 1e-05
@@ -488,6 +493,1030 @@
     )
 
 
+def place():
+    pipe, seq, dp = (lax.axis_index("pipe"), lax.axis_index("seq"), lax.axis_index("dp"))
+    core = lax.rem(dp, 2)
+    pair = lax.div(dp, 2)
+    return (pipe, seq, dp, core, pair)
+
+
+def neighbours(pipe, seq, dp, core, pair):
+    other_core = (pipe, seq, dp + 1 - 2 * core)
+    other_pair = (pipe, seq, dp + 2 - 4 * pair)
+    return (other_core, other_pair)
+
+
+def greet(pipe, seq, dp, core, pair):
+    barrier = pltpu.get_barrier_semaphore()
+    other_core, other_pair = neighbours(pipe, seq, dp, core, pair)
+    count = 0
+    for step in range(LINE):
+        for flip in range(2):
+            if step == 0 and flip == 0:
+                continue
+            where = dp if flip == 0 else dp + 1 - 2 * core
+            pl.semaphore_signal(
+                barrier,
+                inc=1,
+                device_id=(pipe, lax.rem(seq + step, LINE), where),
+                device_id_type=MESH,
+            )
+            count += 1
+    pl.semaphore_signal(barrier, inc=1, device_id=other_pair, device_id_type=MESH)
+    pl.semaphore_wait(barrier, count + 1)
+
+
+def remote(source, target, send, recv, device):
+    return pltpu.make_async_remote_copy(
+        src_ref=source,
+        dst_ref=target,
+        send_sem=send,
+        recv_sem=recv,
+        device_id=device,
+        device_id_type=MESH,
+    )
+
+
+def swap_rows(source, target, send, recv, local, where):
+    pipe, seq, dp, core, pair = where
+    half, rest = (lax.div(seq, 2), lax.rem(seq, 2))
+
+    def each(action):
+        for index in range(2):
+            line = 2 * core + index
+            here = jnp.logical_and(line == seq, half == core)
+            copy = remote(
+                source.at[index],
+                target.at[rest],
+                send.at[index],
+                recv.at[rest],
+                (pipe, line, dp - core + half),
+            )
+            arriving = remote(
+                source.at[index],
+                target.at[index],
+                send.at[index],
+                recv.at[index],
+                (pipe, line, dp - core + half),
+            )
+            inside = pltpu.make_async_copy(source.at[index], target.at[rest], local)
+            action(here, copy, arriving, inside)
+
+    def start(here, copy, arriving, inside):
+        pl.when(here)(inside.start)
+        pl.when(jnp.logical_not(here))(copy.start)
+
+    def finish(here, copy, arriving, inside):
+        pl.when(here)(inside.wait)
+        pl.when(jnp.logical_not(here))(copy.wait_send)
+        pl.when(jnp.logical_not(here))(arriving.wait_recv)
+
+    return (lambda: each(start), lambda: each(finish))
+
+
+def gather_kernel(*refs):
+    shards, refs = (refs[:6], refs[6:])
+    piece, meta, rows = refs[:3]
+    wholes, refs = (refs[3:9], refs[9:])
+    piece_out, meta_out, rows_out = refs[:3]
+    (
+        own_sem,
+        line_send,
+        line_recv,
+        pair_send,
+        pair_recv,
+        core_send,
+        core_recv,
+        piece_send,
+        piece_recv,
+        meta_send,
+        meta_recv,
+        rows_send,
+        rows_recv,
+    ) = refs[3:]
+    where = place()
+    pipe, seq, dp, core, pair = where
+    other_core, other_pair = neighbours(*where)
+    quarter = dp
+    greet(*where)
+    right, left = ((pipe, seq + 1, dp), (pipe, seq - 1, dp))
+
+    def region(index, source, part):
+        depth = shards[index].shape[0]
+        share = depth // 4
+        start = pl.multiple_of(source * depth + part * share, share)
+        return wholes[index].at[pl.ds(start, share)]
+
+    start_piece, finish_piece = swap_rows(
+        piece, piece_out, piece_send, piece_recv, own_sem.at[7], where
+    )
+    start_meta, finish_meta = swap_rows(meta, meta_out, meta_send, meta_recv, own_sem.at[8], where)
+    start_meta()
+    start_piece()
+    row_copies = []
+    for step in range(1, LINE):
+        target = (pipe, lax.rem(seq + step, LINE), dp)
+        copy = remote(rows, rows_out.at[seq], rows_send.at[step - 1], rows_recv.at[seq], target)
+        copy.start()
+        row_copies.append(copy)
+    own = [pltpu.make_async_copy(rows, rows_out.at[seq], own_sem.at[6])]
+    for index in range(6):
+        depth = shards[index].shape[0]
+        own.append(
+            pltpu.make_async_copy(
+                shards[index],
+                wholes[index].at[pl.ds(pl.multiple_of(seq * depth, depth), depth)],
+                own_sem.at[index],
+            )
+        )
+
+    for index in range(6):
+        share = shards[index].shape[0] // 4
+        mine = shards[index].at[pl.ds(pl.multiple_of(quarter * share, share), share)]
+
+        @pl.when(seq < LINE - 1)
+        def _():
+            remote(
+                mine,
+                region(index, seq, quarter),
+                line_send.at[0, seq, index],
+                line_recv.at[seq, index],
+                right,
+            ).start()
+
+        @pl.when(seq > 0)
+        def _():
+            remote(
+                mine,
+                region(index, seq, quarter),
+                line_send.at[1, seq, index],
+                line_recv.at[seq, index],
+                left,
+            ).start()
+
+    for copy in own:
+        copy.start()
+
+    def over(kind, source, index, part, target):
+        block = region(index, source, part)
+        if kind == "pair":
+            return remote(
+                block, block, pair_send.at[source, index], pair_recv.at[source, index], target
+            )
+        lane = 0 if kind == "core" else 1
+        return remote(
+            block,
+            block,
+            core_send.at[lane, source, index],
+            core_recv.at[lane, source, index],
+            target,
+        )
+
+    def along(source, index, direction, target):
+        block = region(index, source, quarter)
+        return remote(
+            block,
+            block,
+            line_send.at[direction, source, index],
+            line_recv.at[source, index],
+            target,
+        )
+
+    across = quarter + 2 - 4 * pair
+    opposite = quarter + 1 - 2 * core
+    opposite_across = across + 1 - 2 * core
+
+    def arrive(step, index):
+        for direction in range(2):
+            source = seq - step if direction == 0 else seq + step
+            present = source >= 0 if direction == 0 else source < LINE
+            onward = seq < LINE - 1 if direction == 0 else seq > 0
+            target = right if direction == 0 else left
+
+            @pl.when(present)
+            def _():
+                along(source, index, direction, target).wait_recv()
+                over("pair", source, index, quarter, other_pair).start()
+                over("core", source, index, quarter, other_core).start()
+
+            @pl.when(jnp.logical_and(present, onward))
+            def _():
+                along(source, index, direction, target).start()
+
+    def forward(step, index):
+        for direction in range(2):
+            source = seq - step if direction == 0 else seq + step
+            present = source >= 0 if direction == 0 else source < LINE
+
+            @pl.when(present)
+            def _():
+                over("pair", source, index, across, other_pair).wait_recv()
+                over("relay", source, index, across, other_core).start()
+
+    events = [(step, index) for step in range(1, LINE) for index in range(6)]
+    lag = 2
+    for count in range(len(events) + lag):
+        if count < len(events):
+            arrive(*events[count])
+        if count >= lag:
+            forward(*events[count - lag])
+
+    for index in range(6):
+
+        @pl.when(seq < LINE - 1)
+        def _():
+            along(seq, index, 0, right).wait_send()
+
+        @pl.when(seq > 0)
+        def _():
+            along(seq, index, 1, left).wait_send()
+
+    for step, index in events:
+        for direction in range(2):
+            source = seq - step if direction == 0 else seq + step
+            present = source >= 0 if direction == 0 else source < LINE
+            onward = seq < LINE - 1 if direction == 0 else seq > 0
+            target = right if direction == 0 else left
+
+            @pl.when(present)
+            def _():
+                over("pair", source, index, quarter, other_pair).wait_send()
+                over("core", source, index, quarter, other_core).wait_send()
+                over("relay", source, index, across, other_core).wait_send()
+                over("core", source, index, opposite, other_core).wait_recv()
+                over("relay", source, index, opposite_across, other_core).wait_recv()
+
+            @pl.when(jnp.logical_and(present, onward))
+            def _():
+                along(source, index, direction, target).wait_send()
+
+    for copy in own:
+        copy.wait()
+    for step in range(1, LINE):
+        source = lax.rem(seq + LINE - step, LINE)
+        row_copies[step - 1].wait_send()
+        remote(
+            rows, rows_out.at[source], rows_send.at[step - 1], rows_recv.at[source], other_core
+        ).wait_recv()
+    finish_meta()
+    finish_piece()
+
+
+def gather_all(shards, piece, meta, rows):
+    anywhere = pl.BlockSpec(memory_space=pl.ANY)
+    dma = pltpu.SemaphoreType.DMA
+    shapes = [
+        jax.ShapeDtypeStruct((shard.shape[0] * LINE, shard.shape[1]), shard.dtype)
+        for shard in shards
+    ]
+    shapes += [
+        jax.ShapeDtypeStruct(piece.shape, piece.dtype),
+        jax.ShapeDtypeStruct(meta.shape, meta.dtype),
+        jax.ShapeDtypeStruct((LINE,) + rows.shape, rows.dtype),
+    ]
+    return pl.pallas_call(
+        gather_kernel,
+        out_shape=shapes,
+        in_specs=[anywhere] * 9,
+        out_specs=[anywhere] * 9,
+        scratch_shapes=[
+            dma((9,)),
+            dma((2, LINE, 6)),
+            dma((LINE, 6)),
+            dma((LINE, 6)),
+            dma((LINE, 6)),
+            dma((2, LINE, 6)),
+            dma((2, LINE, 6)),
+            dma((2,)),
+            dma((2,)),
+            dma((2,)),
+            dma((2,)),
+            dma((LINE - 1,)),
+            dma((LINE,)),
+        ],
+        compiler_params=pltpu.CompilerParams(collective_id=0, has_side_effects=True),
+        name="gather_weights",
+    )(*shards, piece, meta, rows)
+
+
+def reduce_kernel(chunks, paired, *refs):
+    grads, vector, first, second, cost = refs[:5]
+    out, vector_out, first_out, second_out, cost_out = refs[5:10]
+    (
+        mine,
+        from_core,
+        from_pair,
+        from_left,
+        from_right,
+        late_pair,
+        vec_core,
+        vec_pair,
+        vec_line,
+        load_sem,
+        core_send,
+        core_recv,
+        pair_send,
+        pair_recv,
+        line_send,
+        left_recv,
+        right_recv,
+        late_send,
+        late_recv,
+        share_send,
+        share_recv,
+        out_sem,
+        first_send,
+        first_recv,
+        second_send,
+        second_recv,
+        local_sem,
+        vec_send,
+        vec_recv,
+        cost_send,
+        cost_recv,
+    ) = refs[10:]
+    where = place()
+    pipe, seq, dp, core, pair = where
+    other_core, other_pair = neighbours(*where)
+    right, left = ((pipe, seq + 1, dp), (pipe, seq - 1, dp))
+    units = LINE * chunks
+    depth = mine.shape[2]
+    greet(*where)
+
+    def unit_of(number):
+        order = lax.div(number, chunks)
+        chunk = number - order * chunks
+        half = lax.div(order, 2)
+        target = jnp.where(lax.rem(order, 2) == 0, LINE - 1 - half, half)
+        return (target, chunk)
+
+    def window(chunk):
+        return pl.ds(pl.multiple_of(chunk * depth, depth), depth)
+
+    def load(number, side):
+        target, chunk = unit_of(number)
+        return pltpu.make_async_copy(
+            grads.at[target, 2 * side + core, window(chunk)],
+            mine.at[number, side],
+            load_sem.at[number, side],
+        )
+
+    def to_core(number, side):
+        target, chunk = unit_of(number)
+        return remote(
+            grads.at[target, 2 * side + 1 - core, window(chunk)],
+            from_core.at[number, side],
+            core_send.at[number, side],
+            core_recv.at[number, side],
+            other_core,
+        )
+
+    def issue(number, carry):
+        for side in range(2):
+            to_core(number, side).start()
+            load(number, side).start()
+        return carry
+
+    lax.fori_loop(0, units, issue, 0)
+
+    start_first, finish_first = swap_rows(
+        first, first_out, first_send, first_recv, local_sem.at[0], where
+    )
+    start_second, finish_second = swap_rows(
+        second, second_out, second_send, second_recv, local_sem.at[1], where
+    )
+    start_first()
+    start_second()
+
+    vec_first = remote(vector, vec_core, vec_send.at[0], vec_recv.at[0], other_core)
+    vec_first.start()
+    sender = core == lax.div(seq, 2)
+    spot = lax.rem(seq, 2)
+    cost_own = pltpu.make_async_copy(cost, cost_out.at[spot], local_sem.at[2])
+    cost_copies = [
+        remote(
+            cost,
+            cost_out.at[spot],
+            cost_send.at[step - 1],
+            cost_recv.at[spot],
+            (pipe, lax.rem(seq + step, LINE), dp),
+        )
+        for step in range(1, LINE)
+    ]
+
+    @pl.when(sender)
+    def _():
+        cost_own.start()
+        for copy in cost_copies:
+            copy.start()
+
+    def add(left_value, right_value):
+        return (left_value.astype(jnp.float32) + right_value.astype(jnp.float32)).astype(
+            jnp.bfloat16
+        )
+
+    def to_pair(number):
+        return remote(
+            mine.at[number, 1 - pair],
+            from_pair.at[number],
+            pair_send.at[number],
+            pair_recv.at[number],
+            other_pair,
+        )
+
+    def arrive(number, side):
+        load(number, side).wait()
+        to_core(number, side).wait_recv()
+        mine[number, side] = add(mine[number, side], from_core[number, side])
+
+    def line_copy(number, single, direction):
+        target = right if direction == 0 else left
+        landing = from_left if direction == 0 else from_right
+        sems = left_recv if direction == 0 else right_recv
+        if single:
+            return remote(
+                mine.at[number, pair],
+                landing.at[number, 0],
+                line_send.at[number],
+                sems.at[number],
+                target,
+            )
+        return remote(
+            mine.at[number], landing.at[number], line_send.at[number], sems.at[number], target
+        )
+
+    def take(number, single, direction):
+        landing = from_left if direction == 0 else from_right
+        line_copy(number, single, direction).wait_recv()
+        if single:
+            mine[number, pair] = add(mine[number, pair], landing[number, 0])
+        else:
+            for side in range(2):
+                mine[number, side] = add(mine[number, side], landing[number, side])
+
+    def late_copy(number, chunk, single):
+        if single:
+            return remote(
+                mine.at[number, pair],
+                out.at[dp, window(chunk)],
+                late_send.at[chunk],
+                late_recv.at[chunk],
+                other_pair,
+            )
+        return remote(
+            mine.at[number],
+            late_pair.at[chunk],
+            late_send.at[chunk],
+            late_recv.at[chunk],
+            other_pair,
+        )
+
+    def share_copy(number, chunk, side, relay):
+        spot_out = out.at[2 * side + core, window(chunk)]
+        return remote(
+            spot_out if relay else mine.at[number, side],
+            spot_out,
+            share_send.at[side, chunk],
+            share_recv.at[side, chunk],
+            other_core,
+        )
+
+    def out_copy(number, chunk, side):
+        return pltpu.make_async_copy(
+            mine.at[number, side], out.at[2 * side + core, window(chunk)], out_sem.at[side, chunk]
+        )
+
+    def at(number, condition, body):
+        clipped = jnp.clip(number, 0, units - 1)
+        target, chunk = unit_of(clipped)
+        valid = jnp.logical_and(number >= 0, number < units)
+        valid = jnp.logical_and(valid, condition(target))
+        if paired > 0:
+
+            @pl.when(jnp.logical_and(valid, chunk < paired))
+            def _():
+                body(clipped, chunk, True)
+
+        if paired < chunks:
+
+            @pl.when(jnp.logical_and(valid, chunk >= paired))
+            def _():
+                body(clipped, chunk, False)
+
+    def first_stage(number, chunk, single):
+        if single:
+            for half in range(2):
+                side = 1 - pair if half == 0 else pair
+                arrive(number, side)
+                if half == 0:
+                    to_pair(number).start()
+        else:
+            for side in range(2):
+                arrive(number, side)
+
+    def second_stage(number, chunk, single):
+        if single:
+            to_pair(number).wait_recv()
+            mine[number, pair] = add(mine[number, pair], from_pair[number])
+
+    def hop(direction):
+        def body(number, chunk, single):
+            @pl.when(seq > 0 if direction == 0 else seq < LINE - 1)
+            def _():
+                take(number, single, direction)
+
+            line_copy(number, single, direction).start()
+
+        return body
+
+    def last_stage(number, chunk, single):
+        for direction in range(2):
+
+            @pl.when(seq > 0 if direction == 0 else seq < LINE - 1)
+            def _():
+                take(number, single, direction)
+
+        late_copy(number, chunk, single).start()
+        if single:
+            out_copy(number, chunk, pair).start()
+            share_copy(number, chunk, pair, False).start()
+
+    def share_stage(number, chunk, single):
+        if single:
+            remote(
+                mine.at[number, pair],
+                out.at[dp + 2 - 4 * pair, window(chunk)],
+                late_send.at[chunk],
+                late_recv.at[chunk],
+                other_pair,
+            ).wait_recv()
+            share_copy(number, chunk, 1 - pair, True).start()
+        else:
+            late_copy(number, chunk, False).wait()
+            for side in range(2):
+                mine[number, side] = add(mine[number, side], late_pair[chunk, side])
+                out_copy(number, chunk, side).start()
+                share_copy(number, chunk, side, False).start()
+
+    pair_lag = 2
+    always = lambda target: target >= 0
+    far = jnp.maximum(seq, LINE - 1 - seq)
+
+    def step(number, carry):
+        at(number, always, first_stage)
+        at(number - pair_lag, always, second_stage)
+        at(number - pair_lag - seq, lambda target: target > seq, hop(0))
+        at(number - pair_lag - (LINE - 1 - seq), lambda target: target < seq, hop(1))
+        at(number - pair_lag - far, lambda target: target == seq, last_stage)
+        at(number - pair_lag - far - pair_lag, lambda target: target == seq, share_stage)
+        return carry
+
+    lax.fori_loop(0, units + 2 * pair_lag + LINE - 1, step, 0)
+
+    vec_first.wait()
+    vec_core[...] = vector[...] + vec_core[...]
+    vec_second = remote(vec_core, vec_pair, vec_send.at[1], vec_recv.at[1], other_pair)
+    vec_second.start()
+    vec_second.wait()
+    vec_pair[...] = vec_core[...] + vec_pair[...]
+    for move in range(1, LINE):
+        goal = lax.rem(seq + move, LINE)
+        remote(
+            vec_pair.at[goal],
+            vec_line.at[seq],
+            vec_send.at[1 + move],
+            vec_recv.at[2 + seq],
+            (pipe, goal, dp),
+        ).start()
+    vec_line[seq] = vec_pair[seq]
+    for move in range(1, LINE):
+        goal = lax.rem(seq + move, LINE)
+        source = lax.rem(seq + LINE - move, LINE)
+        remote(
+            vec_pair.at[goal],
+            vec_line.at[source],
+            vec_send.at[1 + move],
+            vec_recv.at[2 + source],
+            (pipe, goal, dp),
+        ).wait()
+    total = vec_line[0]
+    for source in range(1, LINE):
+        total = total + vec_line[source]
+    vector_out[...] = total
+
+    def drain(number, carry):
+        for side in range(2):
+            to_core(number, side).wait_send()
+
+        def sends(number, chunk, single):
+            if single:
+                to_pair(number).wait_send()
+
+        at(number, always, sends)
+        at(
+            number,
+            lambda target: target > seq,
+            lambda number, chunk, single: line_copy(number, single, 0).wait_send(),
+        )
+        at(
+            number,
+            lambda target: target < seq,
+            lambda number, chunk, single: line_copy(number, single, 1).wait_send(),
+        )
+
+        def shared(number, chunk, single):
+            if single:
+                late_copy(number, chunk, True).wait_send()
+                out_copy(number, chunk, pair).wait()
+                share_copy(number, chunk, pair, False).wait_send()
+                share_copy(number, chunk, 1 - pair, True).wait_send()
+            else:
+                for side in range(2):
+                    out_copy(number, chunk, side).wait()
+                    share_copy(number, chunk, side, False).wait_send()
+            for side in range(2):
+                spot_out = out.at[2 * side + 1 - core, window(chunk)]
+                remote(
+                    spot_out,
+                    spot_out,
+                    share_send.at[side, chunk],
+                    share_recv.at[side, chunk],
+                    other_core,
+                ).wait_recv()
+
+        at(number, lambda target: target == seq, shared)
+        return carry
+
+    lax.fori_loop(0, units, drain, 0)
+
+    @pl.when(sender)
+    def _():
+        cost_own.wait()
+        for copy in cost_copies:
+            copy.wait_send()
+
+    for index in range(2):
+
+        @pl.when(2 * core + index != seq)
+        def _():
+            remote(
+                cost, cost_out.at[index], cost_send.at[0], cost_recv.at[index], other_core
+            ).wait_recv()
+
+    finish_first()
+    finish_second()
+
+
+def reduce_all(grads, vector, first, second, cost):
+    anywhere = pl.BlockSpec(memory_space=pl.ANY)
+    inside = pl.BlockSpec(memory_space=pltpu.VMEM)
+    dma = pltpu.SemaphoreType.DMA
+    chunks, paired = (6, 4)
+    rows, columns = grads.shape[2:]
+    depth = rows // chunks
+    units = LINE * chunks
+    block = (depth, columns)
+    return pl.pallas_call(
+        functools.partial(reduce_kernel, chunks, paired),
+        out_shape=[
+            jax.ShapeDtypeStruct(grads.shape[1:], grads.dtype),
+            jax.ShapeDtypeStruct(vector.shape[1:], vector.dtype),
+            jax.ShapeDtypeStruct(first.shape, first.dtype),
+            jax.ShapeDtypeStruct(second.shape, second.dtype),
+            jax.ShapeDtypeStruct((2,) + cost.shape, cost.dtype),
+        ],
+        in_specs=[anywhere, inside, anywhere, anywhere, anywhere],
+        out_specs=[anywhere, inside, anywhere, anywhere, anywhere],
+        scratch_shapes=[
+            pltpu.VMEM((units, 2) + block, jnp.bfloat16),
+            pltpu.VMEM((units, 2) + block, jnp.bfloat16),
+            pltpu.VMEM((units,) + block, jnp.bfloat16),
+            pltpu.VMEM((units, 2) + block, jnp.bfloat16),
+            pltpu.VMEM((units, 2) + block, jnp.bfloat16),
+            pltpu.VMEM((chunks, 2) + block, jnp.bfloat16),
+            pltpu.VMEM(vector.shape, jnp.float32),
+            pltpu.VMEM(vector.shape, jnp.float32),
+            pltpu.VMEM(vector.shape, jnp.float32),
+            dma((units, 2)),
+            dma((units, 2)),
+            dma((units, 2)),
+            dma((units,)),
+            dma((units,)),
+            dma((units,)),
+            dma((units,)),
+            dma((units,)),
+            dma((chunks,)),
+            dma((chunks,)),
+            dma((2, chunks)),
+            dma((2, chunks)),
+            dma((2, chunks)),
+            dma((2,)),
+            dma((2,)),
+            dma((2,)),
+            dma((2,)),
+            dma((3,)),
+            dma((2 + LINE,)),
+            dma((2 + LINE,)),
+            dma((LINE - 1,)),
+            dma((2,)),
+        ],
+        compiler_params=pltpu.CompilerParams(
+            collective_id=1, has_side_effects=True, vmem_limit_bytes=60 * 2**20
+        ),
+        name="reduce_grads",
+    )(grads, vector, first, second, cost)
+
+
+def core_swap(value):
+    return lax.ppermute(value, "dp", [(0, 1), (1, 0), (2, 3), (3, 2)])
+
+
+def chip_forward(source_rows, family_residues, projection_tables, head_count, core):
+    (
+        horizontal_coefficients,
+        w_row_out,
+        vertical_coefficients,
+        w_col_out,
+        w_up,
+        w_down,
+        gain_rows,
+        bias_rows,
+    ) = projection_tables
+    row_count, columns, model_width = source_rows.shape
+    total_rows = 2 * row_count
+    start = source_rows.astype(jnp.float32)
+    layernorm_first = normed(start, gain_rows[0], bias_rows[0]).astype(jnp.bfloat16)
+    horizontal_mixer = product(layernorm_first, horizontal_coefficients).astype(jnp.bfloat16)
+    queries, key_rows, content_lines = row_split(horizontal_mixer, model_width, head_count)
+    logit_factor = 1.0 / (math.sqrt(model_width // head_count) * math.sqrt(total_rows))
+    partial_value = logit_factor * jnp.einsum(
+        "rihe,rjhe->hij", queries, key_rows, preferred_element_type=jnp.float32
+    )
+    partial_value = partial_value.astype(jnp.bfloat16)
+    logits = partial_value.astype(jnp.float32) + core_swap(partial_value).astype(jnp.float32)
+    softmax_share = jax.nn.softmax(logits, axis=-1)
+    log_probs = jax.nn.log_softmax(logits, axis=-1)
+    entropy = -jnp.sum(softmax_share * log_probs, axis=-1)
+    valid_residues = (jnp.arange(columns, dtype=jnp.int32) < family_residues).astype(jnp.float32)
+    disorder_cost = jnp.sum(entropy * valid_residues[None, :]) / float(head_count * columns)
+    blended_lines = jnp.einsum(
+        "vyp,opvl->oyvl",
+        softmax_share.astype(jnp.bfloat16),
+        content_lines,
+        preferred_element_type=jnp.float32,
+    )
+    blended_lines = blended_lines.reshape(row_count, columns, model_width).astype(jnp.bfloat16)
+    after_row = start + product(blended_lines, w_row_out)
+    layernorm_second = normed(after_row, gain_rows[1], bias_rows[1]).astype(jnp.bfloat16)
+    vertical_mixer = product(layernorm_second, vertical_coefficients).astype(jnp.bfloat16)
+    kept = vertical_mixer[..., model_width:]
+    given = core_swap(kept)
+    everyone = jnp.concatenate(
+        [jnp.where(core == 0, kept, given), jnp.where(core == 0, given, kept)], axis=0
+    )
+    mixed_values, log_total = column_forward(
+        vertical_mixer[..., :model_width],
+        everyone[..., :model_width],
+        everyone[..., model_width:],
+        head_count,
+    )
+    column_state = (everyone, log_total)
+    after_col = after_row + product(mixed_values, w_col_out)
+    normal_c = normed(after_col, gain_rows[2], bias_rows[2]).astype(jnp.bfloat16)
+    upward = product(normal_c, w_up)
+    hidden = gelu_exact(upward).astype(jnp.bfloat16)
+    result = after_col + product(hidden, w_down)
+    kept_state = (
+        source_rows,
+        layernorm_first,
+        horizontal_mixer,
+        logits,
+        blended_lines,
+        after_row,
+        layernorm_second,
+        vertical_mixer,
+        column_state,
+        mixed_values,
+        after_col,
+        normal_c,
+        upward,
+        hidden,
+    )
+    return (result.astype(jnp.bfloat16), disorder_cost, kept_state)
+
+
+def chip_backward(kept_state, family_residues, grad_result, projection_tables, head_count, core):
+    (
+        horizontal_coefficients,
+        w_row_out,
+        vertical_coefficients,
+        w_col_out,
+        w_up,
+        w_down,
+        gain_rows,
+        bias_rows,
+    ) = projection_tables
+    (
+        source_rows,
+        layernorm_first,
+        horizontal_mixer,
+        logits,
+        blended_lines,
+        after_row,
+        layernorm_second,
+        vertical_mixer,
+        column_state,
+        mixed_values,
+        after_col,
+        normal_c,
+        upward,
+        hidden,
+    ) = kept_state
+    row_count, columns, model_width = source_rows.shape
+    total_rows = 2 * row_count
+    grad_branch_ffn = grad_result.astype(jnp.bfloat16)
+    grad_hidden = product_back(grad_branch_ffn, w_down)
+    grad_upward = jax.vjp(gelu_exact, upward)[1](grad_hidden)[0].astype(jnp.bfloat16)
+    grad_normal_c = product_back(grad_upward, w_up)
+    from_norm, gain_last, bias_last = jax.vjp(normed, after_col, gain_rows[2], bias_rows[2])[1](
+        grad_normal_c
+    )
+    grad_col = grad_result + from_norm
+    grad_branch_col = grad_col.astype(jnp.bfloat16)
+    grad_attended = product_back(grad_branch_col, w_col_out).astype(jnp.bfloat16)
+    everyone, log_total = column_state
+    grad_query_col, grad_key_col, grad_value_col = column_backward(
+        vertical_mixer[..., :model_width],
+        everyone[..., :model_width],
+        everyone[..., model_width:],
+        log_total,
+        grad_attended,
+        head_count,
+    )
+    grad_kv = jnp.concatenate([grad_key_col, grad_value_col], axis=-1).astype(jnp.bfloat16)
+    kept = jnp.where(core == 0, grad_kv[:row_count], grad_kv[row_count:])
+    given = core_swap(jnp.where(core == 0, grad_kv[row_count:], grad_kv[:row_count]))
+    grad_kv_rows = kept.astype(jnp.float32) + given.astype(jnp.float32)
+    grad_col_proj = jnp.concatenate([grad_query_col, grad_kv_rows], axis=-1).astype(jnp.bfloat16)
+    grad_normal_b = product_back(grad_col_proj, vertical_coefficients)
+    from_norm, gain_middle, bias_middle = jax.vjp(normed, after_row, gain_rows[1], bias_rows[1])[1](
+        grad_normal_b
+    )
+    grad_row = grad_col + from_norm
+    grad_branch_row = grad_row.astype(jnp.bfloat16)
+    grad_mixed = split_heads(
+        product_back(grad_branch_row, w_row_out).astype(jnp.bfloat16), head_count
+    )
+    queries, key_rows, content_lines = row_split(horizontal_mixer, model_width, head_count)
+    softmax_share = jax.nn.softmax(logits, axis=-1)
+    log_probs = jax.nn.log_softmax(logits, axis=-1)
+    entropy = -jnp.sum(softmax_share * log_probs, axis=-1)
+    partial_value = jnp.einsum(
+        "rihe,rjhe->hij", grad_mixed, content_lines, preferred_element_type=jnp.float32
+    ).astype(jnp.bfloat16)
+    grad_probs = partial_value.astype(jnp.float32) + core_swap(partial_value).astype(jnp.float32)
+    grad_values = jnp.einsum(
+        "hij,rihe->rjhe",
+        softmax_share.astype(jnp.bfloat16),
+        grad_mixed,
+        preferred_element_type=jnp.float32,
+    )
+    valid_residues = (jnp.arange(columns, dtype=jnp.int32) < family_residues).astype(jnp.float32)
+    column_weight = float(total_rows * columns) * valid_residues / float(head_count * columns)
+    grad_logits = softmax_share * (
+        grad_probs - jnp.sum(softmax_share * grad_probs, axis=-1, keepdims=True)
+    )
+    grad_logits = grad_logits - column_weight[None, :, None] * softmax_share * (
+        log_probs + entropy[..., None]
+    )
+    grad_logits = grad_logits.astype(jnp.bfloat16)
+    logit_factor = 1.0 / (math.sqrt(model_width // head_count) * math.sqrt(total_rows))
+    grad_queries = logit_factor * jnp.einsum(
+        "vyp,opvl->oyvl", grad_logits, key_rows, preferred_element_type=jnp.float32
+    )
+    grad_keys = logit_factor * jnp.einsum(
+        "hij,rihe->rjhe", grad_logits, queries, preferred_element_type=jnp.float32
+    )
+    grad_row_proj = jnp.concatenate(
+        [
+            grad_queries.reshape(row_count, columns, model_width),
+            grad_keys.reshape(row_count, columns, model_width),
+            grad_values.reshape(row_count, columns, model_width),
+        ],
+        axis=-1,
+    ).astype(jnp.bfloat16)
+    grad_normal_a = product_back(grad_row_proj, horizontal_coefficients)
+    from_norm, gain_first, bias_first = jax.vjp(
+        normed, source_rows.astype(jnp.float32), gain_rows[0], bias_rows[0]
+    )[1](grad_normal_a)
+    grad_source = (grad_row + from_norm).astype(jnp.bfloat16)
+    operand_pairs = (
+        (layernorm_first, grad_row_proj),
+        (blended_lines, grad_branch_row),
+        (layernorm_second, grad_col_proj),
+        (mixed_values, grad_branch_col),
+        (normal_c, grad_upward),
+        (hidden, grad_branch_ffn),
+    )
+    norm_grads = (
+        jnp.stack([gain_first, gain_middle, gain_last]),
+        jnp.stack([bias_first, bias_middle, bias_last]),
+    )
+    return (grad_source, operand_pairs, norm_grads)
+
+
+def packed(term, lanes):
+    share = term.shape[0] // (LINE * 4)
+    parts = term.reshape(LINE, 4, share, term.shape[1] // lanes, lanes)
+    return parts.transpose(0, 1, 3, 2, 4).reshape(LINE, 4, -1, lanes)
+
+
+def unpacked(block, rows, columns, lanes):
+    parts = block.reshape(4, columns // lanes, rows // 4, lanes)
+    return parts.transpose(0, 2, 1, 3).reshape(rows, columns).astype(jnp.float32)
+
+
+def on_device_lined(
+    embedded_families,
+    order,
+    token_quarter_factor,
+    genuine_residue_tally,
+    standardizer_scales,
+    standardizer_offsets,
+    row_qkv,
+    row_out,
+    col_qkv,
+    col_out,
+    ffn_up,
+    ffn_down,
+    upstream_sensitivity,
+):
+    head_count = HEAD_TALLY
+    segment_place = lax.axis_index("pipe")
+    core = lax.rem(lax.axis_index("dp"), 2)
+    sequence = order[0]
+    columns, model_width = embedded_families.shape[2:]
+    piece = jnp.where(
+        segment_place == 0, embedded_families[sequence, 0], upstream_sensitivity[:, 0]
+    )
+    factor = token_quarter_factor[sequence, 0].astype(jnp.float32) * 0.25
+    count = genuine_residue_tally[sequence].astype(jnp.float32)
+    meta = jnp.concatenate(
+        [
+            jnp.broadcast_to(factor[:, :, None], (2, columns, 128)),
+            jnp.broadcast_to(count[:, None, None], (2, 8, 128)),
+        ],
+        axis=1,
+    )
+    share = standardizer_scales.shape[-1]
+    rows = jnp.pad(
+        jnp.concatenate([standardizer_scales[0], standardizer_offsets[0]], axis=0),
+        ((0, 2), (0, 256 - share)),
+    )
+    shards = (row_qkv[0], row_out[0], col_qkv[0], col_out[0], ffn_up[0], ffn_down[0])
+    *wholes, piece, meta, rows = gather_all(shards, piece, meta, rows)
+    rows = rows[:, :6, :share].transpose(1, 0, 2).reshape(6, model_width)
+    projection_tables = tuple(wholes) + (rows[:3], rows[3:])
+    family_residues = meta[0, columns, 0].astype(jnp.int32)
+
+    early = chip_forward(piece, family_residues, projection_tables, head_count, core)
+    received = lax.ppermute(early[0], "pipe", [(0, 1)])
+    later = chip_forward(received, family_residues, projection_tables, head_count, core)
+    activation, cost, kept_state = choose(segment_place == 0, early, later)
+
+    outgrad = piece.astype(jnp.float32) * meta[:, :columns, :1]
+    ahead = chip_backward(kept_state, family_residues, outgrad, projection_tables, head_count, core)
+    grad_received = lax.ppermute(ahead[0], "pipe", [(1, 0)]).astype(jnp.float32)
+    behind = chip_backward(
+        kept_state, family_residues, grad_received, projection_tables, head_count, core
+    )
+    grad_source, operand_pairs, norm_grads = choose(segment_place == 1, ahead, behind)
+    totals = [weight_term(left, right).astype(jnp.bfloat16) for left, right in operand_pairs]
+    grads = jnp.concatenate([packed(total, model_width) for total in totals], axis=2)
+    vector = jnp.concatenate(norm_grads, axis=0).reshape(6, LINE, share).transpose(1, 0, 2)
+    vector = jnp.pad(vector, ((0, 0), (0, 2), (0, 256 - share)))
+    out, vector, activations, derivs, costs = reduce_all(
+        grads, vector, activation, grad_source, jnp.full((8, 128), cost, jnp.float32)
+    )
+    results = []
+    base = 0
+    for shard in shards:
+        depth, wide = shard.shape
+        length = depth // 4 * (wide // model_width)
+        results.append(
+            unpacked(out[:, base : base + length], depth, wide, model_width)[None]
+        )
+        base += length
+    return (
+        activations[None, :, None],
+        derivs[None, :, None],
+        costs[:, 0, 0][None],
+        *results,
+        vector[None, :3, :share],
+        vector[None, 3:6, :share],
+    )
+
+
 def solution(mesh):
     in_specs = (
         P("dp", "seq", None, None),
@@ -517,6 +1546,7 @@
         P("pipe", None, "seq"),
         P("pipe", None, "seq"),
     )
+    lined = mesh.shape["seq"] == LINE and mesh.shape["dp"] == 4 and mesh.shape["pipe"] == 2
     return jax.shard_map(
-        on_device, mesh=mesh, in_specs=in_specs, out_specs=out_specs, check_vma=False
-    )
+        on_device_lined if lined else on_device, mesh=mesh, in_specs=in_specs, out_specs=out_specs, check_vma=False
+    )

time: 1610 us -> 903 us (0.56)
  waiting for transfers between devices: 970 us -> 14 us
  Pallas kernels: 0 us -> 360 us
  local copies, waits for them, and re-layouts: 155 us -> 256 us
  other arithmetic: 178 us -> 97 us
  matrix products: 199 us -> 154 us
  blocking collectives: 44 us -> 0 us
  between operations: 31.9 us -> 5.08 us
    all_gather x9 -> x0, waiting for transfers between devices: 380 us -> none  [the longest x1 88.2 us: on_device(): lax.all_gather(ffn_up, 'seq', axis=1, tiled=True)]
    pallas_call x0 -> x2, Pallas kernels: none -> 360 us  [the longest x1 200 us: reduce_all(): pl.pallas_call(functools.partial(reduce_kernel, chunks, paired), out_shap...]
    reduce_scatter x9 -> x0, waiting for transfers between devices: 338 us -> none  [the longest x1 88.1 us: on_device(): lax.psum_scatter(weight_totals[5].astype(jnp.bfloat16), 'seq', scatter_di...]
    psum x6 -> x0, waiting for transfers between devices: 217 us -> none  [the longest x1 88.1 us: on_device(): lax.psum(shared_row_qkv.astype(jnp.bfloat16), 'dp').astype(jnp.float32)]
    reshape x0 -> x23, local copies, waits for them, and re-layouts: none -> 81.3 us  [the longest x11 36.7 us: split_heads(): values.reshape(values.shape[:-1] + (head_count, values.shape[-1] // head_...]
    all_gather x2 -> x0, blocking collectives: 38.4 us -> none  [the longest x1 19.4 us: on_device(): lax.all_gather(standardizer_scales.astype(jnp.bfloat16), 'seq', axis=2, t...]
    unnamed x28 -> x0, waiting for transfers between devices: 26 us -> none
    select_n x19 -> x5, other arithmetic: 27.7 us -> 6.03 us  [choose(): jnp.where(flag, early, later)]
  transfers between devices with their start and end apart: 30 -> 10, of which waited for: 26 -> 3; matrix products, arithmetic and copies ran while one was open for 18% -> 15% of each run, Pallas kernels for 0% -> 0%
where the time goes in v1:
time: 903 us; the launch traced here: 892 us
  Pallas kernels  360 us (40%)
  local copies, waits for them, and re-layouts  256 us (28%)
  matrix products  154 us (17%)
  other arithmetic  97 us (11%)
  waiting for transfers between devices  14 us (2%)
    pallas_call x1, Pallas kernels, reduce_all(): pl.pallas_call(functools.partial(reduce_kernel, chunks, paired), out_shap...  200 us
    pallas_call x1, Pallas kernels, gather_all(): pl.pallas_call(gather_kernel, out_shape=shapes, in_specs=[anywhere] * 9,...  160 us
    reshape x11, local copies, waits for them, and re-layouts, split_heads(): values.reshape(values.shape[:-1] + (head_count, values.shape[-1] // head_...  36.7 us
    reshape x4, local copies, waits for them, and re-layouts, packed(): parts = term.reshape(LINE, 4, share, term.shape[1] // lanes, lanes)  33 us
    dot_general x12, matrix products, product_back(): lax.dot_general(left, weight, (((left.ndim - 1,), (1,)), ((), ())), prefe...  32.5 us
    unnamed x363, local copies, waits for them, and re-layouts  30.5 us
    dot_general x12, matrix products, product(): lax.dot_general(left, weight, (((left.ndim - 1,), (0,)), ((), ())), prefe...  25.8 us
    dot_general x6, matrix products, weight_term(): lax.dot_general(left, right, (((0, 1), (0, 1)), ((), ())), preferred_elem...  20.6 us
  transfers between devices with their start and end apart: 10, of which 3 were waited for; matrix products, arithmetic and copies ran while one was open for 15% of the time, Pallas kernels for 0%

profile of v1, /device:TPU:0, one launch (start us, length us, event | category | flops | bytes accessed | tf_op | source)
XLA Modules:
  0.0 892.5 jit_solution(2146163776129379790)
XLA Ops:
  9.1 159.6 %gather_weights.1 = (bf16[768,2304]{1,0:T(8,128)(2,1)}, bf16[768,768]{1,0:T(8,128)(2,1)}, bf16[768,2304]{1,0:T(8,128)(2,1)}, bf16[768,768]{1,0:T(8,128)(2,1)}, b...) custom-call(bf16[192,2304]{1,0:T(8,128)(2,1)} %bitcast.412, ...), custom_call_target="tpu_custom_call" | custom-call | tf_op jit(solution)/shard_map/gather_weights/pallas_call | solution.py:777
  207.3 3.9 fusion.297
  224.6 4.9 fusion.170
  229.5 7.7 fusion.35
  242.2 8.9 collective-permute-done.2
  339.5 3.9 fusion.300
  357.9 4.9 fusion.171
  362.9 14.8 %fusion.36 = (f32[2,128,3072]{2,1,0:T(8,128)S(1)}, f32[2,128,3072]{2,1,0:T(8,128)S(1)}, bf16[2,128,3072]{2,1,0:T(8,128)(2,1)}) fusion(f32[2,128,3072]{2,1,0:T(8,128)S(1)} %copy-done.11, f32[2,128,3072]{2,1,0:T(8,128)S(1)} %get-tuple-element.181, pred[]{:T(512)S(6)} %eq.6, u8[128,3072]{1,0:T(8,128)(4,1)S(1)} %get-tuple-element.74, ...), kind=kLoop, calls=%fused_computation.50 | loop fusion | flops 104595456 | bytes 14942209 | tf_op jit(solution)/shard_map/jvp()/erfc | solution.py:33
  395.0 4.3 multiply_reduce_fusion.1
  436.6 4.1 multiply_reduce_fusion.10
  498.1 4.4 collective-permute-done.7
  502.5 6.3 add_convert_fusion
  508.8 5.1 multiply_reduce_fusion.2
  521.8 5.7 multiply_reduce_fusion
  555.9 4.3 fusion.83
  560.1 9.9 %reshape.660 = bf16[4,4,48,4,768]{4,3,2,1,0:T(4,128)(2,1)} reshape(bf16[768,3072]{1,0:T(8,128)(2,1)} %bitcast_convert_fusion.1) | data formatting | bytes 9437184 | tf_op jit(solution)/shard_map/reshape | solution.py:1430
  570.1 5.4 copy.313
  585.2 5.4 bitcast_convert_fusion
  605.4 9.0 %reshape.658 = bf16[4,4,48,3,768]{4,3,2,1,0:T(4,128)(2,1)} reshape(bf16[768,2304]{1,0:T(8,128)(2,1)} %bitcast_convert_fusion.2) | data formatting | bytes 7077888 | tf_op jit(solution)/shard_map/reshape | solution.py:1430
  614.4 4.8 copy.308
  636.4 4.7 bitcast_convert_fusion.3
  641.1 8.8 reshape.656
  659.3 6.5 copy-done.2
  666.4 200.3 %reduce_grads.1 = (bf16[4,768,768]{2,1,0:T(8,128)(2,1)}, f32[8,256]{1,0:T(8,128)}, bf16[2,128,768]{2,1,0:T(8,128)(2,1)}, bf16[2,128,768]{2,1,0:T(8,128)(2,1)}, f32[2,8,128]{2,1,0:T(8,128)}) custom-call(bf16[4,4,768,768]{3,2,1,0:T(8,128)(2,1)} %copy-done.2, f32[4,8,256]{2,1,0:T(8,128)} %pad.10.refs_1_, bf16[2,128,768]{2,1,0:T(8,128)(2,1)} %fusion.130.refs_2_, ...), custom_call_target="tpu_custom_call" | custom-call | tf_op jit(solution)/shard_map/reduce_grads/pallas_call | solution.py:1179
  (635 shorter events, 390.0 us)
Async XLA Ops:
  178.4 1.8 collective-permute-start
  182.4 40.3 %copy-start.12 = (f32[2,128,768]{2,1,0:T(8,128)}, f32[2,128,768]{2,1,0:T(8,128)S(1)}, u32[]{:S(2)}) copy-start(f32[2,128,768]{2,1,0:T(8,128)S(1)} %get-tuple-element.167) | copy-start | bytes 2359300
  186.3 6.9 collective-permute-start.1
  237.2 16.2 %copy-start.72 = (bf16[2,128,2304]{2,1,0:T(8,128)(2,1)S(1)}, bf16[2,128,2304]{2,1,0:T(8,128)(2,1)}, u32[]{:S(2)}) copy-start(bf16[2,128,2304]{2,1,0:T(8,128)(2,1)} %copy-done.71) | copy-start | bytes 3538948
  237.2 16.2 %copy-start.145 = (f32[768]{0:T(1024)S(1)}, f32[768]{0:T(1024)}, u32[]{:S(2)}) copy-start(f32[768]{0:T(1024)} %copy-done.144) | copy-start | bytes 9220
  237.2 16.2 %copy-start.157 = (bf16[768,2304]{1,0:T(8,128)(2,1)S(1)}, bf16[768,2304]{1,0:T(8,128)(2,1)}, u32[]{:S(2)}) copy-start(bf16[768,2304]{1,0:T(8,128)(2,1)} %get-tuple-element.28) | copy-start | bytes 10616836
  238.7 16.9 %copy-start.161 = (bf16[2,128,768]{2,1,0:T(8,128)(2,1)}, bf16[2,128,768]{2,1,0:T(8,128)(2,1)S(1)}, u32[]{:S(2)}) copy-start(bf16[2,128,768]{2,1,0:T(8,128)(2,1)S(1)} %fusion.95) | copy-start | bytes 1179652
  238.7 12.4 %collective-permute-start.2 = (bf16[2,128,768]{2,1,0:T(8,128)(2,1)S(1)}, bf16[2,128,768]{2,1,0:T(8,128)(2,1)S(1)}, u32[]{:S(2)}, u32[]{:S(2)}) collective-permute-start(bf16[2,128,768]{2,1,0:T(8,128)(2,1)S(1)} %fusion.95), channel_id=1, source_target_pairs={{0,16},{1,17},{2,18},{3,19},{4,20},{5,21},{6,22},{7,23},{8,24},{9,... | collective-permute-start | bytes 1179656 | tf_op jit(solution)/shard_map/ppermute | solution.py:1483
  251.1 27.7 %copy-start.47 = (bf16[2,128,768]{2,1,0:T(8,128)(2,1)}, bf16[2,128,768]{2,1,0:T(8,128)(2,1)S(1)}, u32[]{:S(2)}) copy-start(bf16[2,128,768]{2,1,0:T(8,128)(2,1)S(1)} %collective-permute-done.2) | copy-start | bytes 1179652
  262.6 9.9 %collective-permute-start.3 = (bf16[12,128,128]{1,2,0:T(8,128)(2,1)}, bf16[12,128,128]{1,2,0:T(8,128)(2,1)}, u32[]{:S(2)}, u32[]{:S(2)}) collective-permute-start(bf16[12,128,128]{1,2,0:T(8,128)(2,1)} %fusion.98), channel_id=1, source_target_pairs={{0,1},{1,0},{2,3},{3,2},{4,5},{5,4},{6,7},{7,6},{8,9},{9,8},{10,11... | collective-permute-start | bytes 1179656 | tf_op jit(solution)/shard_map/ppermute | solution.py:1231
  282.9 25.6 %collective-permute-start.4 = (bf16[2,128,1536]{2,1,0:T(8,128)(2,1)}, bf16[2,128,1536]{2,1,0:T(8,128)(2,1)}, u32[]{:S(2)}, u32[]{:S(2)}) collective-permute-start(bf16[2,128,1536]{2,1,0:T(8,128)(2,1)} %slice.231), channel_id=1, source_target_pairs={{0,1},{1,0},{2,3},{3,2},{4,5},{5,4},{6,7},{7,6},{8,9},{9,8},{10,11... | collective-permute-start | bytes 2359304 | tf_op jit(solution)/shard_map/ppermute | solution.py:1231
  357.6 25.5 %copy-start.15 = (f32[2,128,768]{2,1,0:T(8,128)}, f32[2,128,768]{2,1,0:T(8,128)S(1)}, u32[]{:S(2)}) copy-start(f32[2,128,768]{2,1,0:T(8,128)S(1)} %get-tuple-element.124) | copy-start | bytes 2359300
  357.6 25.4 %copy-start.107 = (f32[2,128]{1,0:T(2,128)}, f32[2,128]{1,0:T(2,128)S(1)}, u32[]{:S(2)}) copy-start(f32[2,128]{1,0:T(2,128)S(1)} %broadcast_multiply_fusion.2) | copy-start | bytes 3076
  357.9 25.2 %copy-start.125 = (f32[2,128]{1,0:T(2,128)}, f32[2,128]{1,0:T(2,128)S(1)}, u32[]{:S(2)}) copy-start(f32[2,128]{1,0:T(2,128)S(1)} %fusion.262) | copy-start | bytes 3076
  357.9 19.8 %slice-start.8 = ((s8[4718592]{0:T(1024)(128)(4,1)}), s8[4194304]{0:T(1024)(128)(4,1)S(1)}, s32[]{:S(2)}) async-start(s8[4718592]{0:T(1024)(128)(4,1)} %bitcast.430), calls=%async_computation.8 | async-start | bytes 8388608
  362.8 14.8 %copy-start.104 = (f32[2,128]{1,0:T(2,128)S(1)}, f32[2,128]{1,0:T(2,128)}, u32[]{:S(2)}) copy-start(f32[2,128]{1,0:T(2,128)} %slice_reduce_fusion) | copy-start | bytes 3076
  362.9 14.8 %slice-start.9 = ((s8[4718592]{0:T(1024)(128)(4,1)}), s8[524288]{0:T(1024)(128)(4,1)S(1)}, s32[]{:S(2)}) async-start(s8[4718592]{0:T(1024)(128)(4,1)} %bitcast.430), calls=%async_computation.9 | async-start | bytes 1048576
  362.9 17.4 %slice-start.4 = ((s8[4718592]{0:T(1024)(128)(4,1)}), s8[4194304]{0:T(1024)(128)(4,1)S(1)}, s32[]{:S(2)}) async-start(s8[4718592]{0:T(1024)(128)(4,1)} %bitcast.426), calls=%async_computation.4 | async-start | bytes 8388608
  423.5 11.2 %collective-permute-start.5 = (bf16[2,128,1536]{2,1,0:T(8,128)(2,1)}, bf16[2,128,1536]{2,1,0:T(8,128)(2,1)}, u32[]{:S(2)}, u32[]{:S(2)}) collective-permute-start(bf16[2,128,1536]{2,1,0:T(8,128)(2,1)} %broadcast_select_fusion.3), channel_id=1, source_target_pairs={{0,1},{1,0},{2,3},{3,2},{4,5},{5,4},{6,7},{7,6},{8,9},{9,8},{10,11... | collective-permute-start | bytes 2359304 | tf_op jit(solution)/shard_map/ppermute | solution.py:1231
  449.0 19.2 %collective-permute-start.6 = (bf16[12,128,128]{1,2,0:T(8,128)(2,1)}, bf16[12,128,128]{1,2,0:T(8,128)(2,1)}, u32[]{:S(2)}, u32[]{:S(2)}) collective-permute-start(bf16[12,128,128]{1,2,0:T(8,128)(2,1)} %fusion.102), channel_id=1, source_target_pairs={{0,1},{1,0},{2,3},{3,2},{4,5},{5,4},{6,7},{7,6},{8,9},{9,8},{10,11... | collective-permute-start | bytes 1179656 | tf_op jit(solution)/shard_map/ppermute | solution.py:1231
  489.1 13.3 %collective-permute-start.7 = (bf16[2,128,768]{2,1,0:T(8,128)(2,1)}, bf16[2,128,768]{2,1,0:T(8,128)(2,1)}, u32[]{:S(2)}, u32[]{:S(2)}) collective-permute-start(bf16[2,128,768]{2,1,0:T(8,128)(2,1)} %add_convert_fusion.5), channel_id=1, source_target_pairs={{16,0},{17,1},{18,2},{19,3},{20,4},{21,5},{22,6},{23,7},{24,8},{25... | collective-permute-start | bytes 1179656 | tf_op jit(solution)/shard_map/ppermute | solution.py:1489
  555.9 34.7 %collective-permute-start.8 = (bf16[2,128,1536]{2,1,0:T(8,128)(2,1)}, bf16[2,128,1536]{2,1,0:T(8,128)(2,1)}, u32[]{:S(2)}, u32[]{:S(2)}) collective-permute-start(bf16[2,128,1536]{2,1,0:T(8,128)(2,1)} %broadcast_select_fusion.2), channel_id=1, source_target_pairs={{0,1},{1,0},{2,3},{3,2},{4,5},{5,4},{6,7},{7,6},{8,9},{9,8},{10,11... | collective-permute-start | bytes 2359304 | tf_op jit(solution)/shard_map/ppermute | solution.py:1231
  601.4 18.4 %collective-permute-start.9 = (bf16[12,128,128]{1,2,0:T(8,128)(2,1)}, bf16[12,128,128]{1,2,0:T(8,128)(2,1)}, u32[]{:S(2)}, u32[]{:S(2)}) collective-permute-start(bf16[12,128,128]{1,2,0:T(8,128)(2,1)} %fusion.103), channel_id=1, source_target_pairs={{0,1},{1,0},{2,3},{3,2},{4,5},{5,4},{6,7},{7,6},{8,9},{9,8},{10,11... | collective-permute-start | bytes 1179656 | tf_op jit(solution)/shard_map/ppermute | solution.py:1231
  604.7 26.2 %copy-start.89 = (bf16[2,128,768]{2,1,0:T(8,128)(2,1)}, bf16[2,128,768]{2,1,0:T(8,128)(2,1)S(1)}, u32[]{:S(2)}) copy-start(bf16[2,128,768]{2,1,0:T(8,128)(2,1)S(1)} %copy.301) | copy-start | bytes 1179652
  (162 other events, 567.3 us)

commit v2 on v1

--- a/solution.py
+++ b/solution.py
@@ -1227,208 +1227,570 @@
     )(grads, vector, first, second, cost)
 
 
-def core_swap(value):
-    return lax.ppermute(value, "dp", [(0, 1), (1, 0), (2, 3), (3, 2)])
-
-
-def chip_forward(source_rows, family_residues, projection_tables, head_count, core):
-    (
-        horizontal_coefficients,
-        w_row_out,
-        vertical_coefficients,
-        w_col_out,
-        w_up,
-        w_down,
-        gain_rows,
-        bias_rows,
-    ) = projection_tables
-    row_count, columns, model_width = source_rows.shape
-    total_rows = 2 * row_count
-    start = source_rows.astype(jnp.float32)
-    layernorm_first = normed(start, gain_rows[0], bias_rows[0]).astype(jnp.bfloat16)
-    horizontal_mixer = product(layernorm_first, horizontal_coefficients).astype(jnp.bfloat16)
-    queries, key_rows, content_lines = row_split(horizontal_mixer, model_width, head_count)
-    logit_factor = 1.0 / (math.sqrt(model_width // head_count) * math.sqrt(total_rows))
-    partial_value = logit_factor * jnp.einsum(
-        "rihe,rjhe->hij", queries, key_rows, preferred_element_type=jnp.float32
-    )
-    partial_value = partial_value.astype(jnp.bfloat16)
-    logits = partial_value.astype(jnp.float32) + core_swap(partial_value).astype(jnp.float32)
-    softmax_share = jax.nn.softmax(logits, axis=-1)
-    log_probs = jax.nn.log_softmax(logits, axis=-1)
-    entropy = -jnp.sum(softmax_share * log_probs, axis=-1)
-    valid_residues = (jnp.arange(columns, dtype=jnp.int32) < family_residues).astype(jnp.float32)
-    disorder_cost = jnp.sum(entropy * valid_residues[None, :]) / float(head_count * columns)
-    blended_lines = jnp.einsum(
-        "vyp,opvl->oyvl",
-        softmax_share.astype(jnp.bfloat16),
-        content_lines,
+def dot(left, right, left_axis, right_axis):
+    return lax.dot_general(
+        left,
+        right,
+        (((left_axis,), (right_axis,)), ((), ())),
         preferred_element_type=jnp.float32,
     )
-    blended_lines = blended_lines.reshape(row_count, columns, model_width).astype(jnp.bfloat16)
-    after_row = start + product(blended_lines, w_row_out)
-    layernorm_second = normed(after_row, gain_rows[1], bias_rows[1]).astype(jnp.bfloat16)
-    vertical_mixer = product(layernorm_second, vertical_coefficients).astype(jnp.bfloat16)
-    kept = vertical_mixer[..., model_width:]
-    given = core_swap(kept)
-    everyone = jnp.concatenate(
-        [jnp.where(core == 0, kept, given), jnp.where(core == 0, given, kept)], axis=0
-    )
-    mixed_values, log_total = column_forward(
-        vertical_mixer[..., :model_width],
-        everyone[..., :model_width],
-        everyone[..., model_width:],
-        head_count,
-    )
-    column_state = (everyone, log_total)
-    after_col = after_row + product(mixed_values, w_col_out)
-    normal_c = normed(after_col, gain_rows[2], bias_rows[2]).astype(jnp.bfloat16)
-    upward = product(normal_c, w_up)
-    hidden = gelu_exact(upward).astype(jnp.bfloat16)
-    result = after_col + product(hidden, w_down)
-    kept_state = (
-        source_rows,
-        layernorm_first,
-        horizontal_mixer,
-        logits,
-        blended_lines,
-        after_row,
-        layernorm_second,
-        vertical_mixer,
-        column_state,
-        mixed_values,
-        after_col,
-        normal_c,
-        upward,
-        hidden,
-    )
-    return (result.astype(jnp.bfloat16), disorder_cost, kept_state)
-
-
-def chip_backward(kept_state, family_residues, grad_result, projection_tables, head_count, core):
-    (
-        horizontal_coefficients,
-        w_row_out,
-        vertical_coefficients,
-        w_col_out,
-        w_up,
-        w_down,
-        gain_rows,
-        bias_rows,
-    ) = projection_tables
-    (
-        source_rows,
-        layernorm_first,
-        horizontal_mixer,
-        logits,
-        blended_lines,
-        after_row,
-        layernorm_second,
-        vertical_mixer,
-        column_state,
-        mixed_values,
-        after_col,
-        normal_c,
-        upward,
-        hidden,
-    ) = kept_state
-    row_count, columns, model_width = source_rows.shape
-    total_rows = 2 * row_count
-    grad_branch_ffn = grad_result.astype(jnp.bfloat16)
-    grad_hidden = product_back(grad_branch_ffn, w_down)
-    grad_upward = jax.vjp(gelu_exact, upward)[1](grad_hidden)[0].astype(jnp.bfloat16)
-    grad_normal_c = product_back(grad_upward, w_up)
-    from_norm, gain_last, bias_last = jax.vjp(normed, after_col, gain_rows[2], bias_rows[2])[1](
-        grad_normal_c
-    )
-    grad_col = grad_result + from_norm
-    grad_branch_col = grad_col.astype(jnp.bfloat16)
-    grad_attended = product_back(grad_branch_col, w_col_out).astype(jnp.bfloat16)
-    everyone, log_total = column_state
-    grad_query_col, grad_key_col, grad_value_col = column_backward(
-        vertical_mixer[..., :model_width],
-        everyone[..., :model_width],
-        everyone[..., model_width:],
-        log_total,
-        grad_attended,
-        head_count,
-    )
-    grad_kv = jnp.concatenate([grad_key_col, grad_value_col], axis=-1).astype(jnp.bfloat16)
-    kept = jnp.where(core == 0, grad_kv[:row_count], grad_kv[row_count:])
-    given = core_swap(jnp.where(core == 0, grad_kv[row_count:], grad_kv[:row_count]))
-    grad_kv_rows = kept.astype(jnp.float32) + given.astype(jnp.float32)
-    grad_col_proj = jnp.concatenate([grad_query_col, grad_kv_rows], axis=-1).astype(jnp.bfloat16)
-    grad_normal_b = product_back(grad_col_proj, vertical_coefficients)
-    from_norm, gain_middle, bias_middle = jax.vjp(normed, after_row, gain_rows[1], bias_rows[1])[1](
-        grad_normal_b
-    )
-    grad_row = grad_col + from_norm
-    grad_branch_row = grad_row.astype(jnp.bfloat16)
-    grad_mixed = split_heads(
-        product_back(grad_branch_row, w_row_out).astype(jnp.bfloat16), head_count
-    )
-    queries, key_rows, content_lines = row_split(horizontal_mixer, model_width, head_count)
-    softmax_share = jax.nn.softmax(logits, axis=-1)
-    log_probs = jax.nn.log_softmax(logits, axis=-1)
-    entropy = -jnp.sum(softmax_share * log_probs, axis=-1)
-    partial_value = jnp.einsum(
-        "rihe,rjhe->hij", grad_mixed, content_lines, preferred_element_type=jnp.float32
-    ).astype(jnp.bfloat16)
-    grad_probs = partial_value.astype(jnp.float32) + core_swap(partial_value).astype(jnp.float32)
-    grad_values = jnp.einsum(
-        "hij,rihe->rjhe",
-        softmax_share.astype(jnp.bfloat16),
-        grad_mixed,
-        preferred_element_type=jnp.float32,
-    )
-    valid_residues = (jnp.arange(columns, dtype=jnp.int32) < family_residues).astype(jnp.float32)
-    column_weight = float(total_rows * columns) * valid_residues / float(head_count * columns)
-    grad_logits = softmax_share * (
-        grad_probs - jnp.sum(softmax_share * grad_probs, axis=-1, keepdims=True)
-    )
-    grad_logits = grad_logits - column_weight[None, :, None] * softmax_share * (
-        log_probs + entropy[..., None]
-    )
-    grad_logits = grad_logits.astype(jnp.bfloat16)
-    logit_factor = 1.0 / (math.sqrt(model_width // head_count) * math.sqrt(total_rows))
-    grad_queries = logit_factor * jnp.einsum(
-        "vyp,opvl->oyvl", grad_logits, key_rows, preferred_element_type=jnp.float32
-    )
-    grad_keys = logit_factor * jnp.einsum(
-        "hij,rihe->rjhe", grad_logits, queries, preferred_element_type=jnp.float32
-    )
-    grad_row_proj = jnp.concatenate(
-        [
-            grad_queries.reshape(row_count, columns, model_width),
-            grad_keys.reshape(row_count, columns, model_width),
-            grad_values.reshape(row_count, columns, model_width),
+
+
+def unit_rows(values):
+    average = jnp.mean(values, axis=-1, keepdims=True)
+    centered = values - average
+    variance = jnp.mean(centered * centered, axis=-1, keepdims=True)
+    root = lax.rsqrt(variance + norm_epsilon)
+    return (centered * root, root)
+
+
+def unit_rows_back(grad, values, gain_row):
+    unit, root = unit_rows(values)
+    scaled = grad * gain_row
+    inner = jnp.mean(scaled * unit, axis=-1, keepdims=True)
+    term = root * (scaled - jnp.mean(scaled, axis=-1, keepdims=True) - unit * inner)
+    gain = jnp.sum(grad * unit, axis=0, keepdims=True)
+    bias = jnp.sum(grad, axis=0, keepdims=True)
+    return (term, gain, bias)
+
+
+def layers_kernel(
+    entry,
+    factor,
+    count,
+    rows,
+    w_row_any,
+    w_row_out_any,
+    w_col_any,
+    w_col_out_any,
+    w_up_any,
+    w_down_any,
+    act,
+    der,
+    cost,
+    vector,
+    grads,
+    w_row,
+    w_row_out,
+    w_col,
+    w_col_out,
+    w_up,
+    w_down,
+    source,
+    normal_a,
+    normal_b,
+    normal_c,
+    mixer,
+    mixer_col,
+    blended,
+    mixed,
+    after_row,
+    after_col,
+    log_share,
+    col_share,
+    hidden,
+    slope,
+    total_grad,
+    grad_in,
+    branch_ffn,
+    branch_col,
+    branch_row,
+    grad_up,
+    grad_mixer_col,
+    grad_mixer,
+    logit_send,
+    logit_recv,
+    keys_recv,
+    keys_send,
+    keys_back,
+    probs_send,
+    probs_recv,
+    halves,
+    segment,
+    spread,
+    stage,
+    stage_down,
+    weight_sem,
+    logit_sems,
+    keys_sems,
+    back_sems,
+    probs_sems,
+    pipe_sems,
+    stage_sems,
+):
+    pipe, seq, dp, core, pair = place()
+    other_core = (pipe, seq, dp + 1 - 2 * core)
+    other_pipe = (1 - pipe, seq, dp)
+    tokens, width = entry.shape
+    columns = tokens // 2
+    heads = HEAD_TALLY
+    size = width // heads
+    twin = 2 * size
+    couples = heads // 2
+    total_rows = LINE
+    bf16, f32 = (jnp.bfloat16, jnp.float32)
+
+    weights = [
+        pltpu.make_async_copy(far, near, weight_sem.at[index])
+        for index, (far, near) in enumerate(
+            (
+                (w_row_any, w_row),
+                (w_row_out_any, w_row_out),
+                (w_col_any, w_col),
+                (w_col_out_any, w_col_out),
+                (w_up_any, w_up),
+                (w_down_any, w_down),
+            )
+        )
+    ]
+    for copy in weights:
+        copy.start()
+
+    barrier = pltpu.get_barrier_semaphore()
+    for device in (other_core, other_pipe):
+        pl.semaphore_signal(barrier, inc=1, device_id=device, device_id_type=MESH)
+
+    lane = lax.broadcasted_iota(jnp.int32, (columns, 2 * twin), 1)
+    early = (lax.rem(lane, twin) < size).astype(f32)
+    halves[0] = early.astype(bf16)
+    halves[1] = (1.0 - early).astype(bf16)
+    feature = lax.broadcasted_iota(jnp.int32, (width, 128), 0)
+    head = lax.broadcasted_iota(jnp.int32, (width, 128), 1)
+    belongs = jnp.logical_and(feature >= head * size, feature < head * size + size)
+    segment[...] = belongs.astype(f32).astype(bf16)
+    head = lax.broadcasted_iota(jnp.int32, (128, width), 0)
+    feature = lax.broadcasted_iota(jnp.int32, (128, width), 1)
+    belongs = jnp.logical_and(feature >= head * size, feature < head * size + size)
+    spread[...] = belongs.astype(f32).astype(bf16)
+    pl.semaphore_wait(barrier, 2)
+
+    def gain_of(index):
+        return rows[index : index + 1, :]
+
+    def bias_of(index):
+        return rows[3 + index : 4 + index, :]
+
+    def both(ref, start):
+        return jnp.concatenate(
+            [ref[0:columns, start : start + twin], ref[columns:tokens, start : start + twin]],
+            axis=1,
+        )
+
+    def stacked(ref, start):
+        wide = both(ref, start)
+        return jnp.concatenate([wide * halves[0], wide * halves[1]], axis=0)
+
+    def unstack(wide):
+        early_lane = lax.rem(lax.broadcasted_iota(jnp.int32, (columns, 2 * twin), 1), twin) < size
+        return jnp.where(early_lane, wide[0:columns], wide[columns:])
+
+    def put(ref, start, wide):
+        ref[0:columns, start : start + twin] = wide[:, 0:twin].astype(bf16)
+        ref[columns:tokens, start : start + twin] = wide[:, twin:].astype(bf16)
+
+    def to_core(source_ref, target_ref, sems, index):
+        return remote(
+            source_ref, target_ref, sems.at[0, index], sems.at[1, index], other_core
+        )
+
+    send_on = remote(act, source, pipe_sems.at[0], pipe_sems.at[1], other_pipe)
+    send_back = remote(der, grad_in, pipe_sems.at[2], pipe_sems.at[3], other_pipe)
+
+    @pl.when(pipe == 0)
+    def _():
+        source[...] = entry[...]
+
+    @pl.when(pipe == 1)
+    def _():
+        send_on.wait_recv()
+
+    unit, _ = unit_rows(source[...].astype(f32))
+    normal_a[...] = (unit * gain_of(0) + bias_of(0)).astype(bf16)
+    weights[0].wait()
+    for part in range(3):
+        window = slice(part * width, (part + 1) * width)
+        mixer[:, window] = dot(normal_a[...], w_row[:, window], 1, 0).astype(bf16)
+    logit_factor = 1.0 / (math.sqrt(size) * math.sqrt(total_rows))
+    logit_copies = []
+    for couple in range(couples):
+        partial_value = logit_factor * dot(
+            both(mixer, couple * twin), stacked(mixer, width + couple * twin), 1, 1
+        )
+        logit_send[couple] = partial_value.astype(bf16)
+        copy = to_core(logit_send.at[couple], logit_recv.at[couple], logit_sems, couple)
+        copy.start()
+        logit_copies.append(copy)
+    valid = (
+        lax.broadcasted_iota(jnp.int32, (columns, 1), 0).astype(f32) < count[0:1, 0:1]
+    ).astype(f32)
+    disorder = jnp.zeros((columns, 1), f32)
+    for couple in range(couples):
+        logit_copies[couple].wait_recv()
+        wide = logit_send[couple].astype(f32) + logit_recv[couple].astype(f32)
+        shares = []
+        for half in range(2):
+            logits = wide[:, half * columns : (half + 1) * columns]
+            shifted_logits = logits - jnp.max(logits, axis=-1, keepdims=True)
+            powers = jnp.exp(shifted_logits)
+            total = jnp.sum(powers, axis=-1, keepdims=True)
+            logs = shifted_logits - jnp.log(total)
+            share = powers / total
+            log_share[couple, :, half * columns : (half + 1) * columns] = logs
+            disorder = disorder - jnp.sum(share * logs, axis=-1, keepdims=True) * valid
+            shares.append(share.astype(bf16))
+        put(
+            blended,
+            couple * twin,
+            dot(
+                jnp.concatenate(shares, axis=1), stacked(mixer, 2 * width + couple * twin), 1, 0
+            ),
+        )
+    cost[...] = jnp.broadcast_to(
+        jnp.sum(disorder, axis=0, keepdims=True) / float(heads * columns), cost.shape
+    )
+    weights[1].wait()
+    after_row[...] = source[...].astype(f32) + dot(blended[...], w_row_out[...], 1, 0)
+    unit, _ = unit_rows(after_row[...])
+    normal_b[...] = (unit * gain_of(1) + bias_of(1)).astype(bf16)
+    weights[2].wait()
+    keys_copies = []
+    for part in (1, 2, 0):
+        window = slice(part * width, (part + 1) * width)
+        mixer_col[:, window] = dot(normal_b[...], w_col[:, window], 1, 0).astype(bf16)
+        if part > 0:
+            copy = to_core(
+                mixer_col.at[:, window], keys_recv.at[part - 1], keys_sems, part - 1
+            )
+            copy.start()
+            keys_copies.append(copy)
+
+    def line_of(part, place_of):
+        if place_of < 2:
+            rows_of = slice(place_of * columns, (place_of + 1) * columns)
+            return mixer_col[rows_of, (1 + part) * width : (2 + part) * width]
+        rows_of = slice((place_of - 2) * columns, (place_of - 1) * columns)
+        return keys_recv[part, rows_of, :]
+
+    def sums_by_head(wide_ref, start, line):
+        products = [
+            wide_ref[index * columns : (index + 1) * columns, start : start + width] * line
+            for index in range(2)
+        ]
+        return dot(jnp.concatenate(products, axis=0), segment[...], 1, 0)
+
+    def spread_heads(narrow):
+        return dot(narrow, spread[...], 1, 0)
+
+    scores = []
+    for place_of in range(4):
+        if place_of == 2:
+            keys_copies[0].wait_recv()
+        scores.append(sums_by_head(mixer_col, 0, line_of(0, place_of)) / math.sqrt(size))
+    highest = functools.reduce(jnp.maximum, scores)
+    powers = [jnp.exp(score - highest) for score in scores]
+    total = functools.reduce(jnp.add, powers)
+    keys_copies[1].wait_recv()
+    gathered_mix = None
+    for place_of in range(4):
+        share = powers[place_of] / total
+        col_share[place_of] = share
+        wide = spread_heads(share.astype(bf16))
+        line = line_of(1, place_of).astype(f32)
+        term = jnp.concatenate([wide[0:columns] * line, wide[columns:] * line], axis=0)
+        gathered_mix = term if gathered_mix is None else gathered_mix + term
+    mixed[...] = gathered_mix.astype(bf16)
+    weights[3].wait()
+    after_col[...] = after_row[...] + dot(mixed[...], w_col_out[...], 1, 0)
+    unit, _ = unit_rows(after_col[...])
+    normal_c[...] = (unit * gain_of(2) + bias_of(2)).astype(bf16)
+    weights[4].wait()
+    weights[5].wait()
+    parts = hidden.shape[1] // width
+    result = after_col[...]
+    for part in range(parts):
+        window = slice(part * width, (part + 1) * width)
+        upward = dot(normal_c[...], w_up[:, window], 1, 0)
+        inner = 0.5 + 0.5 * lax.erf(upward * math.sqrt(0.5))
+        density = jnp.exp(-0.5 * upward * upward) * (1.0 / math.sqrt(2.0 * math.pi))
+        hidden[:, window] = (upward * inner).astype(bf16)
+        slope[:, window] = (inner + upward * density).astype(bf16)
+        result = result + dot(hidden[:, window], w_down[window, :], 1, 0)
+    act[...] = result.astype(bf16)
+
+    @pl.when(pipe == 0)
+    def _():
+        send_on.start()
+
+    @pl.when(pipe == 1)
+    def _():
+        total_grad[...] = entry[...].astype(f32) * factor[:, 0:1]
+
+    @pl.when(pipe == 0)
+    def _():
+        send_back.wait_recv()
+        total_grad[...] = grad_in[...].astype(f32)
+
+    branch_ffn[...] = total_grad[...].astype(bf16)
+    grad_normal = None
+    for part in range(parts):
+        window = slice(part * width, (part + 1) * width)
+        grad_hidden = dot(branch_ffn[...], w_down[window, :], 1, 1)
+        grad_up[:, window] = (grad_hidden * slope[:, window].astype(f32)).astype(bf16)
+        term = dot(grad_up[:, window], w_up[:, window], 1, 1)
+        grad_normal = term if grad_normal is None else grad_normal + term
+    term, gain, bias = unit_rows_back(grad_normal, after_col[...], gain_of(2))
+    vector[2:3, :] = gain
+    vector[5:6, :] = bias
+    total_grad[...] = total_grad[...] + term
+    branch_col[...] = total_grad[...].astype(bf16)
+    grad_mixed = dot(branch_col[...], w_col_out[...], 1, 1).astype(bf16)
+    grad_probs = []
+    for place_of in range(4):
+        line = line_of(1, place_of)
+        products = [grad_mixed[0:columns] * line, grad_mixed[columns:] * line]
+        grad_probs.append(dot(jnp.concatenate(products, axis=0), segment[...], 1, 0))
+    inner = functools.reduce(
+        jnp.add, [col_share[place_of] * grad_probs[place_of] for place_of in range(4)]
+    )
+    root_size = math.sqrt(size)
+    grad_query = None
+    local_terms = []
+    back_copies = []
+    grad_lines = grad_mixed.astype(f32)
+    query_lines = mixer_col[:, 0:width].astype(f32)
+    for place_of in (2, 3, 0, 1):
+        share = col_share[place_of]
+        narrow = (share * (grad_probs[place_of] - inner)).astype(bf16)
+        wide = spread_heads(narrow)
+        line = line_of(0, place_of).astype(f32)
+        term = jnp.concatenate([wide[0:columns] * line, wide[columns:] * line], axis=0)
+        grad_query = term if grad_query is None else grad_query + term
+        key_term = wide[0:columns] * query_lines[0:columns] + wide[columns:] * query_lines[columns:]
+        key_term = key_term / root_size
+        wide = spread_heads(share.astype(bf16))
+        value_term = wide[0:columns] * grad_lines[0:columns] + wide[columns:] * grad_lines[columns:]
+        if place_of >= 2:
+            index = place_of - 2
+            rows_of = slice(index * columns, (index + 1) * columns)
+            keys_send[rows_of, 0:width] = key_term.astype(bf16)
+            keys_send[rows_of, width:] = value_term.astype(bf16)
+            copy = to_core(keys_send.at[rows_of, :], keys_back.at[rows_of, :], back_sems, index)
+            copy.start()
+            back_copies.append(copy)
+        else:
+            local_terms.append((key_term, value_term))
+    grad_mixer_col[:, 0:width] = (grad_query / root_size).astype(bf16)
+    for place_of in range(2):
+        back_copies[place_of].wait()
+        rows_of = slice(place_of * columns, (place_of + 1) * columns)
+        for part in range(2):
+            window = slice(part * width, (part + 1) * width)
+            grad_mixer_col[rows_of, (1 + part) * width : (2 + part) * width] = (
+                local_terms[place_of][part] + keys_back[rows_of, window].astype(f32)
+            ).astype(bf16)
+    grad_normal = None
+    for part in range(3):
+        window = slice(part * width, (part + 1) * width)
+        term = dot(grad_mixer_col[:, window], w_col[:, window], 1, 1)
+        grad_normal = term if grad_normal is None else grad_normal + term
+    term, gain, bias = unit_rows_back(grad_normal, after_row[...], gain_of(1))
+    vector[1:2, :] = gain
+    vector[4:5, :] = bias
+    total_grad[...] = total_grad[...] + term
+    branch_row[...] = total_grad[...].astype(bf16)
+    keys_send[:, 0:width] = dot(branch_row[...], w_row_out[...], 1, 1).astype(bf16)
+    probs_copies = []
+    for couple in range(couples):
+        partial_value = dot(
+            both(keys_send, couple * twin), stacked(mixer, 2 * width + couple * twin), 1, 1
+        )
+        probs_send[couple] = partial_value.astype(bf16)
+        copy = to_core(probs_send.at[couple], probs_recv.at[couple], probs_sems, couple)
+        copy.start()
+        probs_copies.append(copy)
+    column_weight = (float(total_rows * columns) / float(heads * columns)) * valid
+    for couple in range(couples):
+        start = couple * twin
+        logs = log_share[couple]
+        share = jnp.exp(logs)
+        grad_wide = both(keys_send, start)
+        put(
+            grad_mixer,
+            2 * width + start,
+            unstack(dot(share.astype(bf16), grad_wide, 0, 0)),
+        )
+        probs_copies[couple].wait_recv()
+        wide = probs_send[couple].astype(f32) + probs_recv[couple].astype(f32)
+        pieces = []
+        for half in range(2):
+            window = slice(half * columns, (half + 1) * columns)
+            part_share, part_logs, part_grad = (share[:, window], logs[:, window], wide[:, window])
+            entropy = -jnp.sum(part_share * part_logs, axis=-1, keepdims=True)
+            inner = jnp.sum(part_share * part_grad, axis=-1, keepdims=True)
+            piece = part_share * (part_grad - inner)
+            piece = piece - column_weight * part_share * (part_logs + entropy)
+            pieces.append(piece.astype(bf16))
+        grad_logits = jnp.concatenate(pieces, axis=1)
+        put(
+            grad_mixer,
+            start,
+            logit_factor * dot(grad_logits, stacked(mixer, width + start), 1, 0),
+        )
+        put(
+            grad_mixer,
+            width + start,
+            logit_factor * unstack(dot(grad_logits, both(mixer, start), 0, 0)),
+        )
+    grad_normal = None
+    for part in range(3):
+        window = slice(part * width, (part + 1) * width)
+        term = dot(grad_mixer[:, window], w_row[:, window], 1, 1)
+        grad_normal = term if grad_normal is None else grad_normal + term
+    term, gain, bias = unit_rows_back(grad_normal, source[...].astype(f32), gain_of(0))
+    vector[0:1, :] = gain
+    vector[3:4, :] = bias
+    vector[6:8, :] = jnp.zeros((2, width), f32)
+    der[...] = (total_grad[...] + term).astype(bf16)
+
+    @pl.when(pipe == 1)
+    def _():
+        send_back.start()
+
+    pairs = (
+        (normal_a, grad_mixer),
+        (blended, branch_row),
+        (normal_b, grad_mixer_col),
+        (mixed, branch_col),
+        (normal_c, grad_up),
+    )
+    share = width // (4 * LINE)
+    base = 0
+    waiting = {}
+    number = 0
+    for left, right in pairs:
+        for part in range(right.shape[1] // width):
+            slot = number % 2
+            if slot in waiting:
+                for copy in waiting.pop(slot):
+                    copy.wait()
+            window = slice(part * width, (part + 1) * width)
+            term = dot(left[...], right[:, window], 0, 0).astype(bf16)
+            stage[slot] = term.reshape(LINE, 4, share, width)
+            copies = [
+                pltpu.make_async_copy(
+                    stage.at[slot, target],
+                    grads.at[target, :, pl.ds(base, share)],
+                    stage_sems.at[slot, target],
+                )
+                for target in range(LINE)
+            ]
+            for copy in copies:
+                copy.start()
+            waiting[slot] = copies
+            base += share
+            number += 1
+    for part in range(parts):
+        slot = 2 + part % 2
+        if slot in waiting:
+            for copy in waiting.pop(slot):
+                copy.wait()
+        window = slice(part * width, (part + 1) * width)
+        term = dot(hidden[:, window], branch_ffn[...], 0, 0).astype(bf16)
+        stage_down[slot - 2] = term.reshape(4, width // 4, width)
+        copy = pltpu.make_async_copy(
+            stage_down.at[slot - 2],
+            grads.at[part, :, pl.ds(base, width // 4)],
+            stage_sems.at[slot, 0],
+        )
+        copy.start()
+        waiting[slot] = [copy]
+    for copies in waiting.values():
+        for copy in copies:
+            copy.wait()
+    for copy in logit_copies + keys_copies + probs_copies:
+        copy.wait_send()
+
+    @pl.when(pipe == 0)
+    def _():
+        send_on.wait_send()
+
+    @pl.when(pipe == 1)
+    def _():
+        send_back.wait_send()
+
+
+def run_layers(entry, factor, count, rows, wholes):
+    tokens, width = entry.shape
+    columns = tokens // 2
+    couples = HEAD_TALLY // 2
+    wide = wholes[4].shape[1]
+    anywhere = pl.BlockSpec(memory_space=pl.ANY)
+    inside = pl.BlockSpec(memory_space=pltpu.VMEM)
+    dma = pltpu.SemaphoreType.DMA
+    bf16, f32 = (jnp.bfloat16, jnp.float32)
+    rows_of = lambda columns_of, kind=bf16: pltpu.VMEM((tokens, columns_of), kind)
+    scores = pltpu.VMEM((couples, columns, 2 * columns), bf16)
+    packed_rows = sum(whole.shape[0] * whole.shape[1] for whole in wholes) // (16 * width)
+    return pl.pallas_call(
+        layers_kernel,
+        out_shape=[
+            jax.ShapeDtypeStruct((tokens, width), bf16),
+            jax.ShapeDtypeStruct((tokens, width), bf16),
+            jax.ShapeDtypeStruct((8, 128), f32),
+            jax.ShapeDtypeStruct((8, width), f32),
+            jax.ShapeDtypeStruct((LINE, 4, packed_rows, width), bf16),
         ],
-        axis=-1,
-    ).astype(jnp.bfloat16)
-    grad_normal_a = product_back(grad_row_proj, horizontal_coefficients)
-    from_norm, gain_first, bias_first = jax.vjp(
-        normed, source_rows.astype(jnp.float32), gain_rows[0], bias_rows[0]
-    )[1](grad_normal_a)
-    grad_source = (grad_row + from_norm).astype(jnp.bfloat16)
-    operand_pairs = (
-        (layernorm_first, grad_row_proj),
-        (blended_lines, grad_branch_row),
-        (layernorm_second, grad_col_proj),
-        (mixed_values, grad_branch_col),
-        (normal_c, grad_upward),
-        (hidden, grad_branch_ffn),
-    )
-    norm_grads = (
-        jnp.stack([gain_first, gain_middle, gain_last]),
-        jnp.stack([bias_first, bias_middle, bias_last]),
-    )
-    return (grad_source, operand_pairs, norm_grads)
-
-
-def packed(term, lanes):
-    share = term.shape[0] // (LINE * 4)
-    parts = term.reshape(LINE, 4, share, term.shape[1] // lanes, lanes)
-    return parts.transpose(0, 1, 3, 2, 4).reshape(LINE, 4, -1, lanes)
+        in_specs=[inside] * 4 + [anywhere] * 6,
+        out_specs=[inside] * 4 + [anywhere],
+        scratch_shapes=[pltpu.VMEM(whole.shape, bf16) for whole in wholes]
+        + [
+            rows_of(width),
+            rows_of(width),
+            rows_of(width),
+            rows_of(width),
+            rows_of(3 * width),
+            rows_of(3 * width),
+            rows_of(width),
+            rows_of(width),
+            rows_of(width, f32),
+            rows_of(width, f32),
+            pltpu.VMEM((couples, columns, 2 * columns), f32),
+            pltpu.VMEM((4, tokens, 128), f32),
+            rows_of(wide),
+            rows_of(wide),
+            rows_of(width, f32),
+            rows_of(width),
+            rows_of(width),
+            rows_of(width),
+            rows_of(width),
+            rows_of(wide),
+            rows_of(3 * width),
+            rows_of(3 * width),
+            scores,
+            scores,
+            pltpu.VMEM((2, tokens, width), bf16),
+            rows_of(2 * width),
+            rows_of(2 * width),
+            scores,
+            scores,
+            pltpu.VMEM((2, columns, 2 * columns), bf16),
+            pltpu.VMEM((width, 128), bf16),
+            pltpu.VMEM((128, width), bf16),
+            pltpu.VMEM((2, LINE, 4, width // (4 * LINE), width), bf16),
+            pltpu.VMEM((2, 4, width // 4, width), bf16),
+            dma((6,)),
+            dma((2, couples)),
+            dma((2, 2)),
+            dma((2, 2)),
+            dma((2, couples)),
+            dma((4,)),
+            dma((4, LINE)),
+        ],
+        compiler_params=pltpu.CompilerParams(
+            collective_id=2, has_side_effects=True, vmem_limit_bytes=60 * 2**20
+        ),
+        name="two_layers",
+    )(entry, factor, count, rows, *wholes)
 
 
 def unpacked(block, rows, columns, lanes):
@@ -1451,9 +1813,7 @@
     ffn_down,
     upstream_sensitivity,
 ):
-    head_count = HEAD_TALLY
     segment_place = lax.axis_index("pipe")
-    core = lax.rem(lax.axis_index("dp"), 2)
     sequence = order[0]
     columns, model_width = embedded_families.shape[2:]
     piece = jnp.where(
@@ -1476,27 +1836,23 @@
     shards = (row_qkv[0], row_out[0], col_qkv[0], col_out[0], ffn_up[0], ffn_down[0])
     *wholes, piece, meta, rows = gather_all(shards, piece, meta, rows)
     rows = rows[:, :6, :share].transpose(1, 0, 2).reshape(6, model_width)
-    projection_tables = tuple(wholes) + (rows[:3], rows[3:])
-    family_residues = meta[0, columns, 0].astype(jnp.int32)
-
-    early = chip_forward(piece, family_residues, projection_tables, head_count, core)
-    received = lax.ppermute(early[0], "pipe", [(0, 1)])
-    later = chip_forward(received, family_residues, projection_tables, head_count, core)
-    activation, cost, kept_state = choose(segment_place == 0, early, later)
-
-    outgrad = piece.astype(jnp.float32) * meta[:, :columns, :1]
-    ahead = chip_backward(kept_state, family_residues, outgrad, projection_tables, head_count, core)
-    grad_received = lax.ppermute(ahead[0], "pipe", [(1, 0)]).astype(jnp.float32)
-    behind = chip_backward(
-        kept_state, family_residues, grad_received, projection_tables, head_count, core
-    )
-    grad_source, operand_pairs, norm_grads = choose(segment_place == 1, ahead, behind)
-    totals = [weight_term(left, right).astype(jnp.bfloat16) for left, right in operand_pairs]
-    grads = jnp.concatenate([packed(total, model_width) for total in totals], axis=2)
-    vector = jnp.concatenate(norm_grads, axis=0).reshape(6, LINE, share).transpose(1, 0, 2)
-    vector = jnp.pad(vector, ((0, 0), (0, 2), (0, 256 - share)))
+    tokens = 2 * columns
+    activation, grad_source, cost, vector, grads = run_layers(
+        piece.reshape(tokens, model_width),
+        meta[:, :columns].reshape(tokens, 128),
+        meta[0, columns:],
+        jnp.pad(rows, ((0, 2), (0, 0))),
+        wholes,
+    )
+    vector = jnp.pad(
+        vector.reshape(8, LINE, share).transpose(1, 0, 2), ((0, 0), (0, 0), (0, 256 - share))
+    )
     out, vector, activations, derivs, costs = reduce_all(
-        grads, vector, activation, grad_source, jnp.full((8, 128), cost, jnp.float32)
+        grads,
+        vector,
+        activation.reshape(piece.shape),
+        grad_source.reshape(piece.shape),
+        cost,
     )
     results = []
     base = 0

time: 903 us -> 493 us (0.55)
  local copies, waits for them, and re-layouts: 256 us -> 30.7 us
  matrix products: 154 us -> 0 us
  other arithmetic: 97 us -> 8.67 us
  Pallas kernels: 360 us -> 448 us
  waiting for transfers between devices: 14 us -> 0 us
    dot_general x55 -> x0, matrix products: 154 us -> none  [the longest x12 32.5 us: product_back(): lax.dot_general(left, weight, (((left.ndim - 1,), (1,)), ((), ())), prefe...]
    pallas_call x0 -> x1, Pallas kernels: none -> 91.9 us  [run_layers(): pl.pallas_call(layers_kernel, out_shape=[jax.ShapeDtypeStruct((tokens, wi...]
    reshape x27 -> x3, local copies, waits for them, and re-layouts: 89.7 us -> 0.92 us  [the longest x2 0.83 us: on_device_lined(): vector.reshape(8, LINE, share).transpose(1, 0, 2)]
    slice x28 -> x1, local copies, waits for them, and re-layouts: 40.8 us -> 1.57 us  [on_device_lined(): meta[:, :columns].reshape(tokens, 128)]
    unnamed x363 -> x17, local copies, waits for them, and re-layouts: 30.5 us -> 3.4 us
    reduce_sum x20 -> x0, other arithmetic: 22.9 us -> none  [the longest x2 7.5 us: column_forward(): log_total = jax.nn.logsumexp(scores, axis=-1)]
    convert_element_type x12 -> x0, local copies, waits for them, and re-layouts: 19.1 us -> none  [the longest x4 9.72 us: column_forward(): return (mixed_cols.reshape(queries.shape).astype(jnp.bfloat16), log_total)]
    another operation x3 -> x0, other arithmetic: 18.2 us -> none  [the longest x1 14.8 us: gelu_exact(): return jax.nn.gelu(values, approximate=False)]
  transfers between devices with their start and end apart: 10 -> 0, of which waited for: 3 -> 0; matrix products, arithmetic and copies ran while one was open for 15% -> 0% of each run, Pallas kernels for 0% -> 0%
where the time goes in v2:
time: 493 us; the launch traced here: 489 us
  Pallas kernels  448 us (91%)
  local copies, waits for them, and re-layouts  30.7 us (6%)
  other arithmetic  8.67 us (2%)
    pallas_call x1, Pallas kernels, reduce_all(): pl.pallas_call(functools.partial(reduce_kernel, chunks, paired), out_shap...  197 us
    pallas_call x1, Pallas kernels, gather_all(): pl.pallas_call(gather_kernel, out_shape=shapes, in_specs=[anywhere] * 9,...  160 us
    pallas_call x1, Pallas kernels, run_layers(): pl.pallas_call(layers_kernel, out_shape=[jax.ShapeDtypeStruct((tokens, wi...  91.9 us
    convert_element_type x6, local copies, waits for them, and re-layouts, unpacked(): parts.transpose(0, 2, 1, 3).reshape(rows, columns).astype(jnp.float32)  11.1 us

profile of v2, /device:TPU:0, one launch (start us, length us, event | category | flops | bytes accessed | tf_op | source)
XLA Modules:
  0.0 489.1 jit_solution(2401636581216373693)
XLA Ops:
  1.4 1.2 gather_fusion.1
  2.6 1.3 gather_fusion.2
  6.7 1.8 bitcast_select_fusion.refs_6_
  8.5 159.6 %gather_weights.1 = (bf16[768,2304]{1,0:T(8,128)(2,1)}, bf16[768,768]{1,0:T(8,128)(2,1)}, bf16[768,2304]{1,0:T(8,128)(2,1)}, bf16[768,768]{1,0:T(8,128)(2,1)}, b...) custom-call(bf16[192,2304]{1,0:T(8,128)(2,1)} %bitcast.80, ...), custom_call_target="tpu_custom_call" | custom-call | tf_op jit(solution)/shard_map/gather_weights/pallas_call | solution.py:777
  168.1 1.3 slice_bitcast_fusion.3.count
  169.3 1.6 slice.36
  170.9 0.8 slice_bitcast_fusion
  172.4 91.9 %two_layers.1 = (bf16[256,768]{1,0:T(8,128)(2,1)}, bf16[256,768]{1,0:T(8,128)(2,1)}, f32[8,128]{1,0:T(8,128)}, f32[8,768]{1,0:T(8,128)}, bf16[4,4,768,768]{3,2,1,0:T(8,128)(2,1)}) custom-call(bf16[256,768]{1,0:T(8,128)(2,1)} %bitcast.85, f32[256,128]{1,0:T(8,128)} %bitcast.82, f32[8,128]{1,0:T(8,128)} %slice_bitcast_fusion.3.count, f32[8,768]{1,0:T(8,128)} %pad.14.rows, ...), custom_call_target="tpu_custom_call" | custom-call | tf_op jit(solution)/shard_map/two_layers/pallas_call | solution.py:1734
  264.3 0.8 reshape.162
  265.8 196.9 %reduce_grads.1 = (bf16[4,768,768]{2,1,0:T(8,128)(2,1)}, f32[8,256]{1,0:T(8,128)}, bf16[2,128,768]{2,1,0:T(8,128)(2,1)}, bf16[2,128,768]{2,1,0:T(8,128)(2,1)}, f32[2,8,128]{2,1,0:T(8,128)}) custom-call(bf16[4,4,768,768]{3,2,1,0:T(8,128)(2,1)} %get-tuple-element.39.refs_0_, f32[4,8,256]{2,1,0:T(8,128)} %pad.15.refs_1_, bf16[2,128,768]{2,1,0:T(8,128)(2,1)} %bitcast.86, ...), custom_call_target="tpu_custom_call" | custom-call | tf_op jit(solution)/shard_map/reduce_grads/pallas_call | solution.py:1179
  462.7 1.3 slice_reduce_fusion
  464.0 0.8 slice_bitcast_fusion.1
  466.0 1.1 fusion.2
  467.1 0.9 bitcast_convert_fusion.2
  467.9 0.9 bitcast_convert_fusion.1
  468.8 2.9 fusion.3
  471.7 1.2 fusion.1
  473.1 1.5 copy.36
  474.6 2.3 reshape.169
  476.9 2.9 bitcast_convert_fusion
  480.4 2.5 reshape.165
  482.9 1.8 copy.48
  484.7 2.5 reshape.167
  487.1 0.7 copy.53
  (32 shorter events, 7.6 us)
Async XLA Ops:
  0.6 5.5 %copy-start = (bf16[2,1,128,768]{3,2,1,0:T(8,128)(2,1)S(1)}, bf16[2,1,128,768]{3,2,1,0:T(8,128)(2,1)}, u32[]{:S(2)}) copy-start(bf16[2,1,128,768]{3,2,1,0:T(8,128)(2,1)} %param.13) | copy-start | bytes 1179652
  467.1 4.6 copy-start.2
  476.9 2.9 copy-start.3
  484.6 2.5 copy-start.5
  484.6 4.0 copy-start.1
  484.7 3.2 copy-start.4

commit v3 on v2

--- a/solution.py
+++ b/solution.py
@@ -506,7 +506,7 @@
     return (other_core, other_pair)
 
 
-def greet(pipe, seq, dp, core, pair):
+def greet(pipe, seq, dp, core, pair, across_pipe=False):
     barrier = pltpu.get_barrier_semaphore()
     other_core, other_pair = neighbours(pipe, seq, dp, core, pair)
     count = 0
@@ -522,8 +522,13 @@
                 device_id_type=MESH,
             )
             count += 1
-    pl.semaphore_signal(barrier, inc=1, device_id=other_pair, device_id_type=MESH)
-    pl.semaphore_wait(barrier, count + 1)
+    last = (1 - pipe, seq, dp) if across_pipe else other_pair
+    pl.semaphore_signal(barrier, inc=1, device_id=last, device_id_type=MESH)
+
+    def hear():
+        pl.semaphore_wait(barrier, count + 1)
+
+    return hear
 
 
 def remote(source, target, send, recv, device):
@@ -575,12 +580,16 @@
 
 
 def gather_kernel(*refs):
-    shards, refs = (refs[:6], refs[6:])
-    piece, meta, rows = refs[:3]
-    wholes, refs = (refs[3:9], refs[9:])
+    shards, refs = ([ref.at[0] for ref in refs[:6]], refs[6:])
+    families, upstream, order, quarters, tally, scales, offsets = refs[:7]
+    wholes, refs = (refs[7:13], refs[13:])
     piece_out, meta_out, rows_out = refs[:3]
     (
+        piece,
+        meta,
+        rows,
         own_sem,
+        own_recv,
         line_send,
         line_recv,
         pair_send,
@@ -598,8 +607,23 @@
     pipe, seq, dp, core, pair = where
     other_core, other_pair = neighbours(*where)
     quarter = dp
-    greet(*where)
+    hear = greet(*where)
     right, left = ((pipe, seq + 1, dp), (pipe, seq - 1, dp))
+    straight = order[0, 0] == 0
+    columns = families.shape[2]
+    share_of_width = scales.shape[2]
+    for index in range(2):
+        chosen = jnp.where(straight, families[index, 0], families[1 - index, 0])
+        piece[index] = jnp.where(pipe == 0, chosen, upstream[index, 0])
+        chosen = jnp.where(straight, quarters[index], quarters[1 - index])
+        factor = jnp.broadcast_to(chosen.astype(jnp.float32) * 0.25, (columns, columns))
+        meta[index, 0:columns] = factor.T
+        number = jnp.where(straight, tally[index], tally[1 - index])
+        meta[index, columns:] = jnp.broadcast_to(number, (8, columns)).astype(jnp.float32)
+    rows[...] = jnp.zeros(rows.shape, jnp.float32)
+    rows[0:3, 0:share_of_width] = scales[0]
+    rows[3:6, 0:share_of_width] = offsets[0]
+    hear()
 
     def region(index, source, part):
         depth = shards[index].shape[0]
@@ -623,10 +647,12 @@
     for index in range(6):
         depth = shards[index].shape[0]
         own.append(
-            pltpu.make_async_copy(
+            remote(
                 shards[index],
                 wholes[index].at[pl.ds(pl.multiple_of(seq * depth, depth), depth)],
                 own_sem.at[index],
+                own_recv.at[index],
+                other_core,
             )
         )
 
@@ -714,7 +740,7 @@
                 over("relay", source, index, across, other_core).start()
 
     events = [(step, index) for step in range(1, LINE) for index in range(6)]
-    lag = 2
+    lag = 10
     for count in range(len(events) + lag):
         if count < len(events):
             arrive(*events[count])
@@ -762,25 +788,31 @@
     finish_piece()
 
 
-def gather_all(shards, piece, meta, rows):
+def gather_all(shards, families, upstream, order, quarters, tally, scales, offsets):
     anywhere = pl.BlockSpec(memory_space=pl.ANY)
+    inside = pl.BlockSpec(memory_space=pltpu.VMEM)
+    scalars = pl.BlockSpec(memory_space=pltpu.SMEM)
+    columns, width = families.shape[2:]
+    piece = jax.ShapeDtypeStruct((2, columns, width), families.dtype)
+    meta = jax.ShapeDtypeStruct((2, columns + 8, columns), jnp.float32)
+    rows = jax.ShapeDtypeStruct((8, 256), jnp.float32)
     dma = pltpu.SemaphoreType.DMA
     shapes = [
-        jax.ShapeDtypeStruct((shard.shape[0] * LINE, shard.shape[1]), shard.dtype)
+        jax.ShapeDtypeStruct((shard.shape[1] * LINE, shard.shape[2]), shard.dtype)
         for shard in shards
     ]
-    shapes += [
-        jax.ShapeDtypeStruct(piece.shape, piece.dtype),
-        jax.ShapeDtypeStruct(meta.shape, meta.dtype),
-        jax.ShapeDtypeStruct((LINE,) + rows.shape, rows.dtype),
-    ]
+    shapes += [piece, meta, jax.ShapeDtypeStruct((LINE,) + rows.shape, rows.dtype)]
     return pl.pallas_call(
         gather_kernel,
         out_shape=shapes,
-        in_specs=[anywhere] * 9,
+        in_specs=[anywhere] * 6 + [inside, inside, scalars, inside, scalars, inside, inside],
         out_specs=[anywhere] * 9,
         scratch_shapes=[
+            pltpu.VMEM(piece.shape, piece.dtype),
+            pltpu.VMEM(meta.shape, meta.dtype),
+            pltpu.VMEM(rows.shape, rows.dtype),
             dma((9,)),
+            dma((6,)),
             dma((2, LINE, 6)),
             dma((LINE, 6)),
             dma((LINE, 6)),
@@ -794,14 +826,15 @@
             dma((LINE - 1,)),
             dma((LINE,)),
         ],
-        compiler_params=pltpu.CompilerParams(collective_id=0, has_side_effects=True),
+        compiler_params=pltpu.CompilerParams(
+            collective_id=0, has_side_effects=True, vmem_limit_bytes=60 * 2**20
+        ),
         name="gather_weights",
-    )(*shards, piece, meta, rows)
+    )(*shards, families, upstream, order, quarters, tally, scales, offsets)
 
 
 def reduce_kernel(chunks, paired, *refs):
-    grads, vector, first, second, cost = refs[:5]
-    out, vector_out, first_out, second_out, cost_out = refs[5:10]
+    grads, vector, out, vector_out = refs[:4]
     (
         mine,
         from_core,
@@ -825,30 +858,23 @@
         share_send,
         share_recv,
         out_sem,
-        first_send,
-        first_recv,
-        second_send,
-        second_recv,
-        local_sem,
         vec_send,
         vec_recv,
-        cost_send,
-        cost_recv,
-    ) = refs[10:]
+    ) = refs[4:]
     where = place()
     pipe, seq, dp, core, pair = where
     other_core, other_pair = neighbours(*where)
     right, left = ((pipe, seq + 1, dp), (pipe, seq - 1, dp))
     units = LINE * chunks
     depth = mine.shape[2]
-    greet(*where)
+    greet(*where)()
 
     def unit_of(number):
-        order = lax.div(number, chunks)
-        chunk = number - order * chunks
+        turn = lax.div(number, LINE)
+        order = number - turn * LINE
         half = lax.div(order, 2)
         target = jnp.where(lax.rem(order, 2) == 0, LINE - 1 - half, half)
-        return (target, chunk)
+        return (target, chunks - 1 - turn)
 
     def window(chunk):
         return pl.ds(pl.multiple_of(chunk * depth, depth), depth)
@@ -879,37 +905,8 @@
 
     lax.fori_loop(0, units, issue, 0)
 
-    start_first, finish_first = swap_rows(
-        first, first_out, first_send, first_recv, local_sem.at[0], where
-    )
-    start_second, finish_second = swap_rows(
-        second, second_out, second_send, second_recv, local_sem.at[1], where
-    )
-    start_first()
-    start_second()
-
     vec_first = remote(vector, vec_core, vec_send.at[0], vec_recv.at[0], other_core)
     vec_first.start()
-    sender = core == lax.div(seq, 2)
-    spot = lax.rem(seq, 2)
-    cost_own = pltpu.make_async_copy(cost, cost_out.at[spot], local_sem.at[2])
-    cost_copies = [
-        remote(
-            cost,
-            cost_out.at[spot],
-            cost_send.at[step - 1],
-            cost_recv.at[spot],
-            (pipe, lax.rem(seq + step, LINE), dp),
-        )
-        for step in range(1, LINE)
-    ]
-
-    @pl.when(sender)
-    def _():
-        cost_own.start()
-        for copy in cost_copies:
-            copy.start()
-
     def add(left_value, right_value):
         return (left_value.astype(jnp.float32) + right_value.astype(jnp.float32)).astype(
             jnp.bfloat16
@@ -1058,20 +1055,22 @@
                 out_copy(number, chunk, side).start()
                 share_copy(number, chunk, side, False).start()
 
-    pair_lag = 2
     always = lambda target: target >= 0
     far = jnp.maximum(seq, LINE - 1 - seq)
+    ahead, pair_lag, hop_lag, share_lag = (2, 3, 4, 4)
 
     def step(number, carry):
-        at(number, always, first_stage)
-        at(number - pair_lag, always, second_stage)
-        at(number - pair_lag - seq, lambda target: target > seq, hop(0))
-        at(number - pair_lag - (LINE - 1 - seq), lambda target: target < seq, hop(1))
-        at(number - pair_lag - far, lambda target: target == seq, last_stage)
-        at(number - pair_lag - far - pair_lag, lambda target: target == seq, share_stage)
+        for index in range(ahead):
+            at(ahead * number + index, always, first_stage)
+        base = number - pair_lag
+        at(base, always, second_stage)
+        at(base - hop_lag * seq, lambda target: target > seq, hop(0))
+        at(base - hop_lag * (LINE - 1 - seq), lambda target: target < seq, hop(1))
+        at(base - hop_lag * far, lambda target: target == seq, last_stage)
+        at(base - hop_lag * far - share_lag, lambda target: target == seq, share_stage)
         return carry
 
-    lax.fori_loop(0, units + 2 * pair_lag + LINE - 1, step, 0)
+    lax.fori_loop(0, units + pair_lag + hop_lag * (LINE - 1) + share_lag, step, 0)
 
     vec_first.wait()
     vec_core[...] = vector[...] + vec_core[...]
@@ -1149,25 +1148,8 @@
 
     lax.fori_loop(0, units, drain, 0)
 
-    @pl.when(sender)
-    def _():
-        cost_own.wait()
-        for copy in cost_copies:
-            copy.wait_send()
-
-    for index in range(2):
-
-        @pl.when(2 * core + index != seq)
-        def _():
-            remote(
-                cost, cost_out.at[index], cost_send.at[0], cost_recv.at[index], other_core
-            ).wait_recv()
-
-    finish_first()
-    finish_second()
-
-
-def reduce_all(grads, vector, first, second, cost):
+
+def reduce_all(grads, vector):
     anywhere = pl.BlockSpec(memory_space=pl.ANY)
     inside = pl.BlockSpec(memory_space=pltpu.VMEM)
     dma = pltpu.SemaphoreType.DMA
@@ -1181,12 +1163,9 @@
         out_shape=[
             jax.ShapeDtypeStruct(grads.shape[1:], grads.dtype),
             jax.ShapeDtypeStruct(vector.shape[1:], vector.dtype),
-            jax.ShapeDtypeStruct(first.shape, first.dtype),
-            jax.ShapeDtypeStruct(second.shape, second.dtype),
-            jax.ShapeDtypeStruct((2,) + cost.shape, cost.dtype),
         ],
-        in_specs=[anywhere, inside, anywhere, anywhere, anywhere],
-        out_specs=[anywhere, inside, anywhere, anywhere, anywhere],
+        in_specs=[anywhere, inside],
+        out_specs=[anywhere, inside],
         scratch_shapes=[
             pltpu.VMEM((units, 2) + block, jnp.bfloat16),
             pltpu.VMEM((units, 2) + block, jnp.bfloat16),
@@ -1210,21 +1189,14 @@
             dma((2, chunks)),
             dma((2, chunks)),
             dma((2, chunks)),
-            dma((2,)),
-            dma((2,)),
-            dma((2,)),
-            dma((2,)),
-            dma((3,)),
             dma((2 + LINE,)),
             dma((2 + LINE,)),
-            dma((LINE - 1,)),
-            dma((2,)),
         ],
         compiler_params=pltpu.CompilerParams(
             collective_id=1, has_side_effects=True, vmem_limit_bytes=60 * 2**20
         ),
         name="reduce_grads",
-    )(grads, vector, first, second, cost)
+    )(grads, vector)
 
 
 def dot(left, right, left_axis, right_axis):
@@ -1256,8 +1228,7 @@
 
 def layers_kernel(
     entry,
-    factor,
-    count,
+    meta,
     rows,
     w_row_any,
     w_row_out_any,
@@ -1265,9 +1236,9 @@
     w_col_out_any,
     w_up_any,
     w_down_any,
-    act,
-    der,
-    cost,
+    act_out,
+    der_out,
+    cost_out,
     vector,
     grads,
     w_row,
@@ -1310,6 +1281,9 @@
     spread,
     stage,
     stage_down,
+    act,
+    der,
+    cost,
     weight_sem,
     logit_sems,
     keys_sems,
@@ -1317,12 +1291,17 @@
     probs_sems,
     pipe_sems,
     stage_sems,
+    home_sems,
+    home_local,
+    cost_send,
+    cost_recv,
 ):
-    pipe, seq, dp, core, pair = place()
+    where = place()
+    pipe, seq, dp, core, pair = where
     other_core = (pipe, seq, dp + 1 - 2 * core)
     other_pipe = (1 - pipe, seq, dp)
-    tokens, width = entry.shape
-    columns = tokens // 2
+    _, columns, width = entry.shape
+    tokens = 2 * columns
     heads = HEAD_TALLY
     size = width // heads
     twin = 2 * size
@@ -1346,10 +1325,7 @@
     for copy in weights:
         copy.start()
 
-    barrier = pltpu.get_barrier_semaphore()
-    for device in (other_core, other_pipe):
-        pl.semaphore_signal(barrier, inc=1, device_id=device, device_id_type=MESH)
-
+    hear = greet(*where, across_pipe=True)
     lane = lax.broadcasted_iota(jnp.int32, (columns, 2 * twin), 1)
     early = (lax.rem(lane, twin) < size).astype(f32)
     halves[0] = early.astype(bf16)
@@ -1362,13 +1338,22 @@
     feature = lax.broadcasted_iota(jnp.int32, (128, width), 1)
     belongs = jnp.logical_and(feature >= head * size, feature < head * size + size)
     spread[...] = belongs.astype(f32).astype(bf16)
-    pl.semaphore_wait(barrier, 2)
+    hear()
 
     def gain_of(index):
         return rows[index : index + 1, :]
 
     def bias_of(index):
         return rows[3 + index : 4 + index, :]
+
+    def keep_vector(index, gain, bias):
+        part = width // LINE
+        for target in range(LINE):
+            window = slice(target * part, (target + 1) * part)
+            vector[target, index : index + 1, 0:part] = gain[:, window]
+            vector[target, 3 + index : 4 + index, 0:part] = bias[:, window]
+
+    vector[...] = jnp.zeros(vector.shape, f32)
 
     def both(ref, start):
         return jnp.concatenate(
@@ -1393,6 +1378,26 @@
             source_ref, target_ref, sems.at[0, index], sems.at[1, index], other_core
         )
 
+    start_act, finish_act = swap_rows(
+        act, act_out, home_sems.at[0], home_sems.at[1], home_local.at[0], where
+    )
+    start_der, finish_der = swap_rows(
+        der, der_out, home_sems.at[2], home_sems.at[3], home_local.at[1], where
+    )
+    sender = core == lax.div(seq, 2)
+    spot = lax.rem(seq, 2)
+    cost_own = pltpu.make_async_copy(cost, cost_out.at[spot], home_local.at[2])
+    cost_copies = [
+        remote(
+            cost,
+            cost_out.at[spot],
+            cost_send.at[step - 1],
+            cost_recv.at[spot],
+            (pipe, lax.rem(seq + step, LINE), dp),
+        )
+        for step in range(1, LINE)
+    ]
+
     send_on = remote(act, source, pipe_sems.at[0], pipe_sems.at[1], other_pipe)
     send_back = remote(der, grad_in, pipe_sems.at[2], pipe_sems.at[3], other_pipe)
 
@@ -1404,7 +1409,7 @@
     def _():
         send_on.wait_recv()
 
-    unit, _ = unit_rows(source[...].astype(f32))
+    unit, _ = unit_rows(source[...].reshape(tokens, width).astype(f32))
     normal_a[...] = (unit * gain_of(0) + bias_of(0)).astype(bf16)
     weights[0].wait()
     for part in range(3):
@@ -1421,7 +1426,7 @@
         copy.start()
         logit_copies.append(copy)
     valid = (
-        lax.broadcasted_iota(jnp.int32, (columns, 1), 0).astype(f32) < count[0:1, 0:1]
+        lax.broadcasted_iota(jnp.int32, (columns, 1), 0).astype(f32) < meta[0, columns : columns + 1, 0:1]
     ).astype(f32)
     disorder = jnp.zeros((columns, 1), f32)
     for couple in range(couples):
@@ -1449,7 +1454,7 @@
         jnp.sum(disorder, axis=0, keepdims=True) / float(heads * columns), cost.shape
     )
     weights[1].wait()
-    after_row[...] = source[...].astype(f32) + dot(blended[...], w_row_out[...], 1, 0)
+    after_row[...] = source[...].reshape(tokens, width).astype(f32) + dot(blended[...], w_row_out[...], 1, 0)
     unit, _ = unit_rows(after_row[...])
     normal_b[...] = (unit * gain_of(1) + bias_of(1)).astype(bf16)
     weights[2].wait()
@@ -1515,20 +1520,31 @@
         hidden[:, window] = (upward * inner).astype(bf16)
         slope[:, window] = (inner + upward * density).astype(bf16)
         result = result + dot(hidden[:, window], w_down[window, :], 1, 0)
-    act[...] = result.astype(bf16)
+    act[...] = result.astype(bf16).reshape(2, columns, width)
 
     @pl.when(pipe == 0)
     def _():
         send_on.start()
 
+    start_act()
+
+    @pl.when(sender)
+    def _():
+        cost_own.start()
+        for copy in cost_copies:
+            copy.start()
+
     @pl.when(pipe == 1)
     def _():
-        total_grad[...] = entry[...].astype(f32) * factor[:, 0:1]
+        for index in range(2):
+            total_grad[index * columns : (index + 1) * columns, :] = (
+                entry[index].astype(f32) * meta[index, 0:columns, 0:1]
+            )
 
     @pl.when(pipe == 0)
     def _():
         send_back.wait_recv()
-        total_grad[...] = grad_in[...].astype(f32)
+        total_grad[...] = grad_in[...].reshape(tokens, width).astype(f32)
 
     branch_ffn[...] = total_grad[...].astype(bf16)
     grad_normal = None
@@ -1539,8 +1555,7 @@
         term = dot(grad_up[:, window], w_up[:, window], 1, 1)
         grad_normal = term if grad_normal is None else grad_normal + term
     term, gain, bias = unit_rows_back(grad_normal, after_col[...], gain_of(2))
-    vector[2:3, :] = gain
-    vector[5:6, :] = bias
+    keep_vector(2, gain, bias)
     total_grad[...] = total_grad[...] + term
     branch_col[...] = total_grad[...].astype(bf16)
     grad_mixed = dot(branch_col[...], w_col_out[...], 1, 1).astype(bf16)
@@ -1594,8 +1609,7 @@
         term = dot(grad_mixer_col[:, window], w_col[:, window], 1, 1)
         grad_normal = term if grad_normal is None else grad_normal + term
     term, gain, bias = unit_rows_back(grad_normal, after_row[...], gain_of(1))
-    vector[1:2, :] = gain
-    vector[4:5, :] = bias
+    keep_vector(1, gain, bias)
     total_grad[...] = total_grad[...] + term
     branch_row[...] = total_grad[...].astype(bf16)
     keys_send[:, 0:width] = dot(branch_row[...], w_row_out[...], 1, 1).astype(bf16)
@@ -1646,15 +1660,15 @@
         window = slice(part * width, (part + 1) * width)
         term = dot(grad_mixer[:, window], w_row[:, window], 1, 1)
         grad_normal = term if grad_normal is None else grad_normal + term
-    term, gain, bias = unit_rows_back(grad_normal, source[...].astype(f32), gain_of(0))
-    vector[0:1, :] = gain
-    vector[3:4, :] = bias
-    vector[6:8, :] = jnp.zeros((2, width), f32)
-    der[...] = (total_grad[...] + term).astype(bf16)
+    term, gain, bias = unit_rows_back(grad_normal, source[...].reshape(tokens, width).astype(f32), gain_of(0))
+    keep_vector(0, gain, bias)
+    der[...] = (total_grad[...] + term).astype(bf16).reshape(2, columns, width)
 
     @pl.when(pipe == 1)
     def _():
         send_back.start()
+
+    start_der()
 
     pairs = (
         (normal_a, grad_mixer),
@@ -1718,10 +1732,27 @@
     def _():
         send_back.wait_send()
 
-
-def run_layers(entry, factor, count, rows, wholes):
-    tokens, width = entry.shape
-    columns = tokens // 2
+    finish_act()
+    finish_der()
+
+    @pl.when(sender)
+    def _():
+        cost_own.wait()
+        for copy in cost_copies:
+            copy.wait_send()
+
+    for index in range(2):
+
+        @pl.when(2 * core + index != seq)
+        def _():
+            remote(
+                cost, cost_out.at[index], cost_send.at[0], cost_recv.at[index], other_core
+            ).wait_recv()
+
+
+def run_layers(entry, meta, rows, wholes):
+    _, columns, width = entry.shape
+    tokens = 2 * columns
     couples = HEAD_TALLY // 2
     wide = wholes[4].shape[1]
     anywhere = pl.BlockSpec(memory_space=pl.ANY)
@@ -1734,17 +1765,17 @@
     return pl.pallas_call(
         layers_kernel,
         out_shape=[
-            jax.ShapeDtypeStruct((tokens, width), bf16),
-            jax.ShapeDtypeStruct((tokens, width), bf16),
-            jax.ShapeDtypeStruct((8, 128), f32),
-            jax.ShapeDtypeStruct((8, width), f32),
+            jax.ShapeDtypeStruct(entry.shape, bf16),
+            jax.ShapeDtypeStruct(entry.shape, bf16),
+            jax.ShapeDtypeStruct((2, 8, 128), f32),
+            jax.ShapeDtypeStruct((LINE, 8, 256), f32),
             jax.ShapeDtypeStruct((LINE, 4, packed_rows, width), bf16),
         ],
-        in_specs=[inside] * 4 + [anywhere] * 6,
-        out_specs=[inside] * 4 + [anywhere],
+        in_specs=[inside] * 3 + [anywhere] * 6,
+        out_specs=[anywhere, anywhere, inside, inside, anywhere],
         scratch_shapes=[pltpu.VMEM(whole.shape, bf16) for whole in wholes]
         + [
-            rows_of(width),
+            pltpu.VMEM(entry.shape, bf16),
             rows_of(width),
             rows_of(width),
             rows_of(width),
@@ -1759,7 +1790,7 @@
             rows_of(wide),
             rows_of(wide),
             rows_of(width, f32),
-            rows_of(width),
+            pltpu.VMEM(entry.shape, bf16),
             rows_of(width),
             rows_of(width),
             rows_of(width),
@@ -1778,6 +1809,9 @@
             pltpu.VMEM((128, width), bf16),
             pltpu.VMEM((2, LINE, 4, width // (4 * LINE), width), bf16),
             pltpu.VMEM((2, 4, width // 4, width), bf16),
+            pltpu.VMEM(entry.shape, bf16),
+            pltpu.VMEM(entry.shape, bf16),
+            pltpu.VMEM((8, 128), f32),
             dma((6,)),
             dma((2, couples)),
             dma((2, 2)),
@@ -1785,17 +1819,57 @@
             dma((2, couples)),
             dma((4,)),
             dma((4, LINE)),
+            dma((4, 2)),
+            dma((3,)),
+            dma((LINE - 1,)),
+            dma((2,)),
         ],
         compiler_params=pltpu.CompilerParams(
             collective_id=2, has_side_effects=True, vmem_limit_bytes=60 * 2**20
         ),
         name="two_layers",
-    )(entry, factor, count, rows, *wholes)
-
-
-def unpacked(block, rows, columns, lanes):
-    parts = block.reshape(4, columns // lanes, rows // 4, lanes)
-    return parts.transpose(0, 2, 1, 3).reshape(rows, columns).astype(jnp.float32)
+    )(entry, meta, rows, *wholes)
+
+
+def unpack_kernel(blocks, vector, *refs):
+    results, gain, bias = (refs[:6], refs[6], refs[7])
+    width = blocks.shape[2]
+    base = 0
+    for result in results:
+        depth, wide = result.shape[1:]
+        for part in range(wide // width):
+            result[0, :, part * width : (part + 1) * width] = blocks[
+                0, base : base + depth, :
+            ].astype(jnp.float32)
+            base += depth
+    share = gain.shape[2]
+    gain[0] = vector[0:3, 0:share]
+    bias[0] = vector[3:6, 0:share]
+
+
+def unpack_all(blocks, vector, shapes, share):
+    width = blocks.shape[2]
+    small = jax.ShapeDtypeStruct((1, 3, share), jnp.float32)
+    return pl.pallas_call(
+        unpack_kernel,
+        grid=(4,),
+        out_shape=[jax.ShapeDtypeStruct((1,) + shape, jnp.float32) for shape in shapes]
+        + [small, small],
+        in_specs=[
+            pl.BlockSpec((1,) + blocks.shape[1:], lambda step: (step, 0, 0)),
+            pl.BlockSpec(vector.shape, lambda step: (0, 0)),
+        ],
+        out_specs=[
+            pl.BlockSpec((1, shape[0] // 4, shape[1]), lambda step: (0, step, 0))
+            for shape in shapes
+        ]
+        + [pl.BlockSpec(small.shape, lambda step: (0, 0, 0))] * 2,
+        compiler_params=pltpu.CompilerParams(vmem_limit_bytes=60 * 2**20),
+        cost_estimate=pl.CostEstimate(
+            flops=blocks.size, bytes_accessed=6 * blocks.size, transcendentals=0
+        ),
+        name="unpack_grads",
+    )(blocks, vector)
 
 
 def on_device_lined(
@@ -1813,63 +1887,28 @@
     ffn_down,
     upstream_sensitivity,
 ):
-    segment_place = lax.axis_index("pipe")
-    sequence = order[0]
-    columns, model_width = embedded_families.shape[2:]
-    piece = jnp.where(
-        segment_place == 0, embedded_families[sequence, 0], upstream_sensitivity[:, 0]
-    )
-    factor = token_quarter_factor[sequence, 0].astype(jnp.float32) * 0.25
-    count = genuine_residue_tally[sequence].astype(jnp.float32)
-    meta = jnp.concatenate(
-        [
-            jnp.broadcast_to(factor[:, :, None], (2, columns, 128)),
-            jnp.broadcast_to(count[:, None, None], (2, 8, 128)),
-        ],
-        axis=1,
-    )
+    model_width = embedded_families.shape[-1]
     share = standardizer_scales.shape[-1]
-    rows = jnp.pad(
-        jnp.concatenate([standardizer_scales[0], standardizer_offsets[0]], axis=0),
-        ((0, 2), (0, 256 - share)),
-    )
-    shards = (row_qkv[0], row_out[0], col_qkv[0], col_out[0], ffn_up[0], ffn_down[0])
-    *wholes, piece, meta, rows = gather_all(shards, piece, meta, rows)
-    rows = rows[:, :6, :share].transpose(1, 0, 2).reshape(6, model_width)
-    tokens = 2 * columns
-    activation, grad_source, cost, vector, grads = run_layers(
-        piece.reshape(tokens, model_width),
-        meta[:, :columns].reshape(tokens, 128),
-        meta[0, columns:],
-        jnp.pad(rows, ((0, 2), (0, 0))),
-        wholes,
-    )
-    vector = jnp.pad(
-        vector.reshape(8, LINE, share).transpose(1, 0, 2), ((0, 0), (0, 0), (0, 256 - share))
-    )
-    out, vector, activations, derivs, costs = reduce_all(
-        grads,
-        vector,
-        activation.reshape(piece.shape),
-        grad_source.reshape(piece.shape),
-        cost,
-    )
-    results = []
-    base = 0
-    for shard in shards:
-        depth, wide = shard.shape
-        length = depth // 4 * (wide // model_width)
-        results.append(
-            unpacked(out[:, base : base + length], depth, wide, model_width)[None]
-        )
-        base += length
+    shards = (row_qkv, row_out, col_qkv, col_out, ffn_up, ffn_down)
+    *wholes, piece, meta, rows = gather_all(
+        shards,
+        embedded_families,
+        upstream_sensitivity,
+        order,
+        token_quarter_factor,
+        genuine_residue_tally,
+        standardizer_scales,
+        standardizer_offsets,
+    )
+    rows = rows[:, :, :share].transpose(1, 0, 2).reshape(8, model_width)
+    activations, derivs, costs, vector, grads = run_layers(piece, meta, rows, wholes)
+    out, vector = reduce_all(grads, vector)
+    results = unpack_all(out, vector, [shard.shape[1:] for shard in shards], share)
     return (
         activations[None, :, None],
         derivs[None, :, None],
         costs[:, 0, 0][None],
         *results,
-        vector[None, :3, :share],
-        vector[None, 3:6, :share],
     )
 
 

time: 493 us -> 349 us (0.71)
  Pallas kernels: 448 us -> 339 us
  local copies, waits for them, and re-layouts: 30.7 us -> 9.37 us
  other arithmetic: 8.67 us -> 0 us
    pallas_call x1, Pallas kernels: 197 us -> 135 us  [reduce_all(): pl.pallas_call(functools.partial(reduce_kernel, chunks, paired), out_shap...]
    pallas_call x2 -> x3, Pallas kernels: 252 us -> 204 us  [the longest x1 106 us: gather_all(): pl.pallas_call(gather_kernel, out_shape=shapes, in_specs=[anywhere] * 6 +...]
    convert_element_type x6 -> x0, local copies, waits for them, and re-layouts: 11.1 us -> none  [unpacked(): parts.transpose(0, 2, 1, 3).reshape(rows, columns).astype(jnp.float32)]
    slice x4 -> x0, local copies, waits for them, and re-layouts: 6.7 us -> none  [the longest x3 5.13 us: on_device_lined(): out[:, base:base + length]]
where the time goes in v3:
time: 349 us
  Pallas kernels  339 us (97%)
  local copies, waits for them, and re-layouts  9.37 us (3%)
    pallas_call x1, Pallas kernels, reduce_all(): pl.pallas_call(functools.partial(reduce_kernel, chunks, paired), out_shap...  135 us
    pallas_call x1, Pallas kernels, gather_all(): pl.pallas_call(gather_kernel, out_shape=shapes, in_specs=[anywhere] * 6 +...  106 us
    pallas_call x1, Pallas kernels, run_layers(): pl.pallas_call(layers_kernel, out_shape=[jax.ShapeDtypeStruct(entry.shape...  91.8 us

profile of v3, /device:TPU:0, one launch (start us, length us, event | category | flops | bytes accessed | tf_op | source)
XLA Modules:
  0.0 348.9 jit_solution(7752488233613068260)
XLA Ops:
  0.6 1.3 copy.31.refs_11_
  1.9 1.3 copy.32.refs_12_
  3.2 105.8 %gather_weights.1 = (bf16[768,2304]{1,0:T(8,128)(2,1)}, bf16[768,768]{1,0:T(8,128)(2,1)}, bf16[768,2304]{1,0:T(8,128)(2,1)}, bf16[768,768]{1,0:T(8,128)(2,1)}, b...) custom-call(bf16[1,192,2304]{2,1,0:T(8,128)(2,1)} %refs_0_.1, ...), custom_call_target="tpu_custom_call" | custom-call | tf_op jit(solution)/shard_map/gather_weights/pallas_call | solution.py:805
  109.0 0.8 slice_bitcast_fusion
  109.8 0.7 reshape.25.rows
  110.4 91.8 %two_layers.1 = (bf16[2,128,768]{2,1,0:T(8,128)(2,1)}, bf16[2,128,768]{2,1,0:T(8,128)(2,1)}, f32[2,8,128]{2,1,0:T(8,128)}, f32[4,8,256]{2,1,0:T(8,128)}, bf16[4,4,768,768]{3,2,1,0:T(8,128)(2,1)}) custom-call(bf16[2,128,768]{2,1,0:T(8,128)(2,1)} %get-tuple-element.35.entry, f32[2,136,128]{2,1,0:T(8,128)} %get-tuple-element.36.meta, f32[8,768]{1,0:T(8,128)} %reshape.25.rows, ...), custom_call_target="tpu_custom_call" | custom-call | tf_op jit(solution)/shard_map/two_layers/pallas_call | solution.py:1765
  202.3 1.3 slice_reduce_fusion
  203.6 134.7 %reduce_grads.1 = (bf16[4,768,768]{2,1,0:T(8,128)(2,1)}, f32[8,256]{1,0:T(8,128)}) custom-call(bf16[4,4,768,768]{3,2,1,0:T(8,128)(2,1)} %get-tuple-element.47.refs_0_, f32[4,8,256]{2,1,0:T(8,128)} %get-tuple-element.48.refs_1_), custom_call_target="tpu_custom_call" | custom-call | tf_op jit(solution)/shard_map/reduce_grads/pallas_call | solution.py:1161
  338.3 0.0 copy-start.1
  338.4 0.0 copy-start
  338.4 6.5 %unpack_grads.1 = (f32[1,192,2304]{2,1,0:T(8,128)}, f32[1,192,768]{2,1,0:T(8,128)}, f32[1,192,2304]{2,1,0:T(8,128)}, f32[1,192,768]{2,1,0:T(8,128)}, f32[1,192,3...) custom-call(bf16[4,768,768]{2,1,0:T(8,128)(2,1)} %get-tuple-element.49.blocks, ...), custom_call_target="tpu_custom_call" | custom-call | flops 2359296 | bytes 14155776 | tf_op jit(solution)/shard_map/unpack_grads/pallas_call | solution.py:1853
  344.8 1.3 copy.36
  346.1 1.3 copy.37
  347.4 0.0 copy-done.1
  347.4 0.7 copy.40
  348.1 0.0 copy-done
  348.1 0.7 copy.41
  (1 shorter events, 0.0 us)
Async XLA Ops:
  338.3 9.0 %copy-start.1 = (bf16[2,128,768]{2,1,0:T(8,128)(2,1)S(1)}, bf16[2,128,768]{2,1,0:T(8,128)(2,1)}, u32[]{:S(2)}) copy-start(bf16[2,128,768]{2,1,0:T(8,128)(2,1)} %get-tuple-element.44) | copy-start | bytes 1179652
  338.4 9.8 %copy-start = (bf16[2,128,768]{2,1,0:T(8,128)(2,1)S(1)}, bf16[2,128,768]{2,1,0:T(8,128)(2,1)}, u32[]{:S(2)}) copy-start(bf16[2,128,768]{2,1,0:T(8,128)(2,1)} %get-tuple-element.45) | copy-start | bytes 1179652

commit v4 on v3

--- a/solution.py
+++ b/solution.py
@@ -522,11 +522,12 @@
                 device_id_type=MESH,
             )
             count += 1
-    last = (1 - pipe, seq, dp) if across_pipe else other_pair
-    pl.semaphore_signal(barrier, inc=1, device_id=last, device_id_type=MESH)
+    more = [other_pair] + ([(1 - pipe, seq, dp)] if across_pipe else [])
+    for device in more:
+        pl.semaphore_signal(barrier, inc=1, device_id=device, device_id_type=MESH)
 
     def hear():
-        pl.semaphore_wait(barrier, count + 1)
+        pl.semaphore_wait(barrier, count + len(more))
 
     return hear
 
@@ -577,260 +578,6 @@
         pl.when(jnp.logical_not(here))(arriving.wait_recv)
 
     return (lambda: each(start), lambda: each(finish))
-
-
-def gather_kernel(*refs):
-    shards, refs = ([ref.at[0] for ref in refs[:6]], refs[6:])
-    families, upstream, order, quarters, tally, scales, offsets = refs[:7]
-    wholes, refs = (refs[7:13], refs[13:])
-    piece_out, meta_out, rows_out = refs[:3]
-    (
-        piece,
-        meta,
-        rows,
-        own_sem,
-        own_recv,
-        line_send,
-        line_recv,
-        pair_send,
-        pair_recv,
-        core_send,
-        core_recv,
-        piece_send,
-        piece_recv,
-        meta_send,
-        meta_recv,
-        rows_send,
-        rows_recv,
-    ) = refs[3:]
-    where = place()
-    pipe, seq, dp, core, pair = where
-    other_core, other_pair = neighbours(*where)
-    quarter = dp
-    hear = greet(*where)
-    right, left = ((pipe, seq + 1, dp), (pipe, seq - 1, dp))
-    straight = order[0, 0] == 0
-    columns = families.shape[2]
-    share_of_width = scales.shape[2]
-    for index in range(2):
-        chosen = jnp.where(straight, families[index, 0], families[1 - index, 0])
-        piece[index] = jnp.where(pipe == 0, chosen, upstream[index, 0])
-        chosen = jnp.where(straight, quarters[index], quarters[1 - index])
-        factor = jnp.broadcast_to(chosen.astype(jnp.float32) * 0.25, (columns, columns))
-        meta[index, 0:columns] = factor.T
-        number = jnp.where(straight, tally[index], tally[1 - index])
-        meta[index, columns:] = jnp.broadcast_to(number, (8, columns)).astype(jnp.float32)
-    rows[...] = jnp.zeros(rows.shape, jnp.float32)
-    rows[0:3, 0:share_of_width] = scales[0]
-    rows[3:6, 0:share_of_width] = offsets[0]
-    hear()
-
-    def region(index, source, part):
-        depth = shards[index].shape[0]
-        share = depth // 4
-        start = pl.multiple_of(source * depth + part * share, share)
-        return wholes[index].at[pl.ds(start, share)]
-
-    start_piece, finish_piece = swap_rows(
-        piece, piece_out, piece_send, piece_recv, own_sem.at[7], where
-    )
-    start_meta, finish_meta = swap_rows(meta, meta_out, meta_send, meta_recv, own_sem.at[8], where)
-    start_meta()
-    start_piece()
-    row_copies = []
-    for step in range(1, LINE):
-        target = (pipe, lax.rem(seq + step, LINE), dp)
-        copy = remote(rows, rows_out.at[seq], rows_send.at[step - 1], rows_recv.at[seq], target)
-        copy.start()
-        row_copies.append(copy)
-    own = [pltpu.make_async_copy(rows, rows_out.at[seq], own_sem.at[6])]
-    for index in range(6):
-        depth = shards[index].shape[0]
-        own.append(
-            remote(
-                shards[index],
-                wholes[index].at[pl.ds(pl.multiple_of(seq * depth, depth), depth)],
-                own_sem.at[index],
-                own_recv.at[index],
-                other_core,
-            )
-        )
-
-    for index in range(6):
-        share = shards[index].shape[0] // 4
-        mine = shards[index].at[pl.ds(pl.multiple_of(quarter * share, share), share)]
-
-        @pl.when(seq < LINE - 1)
-        def _():
-            remote(
-                mine,
-                region(index, seq, quarter),
-                line_send.at[0, seq, index],
-                line_recv.at[seq, index],
-                right,
-            ).start()
-
-        @pl.when(seq > 0)
-        def _():
-            remote(
-                mine,
-                region(index, seq, quarter),
-                line_send.at[1, seq, index],
-                line_recv.at[seq, index],
-                left,
-            ).start()
-
-    for copy in own:
-        copy.start()
-
-    def over(kind, source, index, part, target):
-        block = region(index, source, part)
-        if kind == "pair":
-            return remote(
-                block, block, pair_send.at[source, index], pair_recv.at[source, index], target
-            )
-        lane = 0 if kind == "core" else 1
-        return remote(
-            block,
-            block,
-            core_send.at[lane, source, index],
-            core_recv.at[lane, source, index],
-            target,
-        )
-
-    def along(source, index, direction, target):
-        block = region(index, source, quarter)
-        return remote(
-            block,
-            block,
-            line_send.at[direction, source, index],
-            line_recv.at[source, index],
-            target,
-        )
-
-    across = quarter + 2 - 4 * pair
-    opposite = quarter + 1 - 2 * core
-    opposite_across = across + 1 - 2 * core
-
-    def arrive(step, index):
-        for direction in range(2):
-            source = seq - step if direction == 0 else seq + step
-            present = source >= 0 if direction == 0 else source < LINE
-            onward = seq < LINE - 1 if direction == 0 else seq > 0
-            target = right if direction == 0 else left
-
-            @pl.when(present)
-            def _():
-                along(source, index, direction, target).wait_recv()
-                over("pair", source, index, quarter, other_pair).start()
-                over("core", source, index, quarter, other_core).start()
-
-            @pl.when(jnp.logical_and(present, onward))
-            def _():
-                along(source, index, direction, target).start()
-
-    def forward(step, index):
-        for direction in range(2):
-            source = seq - step if direction == 0 else seq + step
-            present = source >= 0 if direction == 0 else source < LINE
-
-            @pl.when(present)
-            def _():
-                over("pair", source, index, across, other_pair).wait_recv()
-                over("relay", source, index, across, other_core).start()
-
-    events = [(step, index) for step in range(1, LINE) for index in range(6)]
-    lag = 10
-    for count in range(len(events) + lag):
-        if count < len(events):
-            arrive(*events[count])
-        if count >= lag:
-            forward(*events[count - lag])
-
-    for index in range(6):
-
-        @pl.when(seq < LINE - 1)
-        def _():
-            along(seq, index, 0, right).wait_send()
-
-        @pl.when(seq > 0)
-        def _():
-            along(seq, index, 1, left).wait_send()
-
-    for step, index in events:
-        for direction in range(2):
-            source = seq - step if direction == 0 else seq + step
-            present = source >= 0 if direction == 0 else source < LINE
-            onward = seq < LINE - 1 if direction == 0 else seq > 0
-            target = right if direction == 0 else left
-
-            @pl.when(present)
-            def _():
-                over("pair", source, index, quarter, other_pair).wait_send()
-                over("core", source, index, quarter, other_core).wait_send()
-                over("relay", source, index, across, other_core).wait_send()
-                over("core", source, index, opposite, other_core).wait_recv()
-                over("relay", source, index, opposite_across, other_core).wait_recv()
-
-            @pl.when(jnp.logical_and(present, onward))
-            def _():
-                along(source, index, direction, target).wait_send()
-
-    for copy in own:
-        copy.wait()
-    for step in range(1, LINE):
-        source = lax.rem(seq + LINE - step, LINE)
-        row_copies[step - 1].wait_send()
-        remote(
-            rows, rows_out.at[source], rows_send.at[step - 1], rows_recv.at[source], other_core
-        ).wait_recv()
-    finish_meta()
-    finish_piece()
-
-
-def gather_all(shards, families, upstream, order, quarters, tally, scales, offsets):
-    anywhere = pl.BlockSpec(memory_space=pl.ANY)
-    inside = pl.BlockSpec(memory_space=pltpu.VMEM)
-    scalars = pl.BlockSpec(memory_space=pltpu.SMEM)
-    columns, width = families.shape[2:]
-    piece = jax.ShapeDtypeStruct((2, columns, width), families.dtype)
-    meta = jax.ShapeDtypeStruct((2, columns + 8, columns), jnp.float32)
-    rows = jax.ShapeDtypeStruct((8, 256), jnp.float32)
-    dma = pltpu.SemaphoreType.DMA
-    shapes = [
-        jax.ShapeDtypeStruct((shard.shape[1] * LINE, shard.shape[2]), shard.dtype)
-        for shard in shards
-    ]
-    shapes += [piece, meta, jax.ShapeDtypeStruct((LINE,) + rows.shape, rows.dtype)]
-    return pl.pallas_call(
-        gather_kernel,
-        out_shape=shapes,
-        in_specs=[anywhere] * 6 + [inside, inside, scalars, inside, scalars, inside, inside],
-        out_specs=[anywhere] * 9,
-        scratch_shapes=[
-            pltpu.VMEM(piece.shape, piece.dtype),
-            pltpu.VMEM(meta.shape, meta.dtype),
-            pltpu.VMEM(rows.shape, rows.dtype),
-            dma((9,)),
-            dma((6,)),
-            dma((2, LINE, 6)),
-            dma((LINE, 6)),
-            dma((LINE, 6)),
-            dma((LINE, 6)),
-            dma((2, LINE, 6)),
-            dma((2, LINE, 6)),
-            dma((2,)),
-            dma((2,)),
-            dma((2,)),
-            dma((2,)),
-            dma((LINE - 1,)),
-            dma((LINE,)),
-        ],
-        compiler_params=pltpu.CompilerParams(
-            collective_id=0, has_side_effects=True, vmem_limit_bytes=60 * 2**20
-        ),
-        name="gather_weights",
-    )(*shards, families, upstream, order, quarters, tally, scales, offsets)
 
 
 def reduce_kernel(chunks, paired, *refs):
@@ -1227,15 +974,18 @@
 
 
 def layers_kernel(
-    entry,
-    meta,
-    rows,
-    w_row_any,
-    w_row_out_any,
-    w_col_any,
-    w_col_out_any,
-    w_up_any,
-    w_down_any,
+    shard_row,
+    shard_row_out,
+    shard_col,
+    shard_col_out,
+    shard_up,
+    shard_down,
+    families,
+    upstream,
+    order,
+    quarters,
+    tally,
+    norms,
     act_out,
     der_out,
     cost_out,
@@ -1284,7 +1034,26 @@
     act,
     der,
     cost,
-    weight_sem,
+    piece,
+    piece_in,
+    sensitivity,
+    factor,
+    factor_in,
+    counts,
+    counts_in,
+    norms_in,
+    rows,
+    own_sem,
+    line_send,
+    line_recv,
+    pair_send,
+    pair_recv,
+    core_send,
+    core_recv,
+    entry_sems,
+    entry_local,
+    norm_send,
+    norm_recv,
     logit_sems,
     keys_sems,
     back_sems,
@@ -1300,7 +1069,7 @@
     pipe, seq, dp, core, pair = where
     other_core = (pipe, seq, dp + 1 - 2 * core)
     other_pipe = (1 - pipe, seq, dp)
-    _, columns, width = entry.shape
+    columns, width = families.shape[2:]
     tokens = 2 * columns
     heads = HEAD_TALLY
     size = width // heads
@@ -1308,24 +1077,205 @@
     couples = heads // 2
     total_rows = LINE
     bf16, f32 = (jnp.bfloat16, jnp.float32)
-
-    weights = [
-        pltpu.make_async_copy(far, near, weight_sem.at[index])
-        for index, (far, near) in enumerate(
-            (
-                (w_row_any, w_row),
-                (w_row_out_any, w_row_out),
-                (w_col_any, w_col),
-                (w_col_out_any, w_col_out),
-                (w_up_any, w_up),
-                (w_down_any, w_down),
-            )
-        )
+    part_width = width // LINE
+    shards = [
+        ref.at[0]
+        for ref in (shard_row, shard_row_out, shard_col, shard_col_out, shard_up, shard_down)
     ]
-    for copy in weights:
-        copy.start()
+    wholes = (w_row, w_row_out, w_col, w_col_out, w_up, w_down)
+    other_pair = (pipe, seq, dp + 2 - 4 * pair)
+    right, left = ((pipe, seq + 1, dp), (pipe, seq - 1, dp))
+    later = pipe == 1
 
     hear = greet(*where, across_pipe=True)
+    straight = order[0, 0] == 0
+    for index in range(2):
+        piece[index] = jnp.where(straight, families[index, 0], families[1 - index, 0])
+        chosen = jnp.where(straight, quarters[index], quarters[1 - index])
+        factor[index] = jnp.broadcast_to(chosen.astype(f32) * 0.25, (columns, columns)).T
+        number = jnp.where(straight, tally[index], tally[1 - index])
+        counts[index] = jnp.broadcast_to(number, (8, 128)).astype(f32)
+    hear()
+
+    def entering(number, source_ref, target_ref):
+        return swap_rows(
+            source_ref,
+            target_ref,
+            entry_sems.at[2 * number],
+            entry_sems.at[2 * number + 1],
+            entry_local.at[number],
+            where,
+        )
+
+    start_counts, finish_counts = entering(0, counts, counts_in)
+    start_piece, finish_piece = entering(1, piece, piece_in)
+    start_sensitivity, finish_sensitivity = entering(2, upstream.at[:, 0], sensitivity)
+    start_factor, finish_factor = entering(3, factor, factor_in)
+    start_counts()
+    pl.when(later)(start_piece)
+
+    def norm_copy(step, source):
+        return remote(
+            norms,
+            norms_in.at[source],
+            norm_send.at[step - 1],
+            norm_recv.at[source],
+            (pipe, lax.rem(seq + step, LINE), dp),
+        )
+
+    for step in range(1, LINE):
+        norm_copy(step, seq).start()
+    norms_in[seq] = norms[...]
+
+    def region(index, source, part):
+        depth = shards[index].shape[0]
+        share = depth // 4
+        start = pl.multiple_of(source * depth + part * share, share)
+        return wholes[index].at[pl.ds(start, share)]
+
+    def mine_of(index):
+        share = shards[index].shape[0] // 4
+        return shards[index].at[pl.ds(pl.multiple_of(dp * share, share), share)]
+
+    def own_copy(index):
+        depth = shards[index].shape[0]
+        return pltpu.make_async_copy(
+            shards[index],
+            wholes[index].at[pl.ds(pl.multiple_of(seq * depth, depth), depth)],
+            own_sem.at[index],
+        )
+
+    def own_line(index, direction):
+        return remote(
+            mine_of(index),
+            region(index, seq, dp),
+            line_send.at[direction, seq, index],
+            line_recv.at[seq, index],
+            right if direction == 0 else left,
+        )
+
+    def along(source, index, direction):
+        block = region(index, source, dp)
+        return remote(
+            block,
+            block,
+            line_send.at[direction, source, index],
+            line_recv.at[source, index],
+            right if direction == 0 else left,
+        )
+
+    across = dp + 2 - 4 * pair
+    opposite = dp + 1 - 2 * core
+    opposite_across = across + 1 - 2 * core
+
+    def over_pair(source, index, part):
+        block = region(index, source, part)
+        return remote(
+            block, block, pair_send.at[source, index], pair_recv.at[source, index], other_pair
+        )
+
+    def over_core(lane_of, source, index, part):
+        block = region(index, source, part)
+        return remote(
+            block,
+            block,
+            core_send.at[lane_of, source, index],
+            core_recv.at[lane_of, source, index],
+            other_core,
+        )
+
+    has = (seq < LINE - 1, seq > 0)
+
+    def sources(step):
+        for direction in range(2):
+            source = seq - step if direction == 0 else seq + step
+            yield (direction, source, source >= 0 if direction == 0 else source < LINE)
+
+    def begin(index):
+        for direction in range(2):
+            pl.when(has[direction])(own_line(index, direction).start)
+        own_copy(index).start()
+
+    def arrive(index, step):
+        for direction, source, present in sources(step):
+
+            @pl.when(present)
+            def _():
+                along(source, index, direction).wait_recv()
+
+                @pl.when(has[direction])
+                def _():
+                    along(source, index, direction).start()
+
+                over_pair(source, index, dp).start()
+                over_core(0, source, index, dp).start()
+
+    def relay(index, step):
+        for direction, source, present in sources(step):
+
+            @pl.when(present)
+            def _():
+                over_pair(source, index, across).wait_recv()
+                over_core(1, source, index, across).start()
+
+    def settle(index):
+        own_copy(index).wait()
+        for step in range(1, LINE):
+            for direction, source, present in sources(step):
+
+                @pl.when(present)
+                def _():
+                    over_core(0, source, index, opposite).wait_recv()
+                    over_core(1, source, index, opposite_across).wait_recv()
+
+    def drain(index):
+        for direction in range(2):
+            pl.when(has[direction])(own_line(index, direction).wait_send)
+        for step in range(1, LINE):
+            for direction, source, present in sources(step):
+
+                @pl.when(present)
+                def _():
+                    pl.when(has[direction])(along(source, index, direction).wait_send)
+                    over_pair(source, index, dp).wait_send()
+                    over_core(0, source, index, dp).wait_send()
+                    over_core(1, source, index, across).wait_send()
+
+    def wave(number):
+        if number + 1 < 6:
+            begin(number + 1)
+        for step in range(1, LINE):
+            if 0 <= number + 1 - step < 6:
+                arrive(number + 1 - step, step)
+        for step in range(1, LINE):
+            if 0 <= number - step < 6:
+                relay(number - step, step)
+
+    def gather(*waves):
+        @pl.when(jnp.logical_not(later))
+        def _():
+            for number in waves:
+                wave(number)
+
+    def ready(index):
+        pl.when(jnp.logical_not(later))(lambda: settle(index))
+
+    begin(0)
+    hop = remote(piece_in, source, pipe_sems.at[4], pipe_sems.at[5], other_pipe)
+
+    @pl.when(later)
+    def _():
+        finish_piece()
+        hop.start()
+        for number in range(9):
+            wave(number)
+        start_sensitivity()
+        start_factor()
+        for index in range(6):
+            settle(index)
+            drain(index)
+        hop.wait_send()
+
     lane = lax.broadcasted_iota(jnp.int32, (columns, 2 * twin), 1)
     early = (lax.rem(lane, twin) < size).astype(f32)
     halves[0] = early.astype(bf16)
@@ -1338,7 +1288,11 @@
     feature = lax.broadcasted_iota(jnp.int32, (128, width), 1)
     belongs = jnp.logical_and(feature >= head * size, feature < head * size + size)
     spread[...] = belongs.astype(f32).astype(bf16)
-    hear()
+    for step in range(1, LINE):
+        norm_copy(step, lax.rem(seq + LINE - step, LINE)).wait()
+    for part in range(LINE):
+        rows[:, part * part_width : (part + 1) * part_width] = norms_in[part, :, 0:part_width]
+    finish_counts()
 
     def gain_of(index):
         return rows[index : index + 1, :]
@@ -1401,17 +1355,20 @@
     send_on = remote(act, source, pipe_sems.at[0], pipe_sems.at[1], other_pipe)
     send_back = remote(der, grad_in, pipe_sems.at[2], pipe_sems.at[3], other_pipe)
 
-    @pl.when(pipe == 0)
-    def _():
-        source[...] = entry[...]
-
-    @pl.when(pipe == 1)
+    @pl.when(later)
     def _():
         send_on.wait_recv()
 
+    gather(0, 1)
+
+    @pl.when(jnp.logical_not(later))
+    def _():
+        hop.wait_recv()
+
     unit, _ = unit_rows(source[...].reshape(tokens, width).astype(f32))
     normal_a[...] = (unit * gain_of(0) + bias_of(0)).astype(bf16)
-    weights[0].wait()
+    gather(2, 3)
+    ready(0)
     for part in range(3):
         window = slice(part * width, (part + 1) * width)
         mixer[:, window] = dot(normal_a[...], w_row[:, window], 1, 0).astype(bf16)
@@ -1425,8 +1382,9 @@
         copy = to_core(logit_send.at[couple], logit_recv.at[couple], logit_sems, couple)
         copy.start()
         logit_copies.append(copy)
+    gather(4)
     valid = (
-        lax.broadcasted_iota(jnp.int32, (columns, 1), 0).astype(f32) < meta[0, columns : columns + 1, 0:1]
+        lax.broadcasted_iota(jnp.int32, (columns, 1), 0).astype(f32) < counts_in[0, 0:1, 0:1]
     ).astype(f32)
     disorder = jnp.zeros((columns, 1), f32)
     for couple in range(couples):
@@ -1453,11 +1411,12 @@
     cost[...] = jnp.broadcast_to(
         jnp.sum(disorder, axis=0, keepdims=True) / float(heads * columns), cost.shape
     )
-    weights[1].wait()
+    ready(1)
     after_row[...] = source[...].reshape(tokens, width).astype(f32) + dot(blended[...], w_row_out[...], 1, 0)
     unit, _ = unit_rows(after_row[...])
     normal_b[...] = (unit * gain_of(1) + bias_of(1)).astype(bf16)
-    weights[2].wait()
+    gather(5)
+    ready(2)
     keys_copies = []
     for part in (1, 2, 0):
         window = slice(part * width, (part + 1) * width)
@@ -1486,6 +1445,7 @@
     def spread_heads(narrow):
         return dot(narrow, spread[...], 1, 0)
 
+    gather(6)
     scores = []
     for place_of in range(4):
         if place_of == 2:
@@ -1504,12 +1464,12 @@
         term = jnp.concatenate([wide[0:columns] * line, wide[columns:] * line], axis=0)
         gathered_mix = term if gathered_mix is None else gathered_mix + term
     mixed[...] = gathered_mix.astype(bf16)
-    weights[3].wait()
+    ready(3)
     after_col[...] = after_row[...] + dot(mixed[...], w_col_out[...], 1, 0)
     unit, _ = unit_rows(after_col[...])
     normal_c[...] = (unit * gain_of(2) + bias_of(2)).astype(bf16)
-    weights[4].wait()
-    weights[5].wait()
+    gather(7)
+    ready(4)
     parts = hidden.shape[1] // width
     result = after_col[...]
     for part in range(parts):
@@ -1519,6 +1479,10 @@
         density = jnp.exp(-0.5 * upward * upward) * (1.0 / math.sqrt(2.0 * math.pi))
         hidden[:, window] = (upward * inner).astype(bf16)
         slope[:, window] = (inner + upward * density).astype(bf16)
+    gather(8)
+    ready(5)
+    for part in range(parts):
+        window = slice(part * width, (part + 1) * width)
         result = result + dot(hidden[:, window], w_down[window, :], 1, 0)
     act[...] = result.astype(bf16).reshape(2, columns, width)
 
@@ -1536,13 +1500,17 @@
 
     @pl.when(pipe == 1)
     def _():
+        finish_sensitivity()
+        finish_factor()
         for index in range(2):
             total_grad[index * columns : (index + 1) * columns, :] = (
-                entry[index].astype(f32) * meta[index, 0:columns, 0:1]
+                sensitivity[index].astype(f32) * factor_in[index, :, 0:1]
             )
 
     @pl.when(pipe == 0)
     def _():
+        for index in range(6):
+            drain(index)
         send_back.wait_recv()
         total_grad[...] = grad_in[...].reshape(tokens, width).astype(f32)
 
@@ -1750,13 +1718,19 @@
             ).wait_recv()
 
 
-def run_layers(entry, meta, rows, wholes):
-    _, columns, width = entry.shape
+def run_layers(shards, families, upstream, order, quarters, tally, norms):
+    columns, width = families.shape[2:]
     tokens = 2 * columns
     couples = HEAD_TALLY // 2
-    wide = wholes[4].shape[1]
+    wide = shards[4].shape[2]
+    entry = jax.ShapeDtypeStruct((2, columns, width), families.dtype)
+    wholes = [
+        jax.ShapeDtypeStruct((shard.shape[1] * LINE, shard.shape[2]), shard.dtype)
+        for shard in shards
+    ]
     anywhere = pl.BlockSpec(memory_space=pl.ANY)
     inside = pl.BlockSpec(memory_space=pltpu.VMEM)
+    scalars = pl.BlockSpec(memory_space=pltpu.SMEM)
     dma = pltpu.SemaphoreType.DMA
     bf16, f32 = (jnp.bfloat16, jnp.float32)
     rows_of = lambda columns_of, kind=bf16: pltpu.VMEM((tokens, columns_of), kind)
@@ -1771,7 +1745,7 @@
             jax.ShapeDtypeStruct((LINE, 8, 256), f32),
             jax.ShapeDtypeStruct((LINE, 4, packed_rows, width), bf16),
         ],
-        in_specs=[inside] * 3 + [anywhere] * 6,
+        in_specs=[anywhere] * 6 + [inside, inside, scalars, inside, scalars, inside],
         out_specs=[anywhere, anywhere, inside, inside, anywhere],
         scratch_shapes=[pltpu.VMEM(whole.shape, bf16) for whole in wholes]
         + [
@@ -1812,12 +1786,31 @@
             pltpu.VMEM(entry.shape, bf16),
             pltpu.VMEM(entry.shape, bf16),
             pltpu.VMEM((8, 128), f32),
+            pltpu.VMEM(entry.shape, bf16),
+            pltpu.VMEM(entry.shape, bf16),
+            pltpu.VMEM(entry.shape, bf16),
+            pltpu.VMEM((2, columns, columns), f32),
+            pltpu.VMEM((2, columns, columns), f32),
+            pltpu.VMEM((2, 8, 128), f32),
+            pltpu.VMEM((2, 8, 128), f32),
+            pltpu.VMEM((LINE, 8, 256), f32),
+            pltpu.VMEM((8, width), f32),
             dma((6,)),
+            dma((2, LINE, 6)),
+            dma((LINE, 6)),
+            dma((LINE, 6)),
+            dma((LINE, 6)),
+            dma((2, LINE, 6)),
+            dma((2, LINE, 6)),
+            dma((8, 2)),
+            dma((4,)),
+            dma((LINE - 1,)),
+            dma((LINE,)),
             dma((2, couples)),
             dma((2, 2)),
             dma((2, 2)),
             dma((2, couples)),
-            dma((4,)),
+            dma((6,)),
             dma((4, LINE)),
             dma((4, 2)),
             dma((3,)),
@@ -1828,11 +1821,11 @@
             collective_id=2, has_side_effects=True, vmem_limit_bytes=60 * 2**20
         ),
         name="two_layers",
-    )(entry, meta, rows, *wholes)
-
-
-def unpack_kernel(blocks, vector, *refs):
-    results, gain, bias = (refs[:6], refs[6], refs[7])
+    )(*shards, families, upstream, order, quarters, tally, norms)
+
+
+def unpack_kernel(blocks, vector, act, der, costs, *refs):
+    results, gain, bias, act_out, der_out, cost_out = (refs[:6], *refs[6:])
     width = blocks.shape[2]
     base = 0
     for result in results:
@@ -1845,31 +1838,41 @@
     share = gain.shape[2]
     gain[0] = vector[0:3, 0:share]
     bias[0] = vector[3:6, 0:share]
-
-
-def unpack_all(blocks, vector, shapes, share):
-    width = blocks.shape[2]
+    act_out[0, :, 0] = act[...]
+    der_out[0, :, 0] = der[...]
+    cost_out[...] = jnp.concatenate([costs[0, 0:1, 0:1], costs[1, 0:1, 0:1]], axis=1)
+
+
+def unpack_all(blocks, vector, act, der, costs, shapes, share):
+    columns, width = act.shape[1:]
     small = jax.ShapeDtypeStruct((1, 3, share), jnp.float32)
+    large = jax.ShapeDtypeStruct((1, 2, 1, columns, width), act.dtype)
+    part = pl.BlockSpec((2, columns // 4, width), lambda step: (0, step, 0))
+    wide = pl.BlockSpec((1, 2, 1, columns // 4, width), lambda step: (0, 0, 0, step, 0))
     return pl.pallas_call(
         unpack_kernel,
         grid=(4,),
         out_shape=[jax.ShapeDtypeStruct((1,) + shape, jnp.float32) for shape in shapes]
-        + [small, small],
+        + [small, small, large, large, jax.ShapeDtypeStruct((1, 2), jnp.float32)],
         in_specs=[
             pl.BlockSpec((1,) + blocks.shape[1:], lambda step: (step, 0, 0)),
             pl.BlockSpec(vector.shape, lambda step: (0, 0)),
+            part,
+            part,
+            pl.BlockSpec(costs.shape, lambda step: (0, 0, 0)),
         ],
         out_specs=[
             pl.BlockSpec((1, shape[0] // 4, shape[1]), lambda step: (0, step, 0))
             for shape in shapes
         ]
-        + [pl.BlockSpec(small.shape, lambda step: (0, 0, 0))] * 2,
+        + [pl.BlockSpec(small.shape, lambda step: (0, 0, 0))] * 2
+        + [wide, wide, pl.BlockSpec((1, 2), lambda step: (0, 0))],
         compiler_params=pltpu.CompilerParams(vmem_limit_bytes=60 * 2**20),
         cost_estimate=pl.CostEstimate(
             flops=blocks.size, bytes_accessed=6 * blocks.size, transcendentals=0
         ),
         name="unpack_grads",
-    )(blocks, vector)
+    )(blocks, vector, act, der, costs)
 
 
 def on_device_lined(
@@ -1890,26 +1893,30 @@
     model_width = embedded_families.shape[-1]
     share = standardizer_scales.shape[-1]
     shards = (row_qkv, row_out, col_qkv, col_out, ffn_up, ffn_down)
-    *wholes, piece, meta, rows = gather_all(
+    norms = jnp.pad(
+        jnp.concatenate([standardizer_scales[0], standardizer_offsets[0]], axis=0),
+        ((0, 2), (0, 256 - share)),
+    )
+    activations, derivs, costs, vector, grads = run_layers(
         shards,
         embedded_families,
         upstream_sensitivity,
         order,
         token_quarter_factor,
         genuine_residue_tally,
-        standardizer_scales,
-        standardizer_offsets,
-    )
-    rows = rows[:, :, :share].transpose(1, 0, 2).reshape(8, model_width)
-    activations, derivs, costs, vector, grads = run_layers(piece, meta, rows, wholes)
+        norms,
+    )
     out, vector = reduce_all(grads, vector)
-    results = unpack_all(out, vector, [shard.shape[1:] for shard in shards], share)
-    return (
-        activations[None, :, None],
-        derivs[None, :, None],
-        costs[:, 0, 0][None],
-        *results,
-    )
+    *results, activations, derivs, costs = unpack_all(
+        out,
+        vector,
+        activations,
+        derivs,
+        costs,
+        [shard.shape[1:] for shard in shards],
+        share,
+    )
+    return (activations, derivs, costs, *results)
 
 
 def solution(mesh):

time: 349 us -> 324 us (0.928)
  Pallas kernels: 339 us -> 319 us
  local copies, waits for them, and re-layouts: 9.37 us -> 3.22 us
    pallas_call x1 -> x0, Pallas kernels: 106 us -> none  [gather_all(): pl.pallas_call(gather_kernel, out_shape=shapes, in_specs=[anywhere] * 6 +...]
    pallas_call x1, Pallas kernels: 91.8 us -> 177 us  [run_layers(): pl.pallas_call(layers_kernel, out_shape=[jax.ShapeDtypeStruct(entry.shape...]
where the time goes in v4:
time: 324 us; the launch traced here: 323 us
  Pallas kernels  319 us (98%)
    pallas_call x1, Pallas kernels, run_layers(): pl.pallas_call(layers_kernel, out_shape=[jax.ShapeDtypeStruct(entry.shape...  177 us
    pallas_call x1, Pallas kernels, reduce_all(): pl.pallas_call(functools.partial(reduce_kernel, chunks, paired), out_shap...  135 us
    pallas_call x1, Pallas kernels, unpack_all(): pl.pallas_call(unpack_kernel, grid=(4,), out_shape=[jax.ShapeDtypeStruct(...  6.81 us

profile of v4, /device:TPU:0, one launch (start us, length us, event | category | flops | bytes accessed | tf_op | source)
XLA Modules:
  0.0 323.3 jit_solution(6643479970409222509)
XLA Ops:
  0.6 0.7 copy_bitcast_fusion
  1.3 0.6 select_maximum_fusion.norms
  2.0 177.5 %two_layers.1 = (bf16[2,128,768]{2,1,0:T(8,128)(2,1)}, bf16[2,128,768]{2,1,0:T(8,128)(2,1)}, f32[2,8,128]{2,1,0:T(8,128)}, f32[4,8,256]{2,1,0:T(8,128)}, bf16[4,4,768,768]{3,2,1,0:T(8,128)(2,1)}) custom-call(bf16[1,192,2304]{2,1,0:T(8,128)(2,1)} %shard_row.1, bf16[1,192,768]{2,1,0:T(8,128)(2,1)} %shard_row_out.1, bf16[1,192,2304]{2,1,0:T(8,128)(2,1)} %shard_col.1, ...), custom_call_target="tpu_custom_call" | custom-call | tf_op jit(solution)/shard_map/two_layers/pallas_call | solution.py:1739
  179.4 134.5 %reduce_grads.1 = (bf16[4,768,768]{2,1,0:T(8,128)(2,1)}, f32[8,256]{1,0:T(8,128)}) custom-call(bf16[4,4,768,768]{3,2,1,0:T(8,128)(2,1)} %get-tuple-element.29.refs_0_, f32[4,8,256]{2,1,0:T(8,128)} %get-tuple-element.30.refs_1_), custom_call_target="tpu_custom_call" | custom-call | tf_op jit(solution)/shard_map/reduce_grads/pallas_call | solution.py:908
  313.9 6.8 %unpack_grads.1 = (f32[1,192,2304]{2,1,0:T(8,128)}, f32[1,192,768]{2,1,0:T(8,128)}, f32[1,192,2304]{2,1,0:T(8,128)}, f32[1,192,768]{2,1,0:T(8,128)}, f32[1,192,3...) custom-call(bf16[4,768,768]{2,1,0:T(8,128)(2,1)} %get-tuple-element., ...), custom_call_target="tpu_custom_call" | custom-call | flops 2359296 | bytes 14155776 | tf_op jit(solution)/shard_map/unpack_grads/pallas_call | solution.py:1852
  320.8 1.3 copy.24
  322.0 1.3 copy.25
